TPU v7x, 32 devices: a whole 2x2x4 slice. The times are simulated.
32 devices in a mesh: dp: 16 (over z, x, core), fsdp: 2 (over y).
Axes of the slice: x: 2, y: 2, z: 4, core: 2. Of those that a mesh axis runs over, the one named last changes fastest.
Arguments:
- decoder_in: float32 [2, 512, 768], P('fsdp', 'dp'), may hold values from -6 to 6
- memory: bfloat16 [2, 6688, 768], P('fsdp', 'dp'), may hold values from -6 to 6
- res_group: int32 [2, 16], P('fsdp'), may hold values from 0 to 1, as said below
- prefix_len: int32 [2, 16], P('fsdp', 'dp'), may hold values from 1 to 32, as said below
- self_gain: bfloat16 [768], P('fsdp'), may hold values from 0.5 to 1.5
- self_qkv: bfloat16 [768, 2304], P('fsdp'), may hold values from -0.3125 to 0.3125
- self_out: bfloat16 [768, 768], P('fsdp'), may hold values from -0.4375 to 0.4375
- cross_gain: bfloat16 [768], P('fsdp'), may hold values from 0.5 to 1.5
- cross_query: bfloat16 [768, 768], P('fsdp'), may hold values from -0.3125 to 0.3125
- cross_kv: bfloat16 [768, 1536], P('fsdp'), may hold values from -0.3125 to 0.3125
- cross_out: bfloat16 [768, 768], P('fsdp'), may hold values from -0.875 to 0.875
- ffn_gain: bfloat16 [768], P('fsdp'), may hold values from 0.5 to 1.5
- ffn_in: bfloat16 [768, 3072], P('fsdp'), may hold values from -0.21875 to 0.21875
- ffn_out: bfloat16 [3072, 768], P('fsdp'), may hold values from -0.109375 to 0.109375
- cotangent: float32 [2, 512, 768], P('fsdp', 'dp'), may hold values from -6 to 6
Outputs:
- decoder_out: float32 [2, 512, 768], P('fsdp', 'dp')
- decoder_grad: float32 [2, 512, 768], P('fsdp', 'dp')
- memory_grad: float32 [2, 6688, 768], P('fsdp', 'dp')
- self_gain_grad: float32 [768], P('fsdp')
- self_qkv_grad: float32 [768, 2304], P('fsdp')
- self_out_grad: float32 [768, 768], P('fsdp')
- cross_gain_grad: float32 [768], P('fsdp')
- cross_query_grad: float32 [768, 768], P('fsdp')
- cross_kv_grad: float32 [768, 1536], P('fsdp')
- cross_out_grad: float32 [768, 768], P('fsdp')
- ffn_gain_grad: float32 [768], P('fsdp')
- ffn_in_grad: float32 [768, 3072], P('fsdp')
- ffn_out_grad: float32 [3072, 768], P('fsdp')
Inputs may be any that keep to these rules, and one draw needn't show every extreme that they name: In every column exactly half of the 16 examples have res_group 1. `prefix_len`: some example has 32 prefix tokens and some has 1.
All inputs are finite; a program needn't handle non-finite values.
Results may differ from a plain program's by a relative error of at most 0.03.
The roundings to bfloat16 on the way count: a program that leaves them out, or rounds other values in their place, can miss the bound.
Values may be sent and summed in bfloat16 or wider, within the bound.
A program may use at most 192 MiB of HBM per device.

v0:
```python
from functools import partial

import jax
import jax.numpy as jnp
from jax import lax
from jax.sharding import PartitionSpec as P

D = 768
HEADS = 12
HEAD_DIM = 64
SUFFIX = 32
PATCH_S = 196
PATCH_L = 576
SLOT_S = 228
SLOT_L = 608


norm_eps = 1e-06


def layer_norm(value, gain):
    mean = jnp.mean(value, axis=-1, keepdims=True)
    centred = value - mean
    variance = jnp.mean(centred * centred, axis=-1, keepdims=True)
    return centred * lax.rsqrt(variance + norm_eps) * gain


def product(left, right):
    return jnp.dot(left, right, preferred_element_type=jnp.float32)


def outer_sum(left, right):
    flat_left = left.reshape(-1, left.shape[-1])
    flat_right = right.reshape(-1, right.shape[-1])
    return lax.dot_general(
        flat_left, flat_right, (((0,), (0,)), ((), ())), preferred_element_type=jnp.float32
    )


def back_product(grad, weight):
    return lax.dot_general(
        grad, weight, (((grad.ndim - 1,), (1,)), ((), ())), preferred_element_type=jnp.float32
    )


def attend(query, keys, values, allowed, scale):
    scores = jnp.einsum("eqhd,ekhd->ehqk", query, keys, preferred_element_type=jnp.float32) * scale
    scores = jnp.where(allowed[:, None], scores, -1e30)
    top = jnp.max(scores, axis=-1, keepdims=True)
    weights = jnp.exp(scores - top)
    probs = weights / jnp.sum(weights, axis=-1, keepdims=True)
    mixed = jnp.einsum(
        "ehqk,ekhd->eqhd", probs.astype(jnp.bfloat16), values, preferred_element_type=jnp.float32
    )
    return (mixed.astype(jnp.bfloat16), probs)


def attend_back(grad_mixed, query, keys, values, probs, scale):
    probs_low = probs.astype(jnp.bfloat16)
    grad_values = jnp.einsum(
        "ehqk,eqhd->ekhd", probs_low, grad_mixed, preferred_element_type=jnp.float32
    )
    grad_probs = jnp.einsum(
        "eqhd,ekhd->ehqk", grad_mixed, values, preferred_element_type=jnp.float32
    )
    grad_scores = probs * (grad_probs - jnp.sum(probs * grad_probs, axis=-1, keepdims=True))
    grad_low = grad_scores.astype(jnp.bfloat16)
    grad_query = (
        jnp.einsum("ehqk,ekhd->eqhd", grad_low, keys, preferred_element_type=jnp.float32) * scale
    )
    grad_keys = (
        jnp.einsum("ehqk,eqhd->ekhd", grad_low, query, preferred_element_type=jnp.float32) * scale
    )
    return (grad_query, grad_keys, grad_values)


def window_layout(res_group, mem_col):
    small = 1 - res_group
    small_count = jnp.sum(small, axis=-1, keepdims=True)
    small_before = jnp.cumsum(small, axis=-1) - small
    large_before = jnp.cumsum(res_group, axis=-1) - res_group
    offset = jnp.where(
        res_group == 1, SLOT_S * small_count + SLOT_L * large_before, SLOT_S * small_before
    )
    start = jnp.minimum(offset, mem_col - SLOT_L)
    return (offset, start)


def take_windows(column, starts):
    return jax.vmap(lambda begin: lax.dynamic_slice_in_dim(column, begin, SLOT_L, 0))(starts)


def forward(decoder_rows, windows, cross_allowed, weights):
    (
        self_gain,
        self_qkv,
        self_out,
        cross_gain,
        cross_query,
        cross_kv,
        cross_out,
        ffn_gain,
        ffn_in,
        ffn_out,
    ) = weights
    count = decoder_rows.shape[0] // SUFFIX
    scale = HEAD_DIM ** (-0.5)
    row_index = lax.broadcasted_iota(jnp.int32, (SUFFIX, SUFFIX), 0)
    col_index = lax.broadcasted_iota(jnp.int32, (SUFFIX, SUFFIX), 1)
    causal = (row_index >= col_index)[None]
    resid = decoder_rows.reshape(count, SUFFIX, D)
    normed_one = layer_norm(resid, self_gain.astype(jnp.float32)).astype(jnp.bfloat16)
    packed = product(normed_one, self_qkv).astype(jnp.bfloat16)
    heads = packed.reshape(count, SUFFIX, 3, HEADS, HEAD_DIM)
    self_mixed, self_probs = attend(heads[:, :, 0], heads[:, :, 1], heads[:, :, 2], causal, scale)
    self_mixed = self_mixed.reshape(count, SUFFIX, D)
    after_self = resid + product(self_mixed, self_out)
    normed_two = layer_norm(after_self, cross_gain.astype(jnp.float32)).astype(jnp.bfloat16)
    cross_q = product(normed_two, cross_query).astype(jnp.bfloat16)
    window_kv = product(windows, cross_kv).astype(jnp.bfloat16)
    query_heads = cross_q.reshape(count, SUFFIX, HEADS, HEAD_DIM)
    kv_heads = window_kv.reshape(count, SLOT_L, 2, HEADS, HEAD_DIM)
    cross_mixed, cross_probs = attend(
        query_heads, kv_heads[:, :, 0], kv_heads[:, :, 1], cross_allowed, scale
    )
    cross_mixed = cross_mixed.reshape(count, SUFFIX, D)
    after_cross = after_self + product(cross_mixed, cross_out)
    normed_three = layer_norm(after_cross, ffn_gain.astype(jnp.float32)).astype(jnp.bfloat16)
    up = product(normed_three, ffn_in)
    act = jax.nn.gelu(up, approximate=True).astype(jnp.bfloat16)
    result = after_cross + product(act, ffn_out)
    return (
        resid,
        normed_one,
        packed,
        self_probs,
        self_mixed,
        after_self,
        normed_two,
        cross_q,
        window_kv,
        cross_probs,
        cross_mixed,
        after_cross,
        normed_three,
        up,
        act,
        result,
    )


def backward(grad_out, saved, weights):
    (
        self_gain,
        self_qkv,
        self_out,
        cross_gain,
        cross_query,
        cross_kv,
        cross_out,
        ffn_gain,
        ffn_in,
        ffn_out,
    ) = weights
    (
        resid,
        normed_one,
        packed,
        self_probs,
        self_mixed,
        after_self,
        normed_two,
        cross_q,
        window_kv,
        cross_probs,
        cross_mixed,
        after_cross,
        normed_three,
        up,
        act,
        result,
    ) = saved
    count = resid.shape[0]
    scale = HEAD_DIM ** (-0.5)
    grad_out = grad_out.reshape(count, SUFFIX, D)
    out_low = grad_out.astype(jnp.bfloat16)
    ffn_out_grad = outer_sum(act, out_low)
    act_grad = back_product(out_low, ffn_out)
    gelu_value, gelu_back = jax.vjp(partial(jax.nn.gelu, approximate=True), up)
    up_grad = gelu_back(act_grad)[0].astype(jnp.bfloat16)
    ffn_in_grad = outer_sum(normed_three, up_grad)
    normed_three_grad = back_product(up_grad, ffn_in)
    norm_value, norm_back = jax.vjp(layer_norm, after_cross, ffn_gain.astype(jnp.float32))
    resid_part, ffn_gain_grad = norm_back(normed_three_grad)
    cross_res_grad = grad_out + resid_part
    cross_low = cross_res_grad.astype(jnp.bfloat16)
    cross_out_grad = outer_sum(cross_mixed, cross_low)
    mixed_grad = (
        back_product(cross_low, cross_out)
        .astype(jnp.bfloat16)
        .reshape(count, SUFFIX, HEADS, HEAD_DIM)
    )
    query_heads = cross_q.reshape(count, SUFFIX, HEADS, HEAD_DIM)
    kv_heads = window_kv.reshape(count, SLOT_L, 2, HEADS, HEAD_DIM)
    query_grad, keys_grad, values_grad = attend_back(
        mixed_grad, query_heads, kv_heads[:, :, 0], kv_heads[:, :, 1], cross_probs, scale
    )
    cross_q_grad = query_grad.reshape(count, SUFFIX, D).astype(jnp.bfloat16)
    window_kv_grad = (
        jnp.stack((keys_grad, values_grad), axis=2)
        .reshape(count, SLOT_L, 2 * D)
        .astype(jnp.bfloat16)
    )
    cross_query_grad = outer_sum(normed_two, cross_q_grad)
    normed_two_grad = back_product(cross_q_grad, cross_query)
    norm_value, norm_back = jax.vjp(layer_norm, after_self, cross_gain.astype(jnp.float32))
    resid_part, cross_gain_grad = norm_back(normed_two_grad)
    self_res_grad = cross_res_grad + resid_part
    self_low = self_res_grad.astype(jnp.bfloat16)
    self_out_grad = outer_sum(self_mixed, self_low)
    mixed_grad = (
        back_product(self_low, self_out)
        .astype(jnp.bfloat16)
        .reshape(count, SUFFIX, HEADS, HEAD_DIM)
    )
    heads = packed.reshape(count, SUFFIX, 3, HEADS, HEAD_DIM)
    query_grad, keys_grad, values_grad = attend_back(
        mixed_grad, heads[:, :, 0], heads[:, :, 1], heads[:, :, 2], self_probs, scale
    )
    packed_grad = (
        jnp.stack((query_grad, keys_grad, values_grad), axis=2)
        .reshape(count, SUFFIX, 3 * D)
        .astype(jnp.bfloat16)
    )
    self_qkv_grad = outer_sum(normed_one, packed_grad)
    normed_one_grad = back_product(packed_grad, self_qkv)
    norm_value, norm_back = jax.vjp(layer_norm, resid, self_gain.astype(jnp.float32))
    resid_part, self_gain_grad = norm_back(normed_one_grad)
    decoder_grad = self_res_grad + resid_part
    weight_grads = (
        self_gain_grad,
        self_qkv_grad,
        self_out_grad,
        cross_gain_grad,
        cross_query_grad,
        cross_out_grad,
        ffn_gain_grad,
        ffn_in_grad,
        ffn_out_grad,
    )
    return (decoder_grad, window_kv_grad, weight_grads)


def make_placer(all_starts, lowest, own_rows):

    def place(total, piece, begin):

        def add_one(item, acc):
            relative = all_starts[item] - lowest
            inside = ((relative > -SLOT_L) & (relative < own_rows)).astype(jnp.float32)
            spot = jnp.clip(relative + SLOT_L, 0, own_rows + SLOT_L)
            current = lax.dynamic_slice_in_dim(acc, spot, SLOT_L, 0)
            added = current + piece[item].astype(jnp.float32) * inside
            return lax.dynamic_update_slice_in_dim(acc, added, spot, 0)

        return lax.fori_loop(0, piece.shape[0], add_one, total)

    return place


def body(
    decoder_in,
    memory,
    res_group,
    prefix_len,
    self_gain,
    self_qkv,
    self_out,
    cross_gain,
    cross_query,
    cross_kv,
    cross_out,
    ffn_gain,
    ffn_in,
    ffn_out,
    cotangent,
):
    count = prefix_len.shape[1]
    own_rows = memory.shape[1]
    mem_col = own_rows * lax.axis_size("dp")
    offset, start = window_layout(res_group, mem_col)
    all_starts = start[0]
    first = lax.axis_index("dp") * count
    own_offset = lax.dynamic_slice_in_dim(offset[0], first, count)
    own_start = lax.dynamic_slice_in_dim(all_starts, first, count)
    own_group = lax.dynamic_slice_in_dim(res_group[0], first, count)
    valid = jnp.where(own_group == 1, PATCH_L, PATCH_S) + prefix_len[0]
    positions = own_start[:, None] + jnp.arange(SLOT_L, dtype=jnp.int32)[None]
    cross_allowed = (
        (positions >= own_offset[:, None]) & (positions < (own_offset + valid)[:, None])
    )[:, None]
    weights = (
        lax.all_gather(self_gain, "fsdp", axis=0, tiled=True),
        lax.all_gather(self_qkv, "fsdp", axis=0, tiled=True),
        lax.all_gather(self_out, "fsdp", axis=0, tiled=True),
        lax.all_gather(cross_gain, "fsdp", axis=0, tiled=True),
        lax.all_gather(cross_query, "fsdp", axis=0, tiled=True),
        lax.all_gather(cross_kv, "fsdp", axis=0, tiled=True),
        lax.all_gather(cross_out, "fsdp", axis=0, tiled=True),
        lax.all_gather(ffn_gain, "fsdp", axis=0, tiled=True),
        lax.all_gather(ffn_in, "fsdp", axis=0, tiled=True),
        lax.all_gather(ffn_out, "fsdp", axis=0, tiled=True),
    )
    column = lax.all_gather(memory[0], "dp", axis=0, tiled=True)
    windows = take_windows(column, own_start)
    saved = forward(decoder_in[0], windows, cross_allowed, weights)
    decoder_out = saved[-1]
    weights = (
        lax.all_gather(self_gain, "fsdp", axis=0, tiled=True),
        lax.all_gather(self_qkv, "fsdp", axis=0, tiled=True),
        lax.all_gather(self_out, "fsdp", axis=0, tiled=True),
        lax.all_gather(cross_gain, "fsdp", axis=0, tiled=True),
        lax.all_gather(cross_query, "fsdp", axis=0, tiled=True),
        lax.all_gather(cross_kv, "fsdp", axis=0, tiled=True),
        lax.all_gather(cross_out, "fsdp", axis=0, tiled=True),
        lax.all_gather(ffn_gain, "fsdp", axis=0, tiled=True),
        lax.all_gather(ffn_in, "fsdp", axis=0, tiled=True),
        lax.all_gather(ffn_out, "fsdp", axis=0, tiled=True),
    )
    column = lax.all_gather(memory[0], "dp", axis=0, tiled=True)
    windows = take_windows(column, own_start)
    saved = forward(decoder_in[0], windows, cross_allowed, weights)
    whole_kv = weights[5]
    decoder_grad, window_kv_grad, local_grads = backward(cotangent[0], saved, weights)
    lowest = lax.axis_index("dp") * own_rows
    place = make_placer(all_starts, lowest, own_rows)
    empty = jnp.zeros((own_rows + 2 * SLOT_L, 2 * D), jnp.float32)
    summed = place(empty, lax.all_gather(window_kv_grad, "dp", axis=0, tiled=True), jnp.int32(0))
    own_kv_grad = summed[SLOT_L : SLOT_L + own_rows].astype(jnp.bfloat16)
    memory_grad = back_product(own_kv_grad, whole_kv)
    cross_kv_part = outer_sum(memory[0], own_kv_grad)
    grads = (
        local_grads[0],
        local_grads[1],
        local_grads[2],
        local_grads[3],
        local_grads[4],
        cross_kv_part,
        local_grads[5],
        local_grads[6],
        local_grads[7],
        local_grads[8],
    )
    shards = (
        lax.psum_scatter(
            grads[0].astype(jnp.bfloat16), "fsdp", scatter_dimension=0, tiled=True
        ).astype(jnp.float32),
        lax.psum_scatter(
            grads[1].astype(jnp.bfloat16), "fsdp", scatter_dimension=0, tiled=True
        ).astype(jnp.float32),
        lax.psum_scatter(
            grads[2].astype(jnp.bfloat16), "fsdp", scatter_dimension=0, tiled=True
        ).astype(jnp.float32),
        lax.psum_scatter(
            grads[3].astype(jnp.bfloat16), "fsdp", scatter_dimension=0, tiled=True
        ).astype(jnp.float32),
        lax.psum_scatter(
            grads[4].astype(jnp.bfloat16), "fsdp", scatter_dimension=0, tiled=True
        ).astype(jnp.float32),
        lax.psum_scatter(
            grads[5].astype(jnp.bfloat16), "fsdp", scatter_dimension=0, tiled=True
        ).astype(jnp.float32),
        lax.psum_scatter(
            grads[6].astype(jnp.bfloat16), "fsdp", scatter_dimension=0, tiled=True
        ).astype(jnp.float32),
        lax.psum_scatter(
            grads[7].astype(jnp.bfloat16), "fsdp", scatter_dimension=0, tiled=True
        ).astype(jnp.float32),
        lax.psum_scatter(
            grads[8].astype(jnp.bfloat16), "fsdp", scatter_dimension=0, tiled=True
        ).astype(jnp.float32),
        lax.psum_scatter(
            grads[9].astype(jnp.bfloat16), "fsdp", scatter_dimension=0, tiled=True
        ).astype(jnp.float32),
    )
    totals = (
        lax.psum(shards[0].astype(jnp.bfloat16), "dp").astype(jnp.float32),
        lax.psum(shards[1].astype(jnp.bfloat16), "dp").astype(jnp.float32),
        lax.psum(shards[2].astype(jnp.bfloat16), "dp").astype(jnp.float32),
        lax.psum(shards[3].astype(jnp.bfloat16), "dp").astype(jnp.float32),
        lax.psum(shards[4].astype(jnp.bfloat16), "dp").astype(jnp.float32),
        lax.psum(shards[5].astype(jnp.bfloat16), "dp").astype(jnp.float32),
        lax.psum(shards[6].astype(jnp.bfloat16), "dp").astype(jnp.float32),
        lax.psum(shards[7].astype(jnp.bfloat16), "dp").astype(jnp.float32),
        lax.psum(shards[8].astype(jnp.bfloat16), "dp").astype(jnp.float32),
        lax.psum(shards[9].astype(jnp.bfloat16), "dp").astype(jnp.float32),
    )
    return (
        decoder_out,
        decoder_grad,
        memory_grad[None],
        totals[0],
        totals[1],
        totals[2],
        totals[3],
        totals[4],
        totals[5],
        totals[6],
        totals[7],
        totals[8],
        totals[9],
    )


def solution(mesh):
    placed = (
        P("fsdp", "dp", None),
        P("fsdp", "dp", None),
        P("fsdp", None),
        P("fsdp", "dp"),
        P("fsdp"),
        P("fsdp", None),
        P("fsdp", None),
        P("fsdp"),
        P("fsdp", None),
        P("fsdp", None),
        P("fsdp", None),
        P("fsdp"),
        P("fsdp", None),
        P("fsdp", None),
        P("fsdp", "dp", None),
    )
    return jax.shard_map(
        body,
        mesh=mesh,
        in_specs=placed,
        out_specs=(
            P("fsdp", "dp", None),
            P("fsdp", "dp", None),
            P("fsdp", "dp", None),
            P("fsdp"),
            P("fsdp", None),
            P("fsdp", None),
            P("fsdp"),
            P("fsdp", None),
            P("fsdp", None),
            P("fsdp", None),
            P("fsdp"),
            P("fsdp", None),
            P("fsdp", None),
        ),
        check_vma=False,
    )
```

profile of v0, /device:TPU:3, one launch (start us, length us, event | category | flops | bytes accessed | tf_op | source)
XLA Modules:
  0.0 1345.8 jit_solution(18367103486183297066)
XLA Ops:
  33.7 26.6 %all-gather.14.cloned.1.call-done = bf16[768,2304]{1,0:T(8,128)(2,1)} async-done(((bf16[384,2304]{1,0:T(8,128)(2,1)}), bf16[768,2304]{1,0:T(8,128)(2,1)}) %all-gather.14.cloned.1.call-update) | async-done | bytes 3538960 | tf_op jit(solution)/shard_map/all_gather | solution.py:304
  64.7 19.9 %all-gather.16.cloned.1.call-done = bf16[768,768]{1,0:T(8,128)(2,1)} async-done(((bf16[384,768]{1,0:T(8,128)(2,1)}), bf16[768,768]{1,0:T(8,128)(2,1)}) %all-gather.16.cloned.1.call-update) | async-done | bytes 1179664 | tf_op jit(solution)/shard_map/all_gather | solution.py:305
  86.6 22.4 %all-gather.20.cloned.1.call-done = bf16[768,768]{1,0:T(8,128)(2,1)} async-done(((bf16[384,768]{1,0:T(8,128)(2,1)}), bf16[768,768]{1,0:T(8,128)(2,1)}) %all-gather.20.cloned.1.call-update) | async-done | bytes 1179664 | tf_op jit(solution)/shard_map/all_gather | solution.py:307
  110.8 107.3 %all-gather.30.cloned.1.call-done = bf16[1,6688,768]{2,0,1:T(2,128)(2,1)} async-done(((bf16[1,418,768]{2,0,1:T(2,128)(2,1)}), bf16[1,6688,768]{2,0,1:T(2,128)(2,1)}) %all-gather.30.cloned.1.call-update) | async-done | bytes 10272784 | tf_op jit(solution)/shard_map/all_gather | solution.py:314
  221.6 33.8 %all-gather.18.cloned.1.call-done = bf16[768,1536]{1,0:T(8,128)(2,1)} async-done(((bf16[384,1536]{1,0:T(8,128)(2,1)}), bf16[768,1536]{1,0:T(8,128)(2,1)}) %all-gather.18.cloned.1.call-update) | async-done | bytes 2359312 | tf_op jit(solution)/shard_map/all_gather | solution.py:308
  266.2 13.5 %all-gather.22.cloned.1.call-done = bf16[768,768]{1,0:T(8,128)(2,1)} async-done(((bf16[384,768]{1,0:T(8,128)(2,1)}), bf16[768,768]{1,0:T(8,128)(2,1)}) %all-gather.22.cloned.1.call-update) | async-done | bytes 1179664 | tf_op jit(solution)/shard_map/all_gather | solution.py:309
  281.6 62.2 %all-gather.24.cloned.1.call-done = bf16[768,3072]{1,0:T(8,128)(2,1)} async-done(((bf16[384,3072]{1,0:T(8,128)(2,1)}), bf16[768,3072]{1,0:T(8,128)(2,1)}) %all-gather.24.cloned.1.call-update) | async-done | bytes 4718608 | tf_op jit(solution)/shard_map/all_gather | solution.py:311
  347.2 60.9 %all-gather.26.cloned.1.call-done = bf16[3072,768]{1,0:T(8,128)(2,1)} async-done(((bf16[1536,768]{1,0:T(8,128)(2,1)}), bf16[3072,768]{1,0:T(8,128)(2,1)}) %all-gather.26.cloned.1.call-update) | async-done | bytes 4718608 | tf_op jit(solution)/shard_map/all_gather | solution.py:312
  424.4 150.8 %all-gather.28.cloned.1.call-done = bf16[16,608,1536]{2,1,0:T(8,128)(2,1)} async-done(((bf16[1,608,1536]{2,1,0:T(8,128)(2,1)}), bf16[16,608,1536]{2,1,0:T(8,128)(2,1)}) %all-gather.28.cloned.1.call-update) | async-done | bytes 29884432 | tf_op jit(solution)/shard_map/all_gather | solution.py:338
  580.4 257.6 %while.14 = (s32[]{:T(128)}, f32[1634,1536]{1,0:T(8,128)}, s32[16]{0:T(128)S(1)}, s32[]{:T(128)}, bf16[16,608,1536]{2,1,0:T(8,128)(2,1)}, /*index=5*/s32[]{:T(12...) while((s32[]{:T(128)}, f32[1634,1536]{1,0:T(8,128)}, s32[16]{0:T(128)S(1)}, ...), condition=%wide.region_22.23_spmd, body=%wide.region_21.22_spmd.sunk | while | flops 2801674 | bytes 16810204 | solution.py:266
  602.8 9.7 dynamic_update_slice.8
  618.9 9.7 dynamic_update_slice.8
  635.0 9.7 dynamic_update_slice.8
  667.2 9.7 dynamic_update_slice.8
  683.3 9.7 dynamic_update_slice.8
  715.5 9.7 dynamic_update_slice.8
  731.6 9.7 dynamic_update_slice.8
  747.7 9.7 dynamic_update_slice.8
  763.8 9.7 dynamic_update_slice.8
  779.9 9.7 dynamic_update_slice.8
  796.0 9.7 dynamic_update_slice.8
  812.1 9.7 dynamic_update_slice.8
  828.2 9.7 dynamic_update_slice.8
  868.2 13.0 reduce-scatter.22.cloned.1.call-done
  883.6 22.3 %reduce-scatter.12.cloned.1.call-done = bf16[384,768]{1,0:T(8,128)(2,1)} async-done(((bf16[768,768]{1,0:T(8,128)(2,1)}), bf16[384,768]{1,0:T(8,128)(2,1)}) %reduce-scatter.12.cloned.1.call-update) | async-done | bytes 589840 | tf_op jit(solution)/shard_map/reduce_scatter | solution.py:361
  906.0 24.5 %reduce-scatter.14.cloned.1.call-done = bf16[384,768]{1,0:T(8,128)(2,1)} async-done(((bf16[768,768]{1,0:T(8,128)(2,1)}), bf16[384,768]{1,0:T(8,128)(2,1)}) %reduce-scatter.14.cloned.1.call-update) | async-done | bytes 589840 | tf_op jit(solution)/shard_map/reduce_scatter | solution.py:367
  930.4 24.7 %reduce-scatter.16.cloned.1.call-done = bf16[384,768]{1,0:T(8,128)(2,1)} async-done(((bf16[768,768]{1,0:T(8,128)(2,1)}), bf16[384,768]{1,0:T(8,128)(2,1)}) %reduce-scatter.16.cloned.1.call-update) | async-done | bytes 589840 | tf_op jit(solution)/shard_map/reduce_scatter | solution.py:373
  955.1 50.4 %reduce-scatter.10.cloned.1.call-done = bf16[384,2304]{1,0:T(8,128)(2,1)} async-done(((bf16[768,2304]{1,0:T(8,128)(2,1)}), bf16[384,2304]{1,0:T(8,128)(2,1)}) %reduce-scatter.10.cloned.1.call-update) | async-done | bytes 1769488 | tf_op jit(solution)/shard_map/reduce_scatter | solution.py:358
  1005.5 62.9 %reduce-scatter.18.cloned.1.call-done = bf16[384,3072]{1,0:T(8,128)(2,1)} async-done(((bf16[768,3072]{1,0:T(8,128)(2,1)}), bf16[384,3072]{1,0:T(8,128)(2,1)}) %reduce-scatter.18.cloned.1.call-update) | async-done | bytes 2359312 | tf_op jit(solution)/shard_map/reduce_scatter | solution.py:379
  1068.3 62.8 %reduce-scatter.20.cloned.1.call-done = bf16[1536,768]{1,0:T(8,128)(2,1)} async-done(((bf16[3072,768]{1,0:T(8,128)(2,1)}), bf16[1536,768]{1,0:T(8,128)(2,1)}) %reduce-scatter.20.cloned.1.call-update) | async-done | bytes 2359312 | tf_op jit(solution)/shard_map/reduce_scatter | solution.py:382
  1140.7 27.5 %all-reduce.3 = (bf16[384]{0:T(512)(128)(2,1)S(1)}, bf16[384]{0:T(512)(128)(2,1)S(1)}, bf16[384]{0:T(512)(128)(2,1)S(1)}) all-reduce(bf16[384]{0:T(512)(128)(2,1)S(1)} %dynamic-slice.9, bf16[384]{0:T(512)(128)(2,1)S(1)} %dynamic-slice.11, bf16[384]{0:T(512)(128)(2,1)S(1)} %dynamic-slice.13), channel_id=1, replica_groups=mesh['dp'=16,'fsdp'=2] {'dp'}, use_global_device_ids=true, to_apply=%region_25.26 | all-reduce | flops 1152 | bytes 4608 | tf_op jit(solution)/shard_map/psum | solution.py:387
  1182.9 141.3 %all-reduce.8.cloned.1.call-done = (bf16[384,1536]{0,1:T(8,128)(2,1)}, bf16[384,2304]{1,0:T(8,128)(2,1)}, bf16[384,768]{1,0:T(8,128)(2,1)}, bf16[384,768]{1,0:T(...) async-done(((bf16[384,1536]{0,1:T(8,128)(2,1)}, bf16[384,2304]{1,0:T(8,128)(2,1)}, bf16[384,768]{1,0:T(8,128)(2,1)}, ...) | async-done | bytes 9437200 | tf_op jit(solution)/shard_map/psum | solution.py:392
  (310 shorter events, 262.7 us)
Async XLA Ops:
  7.2 53.1 %all-gather.14.cloned.1.call-start = ((), (), s32[]{:S(2)}) async-start(), calls=%async_computation.7 | async-start | bytes 5308416 | tf_op jit(solution)/shard_map/all_gather | solution.py:304
  7.9 76.7 %all-gather.16.cloned.1.call-start = ((), (), s32[]{:S(2)}) async-start(), calls=%async_computation.8 | async-start | bytes 1769472 | tf_op jit(solution)/shard_map/all_gather | solution.py:305
  8.7 100.3 %all-gather.20.cloned.1.call-start = ((), (), s32[]{:S(2)}) async-start(), calls=%async_computation.10 | async-start | bytes 1769472 | tf_op jit(solution)/shard_map/all_gather | solution.py:307
  9.4 208.7 %all-gather.30.cloned.1.call-start = ((), (), s32[]{:S(2)}) async-start(), calls=%async_computation.21 | async-start | bytes 21829632 | tf_op jit(solution)/shard_map/all_gather | solution.py:314
  11.5 243.8 %all-gather.18.cloned.1.call-start = ((), (), s32[]{:S(2)}) async-start(), calls=%async_computation.9 | async-start | bytes 3538944 | tf_op jit(solution)/shard_map/all_gather | solution.py:308
  12.1 267.6 %all-gather.22.cloned.1.call-start = ((), (), s32[]{:S(2)}) async-start(), calls=%async_computation.11 | async-start | bytes 1769472 | tf_op jit(solution)/shard_map/all_gather | solution.py:309
  12.8 331.1 %all-gather.24.cloned.1.call-start = ((), (), s32[]{:S(2)}) async-start(), calls=%async_computation.12 | async-start | bytes 7077888 | tf_op jit(solution)/shard_map/all_gather | solution.py:311
  13.5 394.6 %all-gather.26.cloned.1.call-start = ((), (), s32[]{:S(2)}) async-start(), calls=%async_computation.13 | async-start | bytes 7077888 | tf_op jit(solution)/shard_map/all_gather | solution.py:312
  14.3 561.0 %all-gather.28.cloned.1.call-start = ((), (), s32[]{:S(2)}) async-start(), calls=%async_computation.14 | async-start | bytes 31752192 | tf_op jit(solution)/shard_map/all_gather | solution.py:338
  63.4 47.4 %copy-start.28 = (bf16[1,32,1,12,64]{4,3,2,1,0:T(8,128)(2,1)}, bf16[1,32,1,12,64]{4,3,2,1,0:T(8,128)(2,1)S(1)}, u32[]{:S(2)}) copy-start(bf16[1,32,1,12,64]{4,3,2,1,0:T(8,128)(2,1)S(1)} %get-tuple-element.209) | copy-start | bytes 147460
  63.4 47.4 %copy-start.30 = (bf16[1,32,1,12,64]{4,3,2,1,0:T(8,128)(2,1)}, bf16[1,32,1,12,64]{4,3,2,1,0:T(8,128)(2,1)S(1)}, u32[]{:S(2)}) copy-start(bf16[1,32,1,12,64]{4,3,2,1,0:T(8,128)(2,1)S(1)} %get-tuple-element.208) | copy-start | bytes 147460
  63.6 154.5 %copy-start.43 = (f32[12,32]{1,0:T(8,128)}, f32[12,32]{1,0:T(8,128)S(1)}, u32[]{:S(2)}) copy-start(f32[12,32]{1,0:T(8,128)S(1)} %get-tuple-element.213) | copy-start | bytes 4612
  64.7 153.4 %copy-start.24 = (bf16[32,768]{1,0:T(8,128)(2,1)}, bf16[32,768]{1,0:T(8,128)(2,1)S(1)}, u32[]{:S(2)}) copy-start(bf16[32,768]{1,0:T(8,128)(2,1)S(1)} %reshape.596) | copy-start | bytes 147460
  86.3 131.8 %copy-start.41 = (f32[32]{0:T(128)}, f32[32]{0:T(128)S(1)}, u32[]{:S(2)}) copy-start(f32[32]{0:T(128)S(1)} %broadcast_multiply_fusion.1) | copy-start | bytes 388
  86.5 131.6 %copy-start.56 = (f32[32]{0:T(128)}, f32[32]{0:T(128)S(1)}, u32[]{:S(2)}) copy-start(f32[32]{0:T(128)S(1)} %multiply_reduce_fusion.3) | copy-start | bytes 388
  86.6 131.6 %copy-start.50 = (f32[32]{0:T(128)}, f32[32]{0:T(128)S(1)}, u32[]{:S(2)}) copy-start(f32[32]{0:T(128)S(1)} %fusion.68) | copy-start | bytes 388
  110.8 151.9 %copy-start.18 = (bf16[32,12,64]{2,1,0:T(8,128)(2,1)}, bf16[32,12,64]{2,1,0:T(8,128)(2,1)S(1)}, u32[]{:S(2)}) copy-start(bf16[32,12,64]{2,1,0:T(8,128)(2,1)S(1)} %reshape.601) | copy-start | bytes 147460
  262.7 155.9 %copy-start.8 = (bf16[608,1536]{0,1:T(8,128)(2,1)}, bf16[608,1536]{0,1:T(8,128)(2,1)S(1)}, u32[]{:S(2)}) copy-start(bf16[608,1536]{0,1:T(8,128)(2,1)S(1)} %copy.90) | copy-start | bytes 5603332
  281.4 578.8 %copy-start.4 = (f32[1,32,768]{2,1,0:T(8,128)}, f32[1,32,768]{2,1,0:T(8,128)S(1)}, u32[]{:S(2)}) copy-start(f32[1,32,768]{2,1,0:T(8,128)S(1)} %get-tuple-element.222) | copy-start | bytes 294916
  281.4 132.8 %copy-start.39 = (f32[32]{0:T(128)}, f32[32]{0:T(128)S(1)}, u32[]{:S(2)}) copy-start(f32[32]{0:T(128)S(1)} %broadcast_multiply_fusion) | copy-start | bytes 388
  281.6 132.6 %copy-start.48 = (f32[32]{0:T(128)}, f32[32]{0:T(128)S(1)}, u32[]{:S(2)}) copy-start(f32[32]{0:T(128)S(1)} %fusion.69) | copy-start | bytes 388
  281.6 126.5 %copy-start.17 = (f32[1,32,768]{2,1,0:T(8,128)S(1)}, f32[1,32,768]{2,1,0:T(8,128)}, u32[]{:S(2)}) copy-start(f32[1,32,768]{2,1,0:T(8,128)} %param.31) | copy-start | bytes 294916
  347.2 517.4 %copy-start.2 = (f32[32,3072]{1,0:T(8,128)}, f32[32,3072]{1,0:T(8,128)S(1)}, u32[]{:S(2)}) copy-start(f32[32,3072]{1,0:T(8,128)S(1)} %fusion.73) | copy-start | bytes 1179652
  424.2 457.1 %reduce-scatter.22.cloned.1.call-start = ((), (), s32[]{:S(2)}) async-start(), calls=%async_computation.22 | async-start | bytes 3538944
  580.4 257.6 %copy-start.21 = (bf16[1,418,768]{2,1,0:T(8,128)(2,1)S(1)}, bf16[1,418,768]{2,1,0:T(8,128)(2,1)}, u32[]{:S(2)}) copy-start(bf16[1,418,768]{2,1,0:T(8,128)(2,1)} %param.18) | copy-start | bytes 1926148
  846.9 59.1 %reduce-scatter.12.cloned.1.call-start = ((), (), s32[]{:S(2)}) async-start(), calls=%async_computation.16 | async-start | bytes 1769472 | tf_op jit(solution)/shard_map/reduce_scatter | solution.py:361
  851.8 78.6 %reduce-scatter.14.cloned.1.call-start = ((), (), s32[]{:S(2)}) async-start(), calls=%async_computation.17 | async-start | bytes 1769472 | tf_op jit(solution)/shard_map/reduce_scatter | solution.py:367
  853.5 101.6 %reduce-scatter.16.cloned.1.call-start = ((), (), s32[]{:S(2)}) async-start(), calls=%async_computation.18 | async-start | bytes 1769472 | tf_op jit(solution)/shard_map/reduce_scatter | solution.py:373
  855.1 150.4 %reduce-scatter.10.cloned.1.call-start = ((), (), s32[]{:S(2)}) async-start(), calls=%async_computation.15 | async-start | bytes 5308416 | tf_op jit(solution)/shard_map/reduce_scatter | solution.py:358
  860.1 208.2 %reduce-scatter.18.cloned.1.call-start = ((), (), s32[]{:S(2)}) async-start(), calls=%async_computation.19 | async-start | bytes 7077888 | tf_op jit(solution)/shard_map/reduce_scatter | solution.py:379
  864.5 266.6 %reduce-scatter.20.cloned.1.call-start = ((), (), s32[]{:S(2)}) async-start(), calls=%async_computation.20 | async-start | bytes 7077888 | tf_op jit(solution)/shard_map/reduce_scatter | solution.py:382
  868.2 456.0 %all-reduce.8.cloned.1.call-start = ((), (), s32[]{:S(2)}) async-start(), calls=%async_computation.23 | async-start | bytes 18874368 | tf_op jit(solution)/shard_map/psum | solution.py:392
  (47 other events, 280.0 us)
Sparse Core Ops, SparseCore 0:
  9.6 50.6 all-gather.13
  61.8 22.7 all-gather.15
  86.2 22.7 all-gather.19
  111.0 107.0 all-gather.29
  219.5 35.8 all-gather.17
  256.8 22.8 all-gather.21
  281.2 62.5 all-gather.23
  345.4 62.6 all-gather.25
  424.3 150.9 all-gather.27
  847.0 34.2 reduce-scatter.21
  884.2 21.7 reduce-scatter.11
  908.6 21.7 reduce-scatter.13
  933.3 21.7 reduce-scatter.15
  957.8 47.6 reduce-scatter.9
  1008.3 59.9 reduce-scatter.17
  1071.1 59.9 reduce-scatter.19
  1136.8 187.3 all-reduce.7
where the time goes:
time: 1350 us
  waiting for transfers between devices  904 us (67%)
  local copies, waits for them, and re-layouts  197 us (15%)
  other arithmetic  109 us (8%)
  matrix products  63.1 us (5%)
  blocking collectives  41.7 us (3%)
  between operations  19.5 us (1%)
    dynamic_update_slice x16, local copies, waits for them, and re-layouts, add_one(): return lax.dynamic_update_slice_in_dim(acc, added, spot, 0)  155 us
    all_gather x1, waiting for transfers between devices, body(): lax.all_gather(window_kv_grad, 'dp', axis=0, tiled=True)  151 us
    psum x1, waiting for transfers between devices, body(): lax.psum(shards[5].astype(jnp.bfloat16), 'dp').astype(jnp.float32)  141 us
    all_gather x1, waiting for transfers between devices, body(): column = lax.all_gather(memory[0], 'dp', axis=0, tiled=True)  107 us
    add x16, other arithmetic, add_one(): added = current + piece[item].astype(jnp.float32) * inside  82.6 us
    reduce_scatter x1, waiting for transfers between devices, body(): lax.psum_scatter(grads[8].astype(jnp.bfloat16), 'fsdp', scatter_dimension...  62.9 us
    reduce_scatter x1, waiting for transfers between devices, body(): lax.psum_scatter(grads[9].astype(jnp.bfloat16), 'fsdp', scatter_dimension...  62.8 us
    all_gather x1, waiting for transfers between devices, body(): lax.all_gather(ffn_in, 'fsdp', axis=0, tiled=True)  62.2 us
  transfers between devices with their start and end apart: 17, of which 17 were waited for; matrix products, arithmetic and copies ran while one was open for 6% of the time, Pallas kernels for 0%

commit v1 on v0

--- a/solution.py
+++ b/solution.py
@@ -3,6 +3,8 @@
 import jax
 import jax.numpy as jnp
 from jax import lax
+from jax.experimental import pallas as pl
+from jax.experimental.pallas import tpu as pltpu
 from jax.sharding import PartitionSpec as P
 
 D = 768
@@ -13,9 +15,978 @@
 PATCH_L = 576
 SLOT_S = 228
 SLOT_L = 608
-
-
+RING = 4
+SIDE = 2
+CORES = 2
 norm_eps = 1e-06
+MESH = pl.DeviceIdType.MESH
+F32 = jnp.float32
+BF16 = jnp.bfloat16
+NONE = -1e30
+
+
+def mm(left, right):
+    return jnp.dot(left, right, preferred_element_type=F32)
+
+
+def mm_nt(left, right):
+    return lax.dot_general(left, right, (((1,), (1,)), ((), ())), preferred_element_type=F32)
+
+
+def mm_tn(left, right):
+    return lax.dot_general(left, right, (((0,), (0,)), ((), ())), preferred_element_type=F32)
+
+
+def normed(value):
+    mean = jnp.mean(value, axis=-1, keepdims=True)
+    centred = value - mean
+    variance = jnp.mean(centred * centred, axis=-1, keepdims=True)
+    scale = lax.rsqrt(variance + norm_eps)
+    return centred * scale, scale
+
+
+def norm_back(grad, hat, scale, gain):
+    inner = grad * gain
+    mean_one = jnp.mean(inner, axis=-1, keepdims=True)
+    mean_two = jnp.mean(inner * hat, axis=-1, keepdims=True)
+    gain_grad = jnp.sum(grad * hat, axis=0, keepdims=True)
+    return scale * (inner - mean_one - hat * mean_two), gain_grad
+
+
+def gelu_parts(up):
+    inner = 0.7978845608 * (up + 0.044715 * up * up * up)
+    tanh = jnp.tanh(inner)
+    slope = 0.7978845608 * (1.0 + 3.0 * 0.044715 * up * up)
+    value = 0.5 * up * (1.0 + tanh)
+    grad = 0.5 * (1.0 + tanh) + 0.5 * up * (1.0 - tanh * tanh) * slope
+    return value, grad
+
+
+class Gather:
+    def __init__(self, place, view, width, sems, at):
+        self.z, self.x, self.c, self.f = place
+        self.view = view
+        half = (width // 256) * 128
+        self.halves = ((0, half), (half, width - half))
+        self.send, self.recv = sems
+        self.at = at
+        self.sent = []
+
+    def dev(self, z, x, c):
+        return (z * (SIDE * CORES) + x * CORES + c, self.f)
+
+    def copy(self, block, half, target, into):
+        z, x, c = block
+        ref = self.view(z, x, c, self.halves[half] if half is not None else None)
+        return pltpu.make_async_remote_copy(
+            src_ref=ref,
+            dst_ref=ref,
+            send_sem=self.send.at[self.at, len(self.sent)],
+            recv_sem=self.recv.at[self.at, into],
+            device_id=self.dev(*target),
+            device_id_type=MESH,
+        )
+
+    def go(self, block, half, target, into):
+        item = self.copy(block, half, target, into)
+        item.start()
+        self.sent.append(item)
+
+    def wait(self, block, half, into):
+        z, x, c = block
+        ref = self.view(z, x, c, self.halves[half] if half is not None else None)
+        pltpu.make_async_remote_copy(
+            src_ref=ref,
+            dst_ref=ref,
+            send_sem=self.send.at[self.at, 0],
+            recv_sem=self.recv.at[self.at, into],
+            device_id=self.dev(self.z, 1 - self.x, self.c),
+            device_id_type=MESH,
+        ).wait_recv()
+
+    def names(self):
+        z, x, c = self.z, self.x, self.c
+        up, down, far = lax.rem(z + 1, RING), lax.rem(z + 3, RING), lax.rem(z + 2, RING)
+        return z, x, c, up, down, far
+
+    def step_one(self):
+        z, x, c, up, down, far = self.names()
+        own = (z, x, c)
+        self.go(own, None, (z, 1 - x, c), 0)
+        self.go(own, None, (up, x, c), 1)
+        self.go(own, None, (down, x, c), 2)
+        self.go(own, None, (z, x, 1 - c), 8)
+
+    def step_two(self):
+        z, x, c, up, down, far = self.names()
+        mate = (z, x, 1 - c)
+        self.wait((z, 1 - x, c), None, 0)
+        self.go((z, 1 - x, c), None, (up, x, c), 5)
+        self.go((z, 1 - x, c), None, (down, x, c), 6)
+        self.go((z, 1 - x, c), None, mate, 9)
+        self.wait((down, x, c), None, 1)
+        self.go((down, x, c), 0, (up, x, c), 3)
+        self.go((down, x, c), None, mate, 10)
+        self.wait((up, x, c), None, 2)
+        self.go((up, x, c), 1, (down, x, c), 4)
+        self.go((up, x, c), None, mate, 11)
+
+    def step_three(self):
+        z, x, c, up, down, far = self.names()
+        mate = (z, x, 1 - c)
+        self.wait((far, x, c), 0, 3)
+        self.wait((far, x, c), 1, 4)
+        self.go((far, x, c), None, (z, 1 - x, c), 7)
+        self.go((far, x, c), None, mate, 12)
+        self.wait((down, 1 - x, c), None, 5)
+        self.go((down, 1 - x, c), None, mate, 13)
+        self.wait((up, 1 - x, c), None, 6)
+        self.go((up, 1 - x, c), None, mate, 14)
+
+    def step_four(self):
+        z, x, c, up, down, far = self.names()
+        mate = (z, x, 1 - c)
+        self.wait((far, 1 - x, c), None, 7)
+        self.go((far, 1 - x, c), None, mate, 15)
+        o = 1 - c
+        self.wait((z, x, o), None, 8)
+        self.wait((z, 1 - x, o), None, 9)
+        self.wait((down, x, o), None, 10)
+        self.wait((up, x, o), None, 11)
+        self.wait((far, x, o), None, 12)
+        self.wait((down, 1 - x, o), None, 13)
+        self.wait((up, 1 - x, o), None, 14)
+        self.wait((far, 1 - x, o), None, 15)
+
+    def finish(self):
+        for item in self.sent:
+            item.wait_send()
+
+
+class Pieces:
+    def __init__(self, count, own_rows):
+        self.half = count // 2
+        self.edge = self.half * SLOT_S
+        self.rows = own_rows
+        self.count = count
+
+    def start(self, rank):
+        return jnp.where(
+            rank < self.half, SLOT_S * rank, self.edge + SLOT_L * (rank - self.half)
+        )
+
+    def size(self, rank):
+        return jnp.where(rank < self.half, SLOT_S, SLOT_L)
+
+    def rank_of(self, row):
+        return jnp.where(
+            row < self.edge,
+            lax.div(row, SLOT_S),
+            self.half + lax.div(jnp.maximum(row - self.edge, 0), SLOT_L),
+        )
+
+    def first_rank(self, device):
+        return self.rank_of(device * self.rows)
+
+    def last_rank(self, device):
+        return self.rank_of(device * self.rows + self.rows - 1)
+
+    def first_device(self, rank):
+        return lax.div(self.start(rank), self.rows)
+
+    def last_device(self, rank):
+        return lax.div(self.start(rank) + self.size(rank) - 1, self.rows)
+
+
+SLOTS = 3
+LANE_QKV, LANE_SO, LANE_CQ, LANE_CKV, LANE_CO, LANE_FI, LANE_FO = 0, 2304, 3072, 3840, 5376, 6144, 9216
+UNITS = 16
+KV_UNITS = (5, 6)
+TOKEN_UNITS = tuple(u for u in range(UNITS) if u not in KV_UNITS)
+GROUPS = ((0, 2304), (2304, 3072), (5376, 6912))
+
+
+def layer_kernel(
+    ranks,
+    columns,
+    x_ref, cot_ref, mem_ref, res_ref, pre_ref, gains_ref,
+    qkv_ref, so_ref, cq_ref, ckv_ref, co_ref, fi_ref, fo_ref,
+    out_ref, grad_ref, memgrad_ref, gain_out_ref, weights_out_ref,
+    wb, gb, rb, sb, xb, cb, ob, gainb, memp, kvb, kvg, kp, kr, kc, cp,
+    cqb, qbuf, osend, ostat_send, obuf, ostat, dob, dstat_b, dobuf, dstat, dqsend, dqbuf, gmine, gpeer,
+    load_sem, gsend, grecv, ysend, yrecv, psend, precv, usend, urecv, ksend, krecv,
+):
+    me = lax.axis_index("dp")
+    f = lax.axis_index("fsdp")
+    z = lax.div(me, SIDE * CORES)
+    x = lax.rem(lax.div(me, CORES), SIDE)
+    c = lax.rem(me, CORES)
+    chip = lax.div(me, CORES)
+    chips = ranks // CORES
+    place = (z, x, c, f)
+    half_rows = D // columns
+    slab = half_rows // chips
+    own_rows = mem_ref.shape[0]
+    padded = memp.shape[0]
+    lay = Pieces(ranks, own_rows)
+    other = 1 - f
+    everyone = ranks * columns
+    lin = f * ranks + me
+
+    loads = []
+
+    def load(src, lane, width):
+        item = pltpu.make_async_copy(
+            src, wb.at[pl.ds(pl.multiple_of(f * half_rows, 128), half_rows), pl.ds(lane, width)],
+            load_sem.at[len(loads)],
+        )
+        item.start()
+        loads.append(item)
+
+    load(qkv_ref, LANE_QKV, 2304)
+    load(so_ref, LANE_SO, 768)
+    load(cq_ref, LANE_CQ, 768)
+    load(ckv_ref, LANE_CKV, 1536)
+    load(co_ref, LANE_CO, 768)
+    load(fi_ref, LANE_FI, 3072)
+    for j in range(4):
+        load(fo_ref.at[pl.ds(j * half_rows, half_rows)], LANE_FO + 768 * j, 768)
+
+    for s in range(SLOTS):
+        qbuf[s] = jnp.zeros_like(qbuf[s])
+        obuf[s] = jnp.zeros_like(obuf[s])
+        ostat[s, 0] = jnp.full_like(ostat[s, 0], NONE)
+        ostat[s, 1] = jnp.zeros_like(ostat[s, 1])
+        dobuf[s] = jnp.zeros_like(dobuf[s])
+        dstat[s] = jnp.zeros_like(dstat[s])
+        dqbuf[s] = jnp.zeros_like(dqbuf[s])
+
+    xb[me, 0:SUFFIX] = x_ref[...]
+    xb[me, SUFFIX : SUFFIX + 8] = jnp.full((8, D), pre_ref[0, 0].astype(F32), F32)
+    cb[me] = cot_ref[...]
+    gainb[f] = gains_ref[...]
+
+    barrier = pltpu.get_barrier_semaphore()
+
+    def greet(i, carry):
+        to = lax.rem(lin + i, everyone)
+        pl.semaphore_signal(
+            barrier, inc=1, device_id=(lax.rem(to, ranks), lax.div(to, ranks)), device_id_type=MESH
+        )
+        return carry
+
+    lax.fori_loop(1, everyone, greet, 0)
+    pl.semaphore_wait(barrier, everyone - 1)
+
+    y_items = []
+
+    def push_y(ref, at):
+        item = pltpu.make_async_remote_copy(
+            src_ref=ref, dst_ref=ref, send_sem=ysend.at[at], recv_sem=yrecv.at[at],
+            device_id=(me, other), device_id_type=MESH,
+        )
+        item.start()
+        y_items.append(item)
+        return item
+
+    def slab_view(first, width, mine):
+        half = width // CORES
+        rows_from = f if mine else other
+
+        def view(zz, xx, cc, part):
+            low, size = part if part is not None else (0, half)
+            row = pl.multiple_of(rows_from * half_rows + (zz * SIDE + xx) * slab, 16)
+            lane = pl.multiple_of(first + cc * half + low, 128)
+            return wb.at[pl.ds(row, slab), pl.ds(lane, size)]
+
+        return view
+
+    sems = (gsend, grecv)
+    ag_x = Gather(place, lambda zz, xx, cc, part: xb.at[zz * 4 + xx * 2 + cc] if part is None else xb.at[zz * 4 + xx * 2 + cc, :, pl.ds(*part)], D, sems, 0)
+    ag_w = [
+        Gather(place, slab_view(first, width, False), width // CORES, sems, 1 + n)
+        for n, (first, width) in enumerate(GROUPS)
+    ]
+    ag_c = Gather(place, lambda zz, xx, cc, part: cb.at[zz * 4 + xx * 2 + cc] if part is None else cb.at[zz * 4 + xx * 2 + cc, :, pl.ds(*part)], D, sems, 4)
+
+    ag_x.step_one()
+    gain_item = push_y(gainb.at[f], 3)
+    y_w = []
+    waits = ((0,), (1, 2, 3), tuple(range(4, 10)))
+    for n, (first, width) in enumerate(GROUPS):
+        for i in waits[n]:
+            loads[i].wait()
+        y_w.append(push_y(slab_view(first, width, True)(z, x, c, None), n))
+    ag_x.step_two()
+    y_w[0].wait_recv()
+    ag_w[0].step_one()
+    ag_x.step_three()
+    ag_w[0].step_two()
+    ag_x.step_four()
+    y_w[1].wait_recv()
+    ag_w[1].step_one()
+    ag_w[0].step_three()
+    ag_c.step_one()
+    ag_w[1].step_two()
+    gain_item.wait_recv()
+
+    memp[0:own_rows] = mem_ref[...]
+    memp[own_rows:padded] = jnp.zeros((padded - own_rows, D), BF16)
+
+    def example_of(rank):
+        small = jnp.int32(0)
+        large = jnp.int32(0)
+        found = jnp.int32(0)
+        for i in range(ranks):
+            group = res_ref[0, i]
+            where = jnp.where(group == 1, lay.half + large, small)
+            found = jnp.where(where == rank, i, found)
+            large = large + group
+            small = small + (1 - group)
+        return found
+
+    def rank_of_example(example):
+        before_large = jnp.int32(0)
+        mine = jnp.int32(0)
+        for i in range(ranks):
+            group = res_ref[0, i]
+            before_large = before_large + jnp.where(i < example, group, 0)
+            mine = jnp.where(i == example, group, mine)
+        return jnp.where(mine == 1, lay.half + before_large, example - before_large)
+
+    gain = [jnp.concatenate([gainb[i, n : n + 1] for i in range(columns)], axis=1) for n in range(3)]
+
+    mine = example_of(me)
+    resid = xb[mine, 0:SUFFIX]
+    hat_one, rs_one = normed(resid)
+    n1 = (hat_one * gain[0]).astype(BF16)
+
+    ag_w[0].step_four()
+
+    lanes = lax.broadcasted_iota(jnp.int32, (1, 256), 1)
+    head_f32 = [(lax.div(lanes, HEAD_DIM) == h).astype(F32) for h in range(4)]
+    head_b16 = [m.astype(BF16) for m in head_f32]
+
+    def stack(value):
+        return jnp.concatenate([value * m for m in head_b16], axis=0)
+
+    def unstack(value):
+        rows = value.shape[0] // 4
+        total = value[0:rows] * head_f32[0]
+        for h in range(1, 4):
+            total = total + value[h * rows : (h + 1) * rows] * head_f32[h]
+        return total
+
+    q = (mm(n1, wb[:, 0:768])).astype(BF16)
+    k = (mm(n1, wb[:, 768:1536])).astype(BF16)
+    v = (mm(n1, wb[:, 1536:2304])).astype(BF16)
+    scale = HEAD_DIM**-0.5
+    qs = (q.astype(F32) * scale).astype(BF16)
+    row_at = lax.broadcasted_iota(jnp.int32, (SUFFIX, SUFFIX), 0)
+    col_at = lax.broadcasted_iota(jnp.int32, (SUFFIX, SUFFIX), 1)
+    causal = jnp.concatenate([(row_at >= col_at).astype(F32)] * 4, axis=0) > 0.0
+    self_p = []
+    mixed = []
+    for g in range(3):
+        sl = slice(256 * g, 256 * g + 256)
+        s = mm_nt(stack(qs[:, sl]), k[:, sl])
+        s = jnp.where(causal, s, NONE)
+        e = jnp.exp(s - jnp.max(s, axis=-1, keepdims=True))
+        p = e / jnp.sum(e, axis=-1, keepdims=True)
+        self_p.append(p)
+        mixed.append(unstack(mm(p.astype(BF16), v[:, sl])))
+    sm = jnp.concatenate(mixed, axis=1).astype(BF16)
+
+    ag_w[1].step_three()
+    ag_w[1].step_four()
+    y_w[2].wait_recv()
+    ag_w[2].step_one()
+    ag_c.step_two()
+
+    after_self = resid + mm(sm, wb[:, LANE_SO : LANE_SO + 768])
+    hat_two, rs_two = normed(after_self)
+    n2 = (hat_two * gain[1]).astype(BF16)
+    cq = mm(n2, wb[:, LANE_CQ : LANE_CQ + 768]).astype(BF16)
+    cqb[...] = cq
+
+    my_first, my_last = lay.first_device(me), lay.last_device(me)
+    held_first, held_last = lay.first_rank(me), lay.last_rank(me)
+
+    def to_holders(pairs):
+        for i in range(SLOTS):
+            target = my_first + i
+            slot = me - lay.first_rank(target)
+            there = target <= my_last
+
+            @pl.when(there & (target == me))
+            def _():
+                for src, dst, at in pairs:
+                    dst[slot] = src[...]
+
+            @pl.when(there & (target != me))
+            def _():
+                for src, dst, at in pairs:
+                    pltpu.make_async_remote_copy(
+                        src_ref=src, dst_ref=dst.at[slot], send_sem=psend.at[at, i],
+                        recv_sem=precv.at[at, slot], device_id=(target, f), device_id_type=MESH,
+                    ).start()
+
+    def to_holders_sent(pairs):
+        for i in range(SLOTS):
+            target = my_first + i
+
+            @pl.when((target <= my_last) & (target != me))
+            def _():
+                for src, dst, at in pairs:
+                    pltpu.make_async_remote_copy(
+                        src_ref=src, dst_ref=dst.at[0], send_sem=psend.at[at, i],
+                        recv_sem=precv.at[at, 0], device_id=(target, f), device_id_type=MESH,
+                    ).wait_send()
+
+    def at_holders(pairs):
+        for s in range(SLOTS):
+            rank = held_first + s
+
+            @pl.when((rank <= held_last) & (rank != me))
+            def _():
+                for src, dst, at in pairs:
+                    pltpu.make_async_remote_copy(
+                        src_ref=src, dst_ref=dst.at[s], send_sem=psend.at[at, 0],
+                        recv_sem=precv.at[at, s], device_id=(rank, f), device_id_type=MESH,
+                    ).wait_recv()
+
+    def to_owners(pairs):
+        for s in range(SLOTS):
+            rank = held_first + s
+            index = me - lay.first_device(rank)
+            there = rank <= held_last
+
+            @pl.when(there & (rank == me))
+            def _():
+                for src, dst, at in pairs:
+                    dst[index] = src[s]
+
+            @pl.when(there & (rank != me))
+            def _():
+                for src, dst, at in pairs:
+                    pltpu.make_async_remote_copy(
+                        src_ref=src.at[s], dst_ref=dst.at[index], send_sem=psend.at[at, s],
+                        recv_sem=precv.at[at, index], device_id=(rank, f), device_id_type=MESH,
+                    ).start()
+
+    def to_owners_sent(pairs):
+        for s in range(SLOTS):
+            rank = held_first + s
+
+            @pl.when((rank <= held_last) & (rank != me))
+            def _():
+                for src, dst, at in pairs:
+                    pltpu.make_async_remote_copy(
+                        src_ref=src.at[s], dst_ref=dst.at[0], send_sem=psend.at[at, s],
+                        recv_sem=precv.at[at, 0], device_id=(rank, f), device_id_type=MESH,
+                    ).wait_send()
+
+    def at_owners(pairs):
+        for i in range(SLOTS):
+            target = my_first + i
+
+            @pl.when((target <= my_last) & (target != me))
+            def _():
+                for src, dst, at in pairs:
+                    pltpu.make_async_remote_copy(
+                        src_ref=src.at[0], dst_ref=dst.at[i], send_sem=psend.at[at, 0],
+                        recv_sem=precv.at[at, i], device_id=(target, f), device_id_type=MESH,
+                    ).wait_recv()
+
+    q_pairs = [(cqb, qbuf, 0)]
+    o_pairs = [(osend, obuf, 1), (ostat_send, ostat, 2)]
+    d_pairs = [(dob, dobuf, 3), (dstat_b, dstat, 4)]
+    dq_pairs = [(dqsend, dqbuf, 5)]
+
+    to_holders(q_pairs)
+
+    def kv_step(i, carry):
+        lane = pl.multiple_of(i * 256, 256)
+        kvb[:, pl.ds(lane, 256)] = mm(memp[...], wb[:, pl.ds(LANE_CKV + lane, 256)]).astype(BF16)
+        return carry
+
+    lax.fori_loop(0, 6, kv_step, 0)
+
+    lane_f = lax.broadcasted_iota(jnp.int32, (SUFFIX, padded), 1).astype(F32)
+    allowed = []
+    for s in range(SLOTS):
+        rank = held_first + s
+        ok = rank <= held_last
+        example = example_of(jnp.minimum(rank, ranks - 1))
+        prefix = xb[example, SUFFIX : SUFFIX + 8, 0:128][0:1, 0:1]
+        low = (lay.start(rank) - me * own_rows).astype(F32)
+        patches = jnp.where(rank < lay.half, PATCH_S, PATCH_L).astype(F32)
+        high = jnp.minimum(low + patches + prefix, jnp.float32(own_rows))
+        high = jnp.where(ok, high, jnp.float32(-1.0))
+        allowed.append(((lane_f >= low) & (lane_f < high)).astype(F32))
+    allowed = jnp.concatenate(allowed * 4, axis=0) > 0.0
+
+    at_holders(q_pairs)
+    to_holders_sent(q_pairs)
+    qh = jnp.concatenate([qbuf[s] for s in range(SLOTS)], axis=0)
+    qh = (qh.astype(F32) * scale).astype(BF16)
+    lane_c = lax.broadcasted_iota(jnp.int32, (SUFFIX, 128), 1)
+    top_c = [jnp.zeros((SUFFIX, 128), F32) for _ in range(SLOTS)]
+    sum_c = [jnp.zeros((SUFFIX, 128), F32) for _ in range(SLOTS)]
+    for g in range(3):
+        sl = slice(256 * g, 256 * g + 256)
+        s = mm_nt(stack(qh[:, sl]), kvb[:, sl])
+        s = jnp.where(allowed, s, NONE)
+        top = jnp.max(s, axis=-1, keepdims=True)
+        e = jnp.where(allowed, jnp.exp(s - top), 0.0)
+        total = jnp.sum(e, axis=-1, keepdims=True)
+        o = mm(e.astype(BF16), kvb[:, 768 + 256 * g : 1024 + 256 * g])
+        o = o * jnp.where(total > 0.0, 1.0 / jnp.where(total > 0.0, total, 1.0), 0.0)
+        o = unstack(o).astype(BF16)
+        for n in range(SLOTS):
+            osend[n, :, sl] = o[n * SUFFIX : (n + 1) * SUFFIX]
+            for h in range(4):
+                at = h * SLOTS * SUFFIX + n * SUFFIX
+                hit = lane_c == 4 * g + h
+                top_c[n] = jnp.where(hit, top[at : at + SUFFIX], top_c[n])
+                sum_c[n] = jnp.where(hit, total[at : at + SUFFIX], sum_c[n])
+    for n in range(SLOTS):
+        ostat_send[n, 0] = top_c[n]
+        ostat_send[n, 1] = sum_c[n]
+    to_owners(o_pairs)
+
+    ag_w[2].step_two()
+    ag_c.step_three()
+
+    at_owners(o_pairs)
+    to_owners_sent(o_pairs)
+
+    def expand(compact):
+        low = lane_c < HEAD_DIM
+        return jnp.concatenate(
+            [jnp.where(low, compact[:, 2 * t : 2 * t + 1], compact[:, 2 * t + 1 : 2 * t + 2]) for t in range(6)],
+            axis=1,
+        )
+
+    tops = [ostat[i, 0] for i in range(SLOTS)]
+    top_all = jnp.maximum(jnp.maximum(tops[0], tops[1]), tops[2])
+    shares = [ostat[i, 1] * jnp.exp(tops[i] - top_all) for i in range(SLOTS)]
+    whole = shares[0] + shares[1] + shares[2]
+    whole = jnp.where(whole > 0.0, whole, 1.0)
+    lse = top_all + jnp.log(whole)
+    cross = jnp.zeros((SUFFIX, D), F32)
+    for i in range(SLOTS):
+        cross = cross + expand(shares[i] / whole) * obuf[i].astype(F32)
+    cm = cross.astype(BF16)
+
+    ag_c.step_four()
+    ag_w[2].step_three()
+    ag_w[2].step_four()
+
+    after_cross = after_self + mm(cm, wb[:, LANE_CO : LANE_CO + 768])
+    hat_three, rs_three = normed(after_cross)
+    n3 = (hat_three * gain[2]).astype(BF16)
+
+    cot = cb[mine]
+    out_low = cot.astype(BF16)
+    acts, up_grads = [], []
+    hidden_grad = [mm_nt(out_low, wb[:, LANE_FO + 768 * j : LANE_FO + 768 * (j + 1)]) for j in range(4)]
+
+    def by_hidden(j):
+        parts = []
+        for t in range(768 // half_rows):
+            at = 768 * j + t * half_rows
+            col, unit = at // (4 * half_rows), (at % (4 * half_rows)) // half_rows
+            parts.append(hidden_grad[unit][:, col * half_rows : (col + 1) * half_rows])
+        return jnp.concatenate(parts, axis=1)
+
+    n3_grad = jnp.zeros((SUFFIX, D), F32)
+    for j in range(4):
+        weight = wb[:, LANE_FI + 768 * j : LANE_FI + 768 * (j + 1)]
+        value, slope = gelu_parts(mm(n3, weight))
+        acts.append(value.astype(BF16))
+        ug = (by_hidden(j) * slope).astype(BF16)
+        up_grads.append(ug)
+        n3_grad = n3_grad + mm_nt(ug, weight)
+    act = jnp.concatenate(acts, axis=1)
+
+    def act_unit(j):
+        return [act[:, i * 4 * half_rows + j * half_rows : i * 4 * half_rows + (j + 1) * half_rows] for i in range(columns)]
+
+    part, ffn_gain_grad = norm_back(n3_grad, hat_three, rs_three, gain[2])
+    cross_res = cot + part
+    cross_low = cross_res.astype(BF16)
+    d_mixed = mm_nt(cross_low, wb[:, LANE_CO : LANE_CO + 768]).astype(BF16)
+    dob[...] = d_mixed
+    prod = d_mixed.astype(F32) * cross
+    delta = jnp.zeros((SUFFIX, 128), F32)
+    for t in range(6):
+        tile = prod[:, 128 * t : 128 * (t + 1)]
+        left = jnp.sum(jnp.where(lane_c < HEAD_DIM, tile, 0.0), axis=-1, keepdims=True)
+        right = jnp.sum(jnp.where(lane_c < HEAD_DIM, 0.0, tile), axis=-1, keepdims=True)
+        delta = jnp.where(lane_c == 2 * t, left, delta)
+        delta = jnp.where(lane_c == 2 * t + 1, right, delta)
+    dstat_b[0] = lse
+    dstat_b[1] = delta
+    to_holders(d_pairs)
+
+    down = jnp.zeros((SUFFIX, D), F32)
+    for j in range(4):
+        down = down + mm(
+            jnp.concatenate(act_unit(j), axis=1), wb[:, LANE_FO + 768 * j : LANE_FO + 768 * (j + 1)]
+        )
+    ob[me, 0:SUFFIX] = after_cross + down
+
+    def unit_device(u):
+        return 2 * u + 1 if u < 8 else 2 * (u - 8)
+
+    unit_items = []
+
+    def push_unit(u, left_parts, right):
+        to = unit_device(u)
+        for col in range(columns):
+            at = u * columns + col
+            sb[at, :, 0:half_rows] = left_parts[col]
+            sb[at, :, half_rows : half_rows + D] = right
+            self_hit = (me == to) & (f == col)
+            row = pl.multiple_of(lin * SUFFIX, SUFFIX)
+
+            @pl.when(self_hit)
+            def _():
+                rb[pl.ds(row, SUFFIX)] = sb[at]
+
+            @pl.when(jnp.logical_not(self_hit))
+            def _():
+                pltpu.make_async_remote_copy(
+                    src_ref=sb.at[at], dst_ref=rb.at[pl.ds(row, SUFFIX)], send_sem=usend.at[at],
+                    recv_sem=urecv.at[lin], device_id=(to, col), device_id_type=MESH,
+                ).start()
+
+            unit_items.append((at, to, col))
+
+    def halves(value):
+        return [value[:, i * half_rows : (i + 1) * half_rows] for i in range(columns)]
+
+    for j in range(4):
+        push_unit(8 + j, halves(n3), up_grads[j])
+        push_unit(12 + j, act_unit(j), out_low)
+    push_unit(7, halves(cm), cross_low)
+
+    at_holders(d_pairs)
+    to_holders_sent(d_pairs)
+
+    doh = jnp.concatenate([dobuf[s] for s in range(SLOTS)], axis=0)
+    for g in range(3):
+        sl = slice(256 * g, 256 * g + 256)
+        kg = kvb[:, sl]
+        vg = kvb[:, 768 + 256 * g : 1024 + 256 * g]
+        q4 = stack(qh[:, sl])
+        do4 = stack(doh[:, sl])
+        lse_col = jnp.concatenate([dstat[n, 0][:, 4 * g + h : 4 * g + h + 1] for h in range(4) for n in range(SLOTS)], axis=0)
+        del_col = jnp.concatenate([dstat[n, 1][:, 4 * g + h : 4 * g + h + 1] for h in range(4) for n in range(SLOTS)], axis=0)
+        s = mm_nt(q4, kg)
+        p = jnp.where(allowed, jnp.exp(jnp.where(allowed, s - lse_col, 0.0)), 0.0)
+        dp = mm_nt(do4, vg)
+        ds = (p * (dp - del_col)).astype(BF16)
+        kvg[:, 768 + 256 * g : 1024 + 256 * g] = mm_tn(p.astype(BF16), do4).astype(BF16)
+        kvg[:, sl] = mm_tn(ds, q4).astype(BF16)
+        dq = unstack(mm(ds, kg)) * scale
+        for n in range(SLOTS):
+            dqsend[n, :, sl] = dq[n * SUFFIX : (n + 1) * SUFFIX]
+    to_owners(dq_pairs)
+
+    def kp_step(i, carry):
+        lane = pl.multiple_of(i * 256, 256)
+        kp[:, pl.ds(lane, 256)] = mm_tn(memp[...], kvg[:, pl.ds(lane, 256)]).astype(BF16)
+        return carry
+
+    lax.fori_loop(0, 6, kp_step, 0)
+    mate = (z * 4 + x * 2 + (1 - c), f)
+    kr_item = pltpu.make_async_remote_copy(
+        src_ref=kp.at[pl.ds(pl.multiple_of((1 - c) * half_rows, 128), half_rows)], dst_ref=kr,
+        send_sem=ksend.at[2 * chips], recv_sem=krecv.at[2 * chips], device_id=mate, device_id_type=MESH,
+    )
+    kr_item.start()
+
+    at_owners(dq_pairs)
+    to_owners_sent(dq_pairs)
+    cqg = (dqbuf[0] + dqbuf[1] + dqbuf[2]).astype(BF16)
+    n2_grad = mm_nt(cqg, wb[:, LANE_CQ : LANE_CQ + 768])
+    part, cross_gain_grad = norm_back(n2_grad, hat_two, rs_two, gain[1])
+    self_res = cross_res + part
+    self_low = self_res.astype(BF16)
+    push_unit(4, halves(n2), cqg)
+    push_unit(3, halves(sm), self_low)
+    dmix = mm_nt(self_low, wb[:, LANE_SO : LANE_SO + 768]).astype(BF16)
+    dqs, dks, dvs = [], [], []
+    for g in range(3):
+        sl = slice(256 * g, 256 * g + 256)
+        q4 = stack(qs[:, sl])
+        do4 = stack(dmix[:, sl])
+        p = self_p[g]
+        dp = mm_nt(do4, v[:, sl])
+        ds = (p * (dp - jnp.sum(p * dp, axis=-1, keepdims=True))).astype(BF16)
+        dvs.append(mm_tn(p.astype(BF16), do4))
+        dks.append(mm_tn(ds, q4))
+        dqs.append(unstack(mm(ds, k[:, sl])) * scale)
+    packed_grad = [jnp.concatenate(parts, axis=1).astype(BF16) for parts in (dqs, dks, dvs)]
+    n1_grad = jnp.zeros((SUFFIX, D), F32)
+    for j in range(3):
+        push_unit(j, halves(n1), packed_grad[j])
+    for j in range(3):
+        n1_grad = n1_grad + mm_nt(packed_grad[j], wb[:, 768 * j : 768 * (j + 1)])
+    part, self_gain_grad = norm_back(n1_grad, hat_one, rs_one, gain[0])
+    ob[me, SUFFIX : 2 * SUFFIX] = self_res + part
+    gmine[...] = jnp.concatenate(
+        [self_gain_grad, cross_gain_grad, ffn_gain_grad, jnp.zeros((5, D), F32)], axis=0
+    )
+    g_item = pltpu.make_async_remote_copy(
+        src_ref=gmine, dst_ref=gpeer, send_sem=ysend.at[4], recv_sem=yrecv.at[4],
+        device_id=(me, other), device_id_type=MESH,
+    )
+    g_item.start()
+
+    kr_item.wait_recv()
+    kc[...] = (
+        kp[pl.ds(pl.multiple_of(c * half_rows, 128), half_rows)].astype(F32) + kr[...].astype(F32)
+    ).astype(BF16)
+    k_items = []
+    for t in range(chips):
+        for j in range(CORES):
+            at = t * CORES + j
+            self_hit = (f == c) & (chip == t) & (c == j)
+            src = kc.at[pl.ds(t * slab, slab), pl.ds(j * D, D)]
+            slot = f * chips + chip
+
+            @pl.when(self_hit)
+            def _():
+                cp[slot] = kc[pl.ds(t * slab, slab), pl.ds(j * D, D)]
+
+            @pl.when(jnp.logical_not(self_hit))
+            def _():
+                pltpu.make_async_remote_copy(
+                    src_ref=src, dst_ref=cp.at[slot], send_sem=ksend.at[at], recv_sem=krecv.at[slot],
+                    device_id=(t * CORES + j, c), device_id_type=MESH,
+                ).start()
+
+            k_items.append((at, src, self_hit))
+
+    g_item.wait_recv()
+    ob[me, 2 * SUFFIX : 2 * SUFFIX + 8] = gmine[...] + gpeer[...]
+    ag_o = Gather(place, lambda zz, xx, cc, part: ob.at[zz * 4 + xx * 2 + cc] if part is None else ob.at[zz * 4 + xx * 2 + cc, :, pl.ds(*part)], D, sems, 5)
+    ag_o.step_one()
+
+    unit = jnp.where(c == 1, chip, chip + 8)
+    has_unit = (unit != KV_UNITS[0]) & (unit != KV_UNITS[1])
+
+    def unit_lane(zz, xx, cc):
+        n = zz * SIDE + xx
+        u = jnp.where(cc == 1, n, n + 8)
+        spare = (u == KV_UNITS[0]) | (u == KV_UNITS[1])
+        return jnp.where(spare, UNITS + u - KV_UNITS[0], u) * D
+
+    @pl.when(has_unit)
+    def _():
+        def take(i, carry):
+            @pl.when(i != lin)
+            def _():
+                pltpu.make_async_remote_copy(
+                    src_ref=sb.at[0], dst_ref=rb.at[pl.ds(pl.multiple_of(i * SUFFIX, SUFFIX), SUFFIX)],
+                    send_sem=usend.at[0], recv_sem=urecv.at[i], device_id=mate, device_id_type=MESH,
+                ).wait_recv()
+            return carry
+
+        lax.fori_loop(0, everyone, take, 0)
+
+        def sum_step(i, carry):
+            lane = pl.multiple_of(i * 256, 256)
+            total = mm_tn(rb[:, 0:half_rows], rb[:, pl.ds(half_rows + lane, 256)])
+            gb[:, pl.ds(pl.multiple_of(unit_lane(z, x, c) + lane, 256), 256)] = total.astype(BF16)
+            return carry
+
+        lax.fori_loop(0, 3, sum_step, 0)
+
+    @pl.when(jnp.logical_not(has_unit))
+    def _():
+        gb[:, pl.ds(pl.multiple_of(unit_lane(z, x, c), 256), D)] = jnp.zeros((half_rows, D), BF16)
+
+    def unit_view(zz, xx, cc, part):
+        low, size = part if part is not None else (0, D)
+        return gb.at[:, pl.ds(pl.multiple_of(unit_lane(zz, xx, cc) + low, 128), size)]
+
+    ag_g = Gather(place, unit_view, D, sems, 6)
+    ag_g.step_one()
+
+    def take_k(i, carry):
+        @pl.when((i != f * chips + chip) | (c != f))
+        def _():
+            pltpu.make_async_remote_copy(
+                src_ref=kc.at[pl.ds(0, slab), pl.ds(0, D)], dst_ref=cp.at[i], send_sem=ksend.at[0],
+                recv_sem=krecv.at[i], device_id=mate, device_id_type=MESH,
+            ).wait_recv()
+        return carry
+
+    lax.fori_loop(0, 2 * chips, take_k, 0)
+    total = cp[0].astype(F32)
+    for i in range(1, 2 * chips):
+        total = total + cp[i].astype(F32)
+    k_lane = pl.multiple_of(LANE_CKV + c * D, 128)
+    gb[pl.ds(pl.multiple_of(chip * slab, 16), slab), pl.ds(k_lane, D)] = total.astype(BF16)
+
+    def kv_view(zz, xx, cc, part):
+        low, size = part if part is not None else (0, D)
+        row = pl.multiple_of((zz * SIDE + xx) * slab, 16)
+        return gb.at[pl.ds(row, slab), pl.ds(pl.multiple_of(LANE_CKV + cc * D + low, 128), size)]
+
+    ag_k = Gather(place, kv_view, D, sems, 7)
+    ag_k.step_one()
+    ag_o.step_two()
+    ag_k.step_two()
+    ag_o.step_three()
+    ag_k.step_three()
+    ag_o.step_four()
+    ag_k.step_four()
+    ag_g.step_two()
+
+    def mg_step(i, carry):
+        row = pl.multiple_of(i * 128, 128)
+        memgrad_ref[pl.ds(row, 128)] = mm_nt(kvg[pl.ds(row, 128)], wb[:, LANE_CKV : LANE_CKV + 2 * D])
+        return carry
+
+    full = own_rows // 128
+    lax.fori_loop(0, full, mg_step, 0)
+    if own_rows % 128:
+        tail = mm_nt(kvg[full * 128 : (full + 1) * 128], wb[:, LANE_CKV : LANE_CKV + 2 * D])
+        memgrad_ref[full * 128 : own_rows] = tail[0 : own_rows - full * 128]
+
+    mine_rank = rank_of_example(me)
+    out_ref[...] = ob[mine_rank, 0:SUFFIX]
+    grad_ref[...] = ob[mine_rank, SUFFIX : 2 * SUFFIX]
+    gains_all = ob[0, 2 * SUFFIX : 2 * SUFFIX + 8]
+    for i in range(1, ranks):
+        gains_all = gains_all + ob[i, 2 * SUFFIX : 2 * SUFFIX + 8]
+    own_gain = gains_all[:, 0:half_rows]
+    for i in range(1, columns):
+        own_gain = jnp.where(f == i, gains_all[:, i * half_rows : (i + 1) * half_rows], own_gain)
+    gain_out_ref[...] = own_gain
+
+    ag_g.step_three()
+    ag_g.step_four()
+    done = pltpu.make_async_copy(gb.at[:, pl.ds(0, UNITS * D)], weights_out_ref, load_sem.at[0])
+    done.start()
+
+    for at, to, col in unit_items:
+        @pl.when(jnp.logical_not((me == to) & (f == col)))
+        def _():
+            pltpu.make_async_remote_copy(
+                src_ref=sb.at[at], dst_ref=rb.at[pl.ds(0, SUFFIX)], send_sem=usend.at[at],
+                recv_sem=urecv.at[0], device_id=(to, col), device_id_type=MESH,
+            ).wait_send()
+    for at, src, self_hit in k_items:
+        @pl.when(jnp.logical_not(self_hit))
+        def _():
+            pltpu.make_async_remote_copy(
+                src_ref=src, dst_ref=cp.at[0], send_sem=ksend.at[at], recv_sem=krecv.at[0],
+                device_id=mate, device_id_type=MESH,
+            ).wait_send()
+    kr_item.wait_send()
+    for item in y_items + [g_item]:
+        item.wait_send()
+    for item in [ag_x, *ag_w, ag_c, ag_o, ag_g, ag_k]:
+        item.finish()
+    done.wait()
+
+
+def fused_body(
+    ranks, columns,
+    decoder_in, memory, res_group, prefix_len, self_gain, self_qkv, self_out, cross_gain, cross_query,
+    cross_kv, cross_out, ffn_gain, ffn_in, ffn_out, cotangent,
+):
+    half_rows = D // columns
+    chips = ranks // CORES
+    slab = half_rows // chips
+    own_rows = memory.shape[1]
+    padded = -(-own_rows // 128) * 128
+    everyone = ranks * columns
+    gains = jnp.stack([self_gain, cross_gain, ffn_gain]).astype(F32)
+    gains = jnp.pad(gains, ((0, 5), (0, 0)))
+    vm = pl.BlockSpec(memory_space=pltpu.VMEM)
+    sm = pl.BlockSpec(memory_space=pltpu.SMEM)
+    hbm = pl.BlockSpec(memory_space=pl.ANY)
+    dma = pltpu.SemaphoreType.DMA
+    scratch = [
+        pltpu.VMEM((D, UNITS * D), BF16),
+        pltpu.VMEM((half_rows, (UNITS + 2) * D), BF16),
+        pltpu.VMEM((everyone * SUFFIX, half_rows + D), BF16),
+        pltpu.VMEM((UNITS * columns, SUFFIX, half_rows + D), BF16),
+        pltpu.VMEM((ranks, SUFFIX + 8, D), F32),
+        pltpu.VMEM((ranks, SUFFIX, D), F32),
+        pltpu.VMEM((ranks, 2 * SUFFIX + 8, D), F32),
+        pltpu.VMEM((columns, 8, half_rows), F32),
+        pltpu.VMEM((padded, D), BF16),
+        pltpu.VMEM((padded, 2 * D), BF16),
+        pltpu.VMEM((padded, 2 * D), BF16),
+        pltpu.VMEM((D, 2 * D), BF16),
+        pltpu.VMEM((half_rows, 2 * D), BF16),
+        pltpu.VMEM((half_rows, 2 * D), BF16),
+        pltpu.VMEM((columns * chips, slab, D), BF16),
+        pltpu.VMEM((SUFFIX, D), BF16),
+        pltpu.VMEM((SLOTS, SUFFIX, D), BF16),
+        pltpu.VMEM((SLOTS, SUFFIX, D), BF16),
+        pltpu.VMEM((SLOTS, 2, SUFFIX, 128), F32),
+        pltpu.VMEM((SLOTS, SUFFIX, D), BF16),
+        pltpu.VMEM((SLOTS, 2, SUFFIX, 128), F32),
+        pltpu.VMEM((SUFFIX, D), BF16),
+        pltpu.VMEM((2, SUFFIX, 128), F32),
+        pltpu.VMEM((SLOTS, SUFFIX, D), BF16),
+        pltpu.VMEM((SLOTS, 2, SUFFIX, 128), F32),
+        pltpu.VMEM((SLOTS, SUFFIX, D), F32),
+        pltpu.VMEM((SLOTS, SUFFIX, D), F32),
+        pltpu.VMEM((8, D), F32),
+        pltpu.VMEM((8, D), F32),
+        dma((10,)),
+        dma((8, 16)),
+        dma((8, 16)),
+        dma((5,)),
+        dma((5,)),
+        dma((6, SLOTS)),
+        dma((6, SLOTS)),
+        dma((UNITS * columns,)),
+        dma((everyone,)),
+        dma((2 * chips + 1,)),
+        dma((2 * chips + 1,)),
+    ]
+    out, grad, memgrad, gain_grads, weight_grads = pl.pallas_call(
+        partial(layer_kernel, ranks, columns),
+        out_shape=(
+            jax.ShapeDtypeStruct((SUFFIX, D), F32),
+            jax.ShapeDtypeStruct((SUFFIX, D), F32),
+            jax.ShapeDtypeStruct((own_rows, D), F32),
+            jax.ShapeDtypeStruct((8, half_rows), F32),
+            jax.ShapeDtypeStruct((half_rows, UNITS * D), BF16),
+        ),
+        in_specs=[vm, vm, vm, sm, sm, vm] + [hbm] * 7,
+        out_specs=(vm, vm, vm, vm, hbm),
+        scratch_shapes=scratch,
+        compiler_params=pltpu.CompilerParams(
+            collective_id=0, has_side_effects=True, vmem_limit_bytes=62 * 2**20
+        ),
+        name="layer",
+    )(
+        decoder_in[0], cotangent[0], memory[0], res_group, prefix_len, gains,
+        self_qkv, self_out, cross_query, cross_kv, cross_out, ffn_in, ffn_out,
+    )
+
+    def lanes(low, width):
+        return weight_grads[:, low : low + width].astype(F32)
+
+    ffn_out_grad = jnp.concatenate([lanes(LANE_FO + D * j, D) for j in range(4)], axis=0)
+    return (
+        out[None], grad[None], memgrad[None],
+        gain_grads[0], lanes(LANE_QKV, 3 * D), lanes(LANE_SO, D),
+        gain_grads[1], lanes(LANE_CQ, D), lanes(LANE_CKV, 2 * D), lanes(LANE_CO, D),
+        gain_grads[2], lanes(LANE_FI, 4 * D), ffn_out_grad,
+    )
 
 
 def layer_norm(value, gain):
@@ -412,6 +1383,14 @@
     )
 
 
+def choose(mesh):
+    ranks, columns = mesh.shape["dp"], mesh.shape["fsdp"]
+    slabs = (D // columns) % (16 * (ranks // CORES)) == 0
+    if slabs and columns == 2 and ranks == RING * SIDE * CORES:
+        return partial(fused_body, ranks, columns)
+    return body
+
+
 def solution(mesh):
     placed = (
         P("fsdp", "dp", None),
@@ -431,7 +1410,7 @@
         P("fsdp", "dp", None),
     )
     return jax.shard_map(
-        body,
+        choose(mesh),
         mesh=mesh,
         in_specs=placed,
         out_specs=(

time: 1350 us -> 382 us (0.28)
  the two profiles are of different devices: /device:TPU:3 before, /device:TPU:21 now
where the time goes in v1:
time: 382 us; the launch traced here: 381 us
  Pallas kernels  357 us (93%)
  other arithmetic  14.2 us (4%)
  local copies, waits for them, and re-layouts  8.59 us (2%)
    pallas_call x1, Pallas kernels, fused_body(): pl.pallas_call(partial(layer_kernel, ranks, columns), out_shape=(jax.Shap...  357 us
    convert_element_type x3, other arithmetic, lanes(): return weight_grads[:, low:low + width].astype(F32)  9.22 us

profile of v1, /device:TPU:21, one launch (start us, length us, event | category | flops | bytes accessed | tf_op | source)
XLA Modules:
  0.0 381.5 jit_solution(9010199522715647265)
XLA Ops:
  1.3 0.7 stack.12
  2.0 0.7 stack.13
  2.7 0.7 stack.14
  3.3 0.6 fusion.5.gains_ref
  3.9 357.3 %layer.1 = (f32[32,768]{1,0:T(8,128)}, f32[32,768]{1,0:T(8,128)}, f32[418,768]{1,0:T(8,128)}, f32[8,384]{1,0:T(8,128)}, bf16[384,12288]{1,0:T(8,128)(2,1)}) custom-call(f32[32,768]{1,0:T(8,128)} %bitcast.8, f32[32,768]{1,0:T(8,128)} %bitcast.9, bf16[418,768]{1,0:T(8,128)(2,1)} %bitcast.7, s32[1,16]{1,0:T(1,128)} %res_ref.1, s32[1,1]{1,0:T(1,128)S(6)} %copy.31.pre_ref, ...), custom_call_target="tpu_custom_call" | custom-call | tf_op jit(solution)/shard_map/layer/pallas_call | solution.py:959
  361.3 1.4 slice_reduce_fusion
  362.7 0.0 copy-start
  362.7 3.8 %copy.28 = f32[1,418,768]{2,0,1:T(1,128)} copy(f32[1,418,768]{2,1,0:T(8,128)} %bitcast.6) | data formatting | bytes 2568192
  366.6 3.0 slice_convert_fusion.2
  369.5 3.5 slice_convert_fusion.1
  373.0 0.0 copy-done
  373.0 2.8 slice_convert_fusion
  375.8 1.9 fusion.6
  377.7 0.0 copy-start.2
  377.7 0.0 copy-start.1
  377.7 2.5 maximum_convert_fusion
  380.2 0.0 copy-done.2
  380.2 0.6 copy.32
  380.8 0.0 copy-done.1
  380.9 0.6 copy.33
Async XLA Ops:
  362.7 10.3 %copy-start = (bf16[384,12288]{1,0:T(8,128)(2,1)S(1)}, bf16[384,12288]{1,0:T(8,128)(2,1)}, u32[]{:S(2)}) copy-start(bf16[384,12288]{1,0:T(8,128)(2,1)} %get-tuple-element.22) | copy-start | bytes 28311556
  377.7 2.6 copy-start.2
  377.7 3.2 copy-start.1

commit v2 on v1

--- a/solution.py
+++ b/solution.py
@@ -62,104 +62,156 @@
     return value, grad
 
 
-class Gather:
-    def __init__(self, place, view, width, sems, at):
+class Relay:
+    def __init__(self, place, view, sems, at, has=None):
         self.z, self.x, self.c, self.f = place
         self.view = view
-        half = (width // 256) * 128
-        self.halves = ((0, half), (half, width - half))
         self.send, self.recv = sems
         self.at = at
+        self.has = has
         self.sent = []
-
-    def dev(self, z, x, c):
-        return (z * (SIDE * CORES) + x * CORES + c, self.f)
-
-    def copy(self, block, half, target, into):
-        z, x, c = block
-        ref = self.view(z, x, c, self.halves[half] if half is not None else None)
+        self.own = (self.z, self.x, self.c)
+        self.side = (self.z, 1 - self.x, self.c)
+        self.up = (lax.rem(self.z + 1, RING), self.x, self.c)
+        self.down = (lax.rem(self.z + 3, RING), self.x, self.c)
+        self.far = (lax.rem(self.z + 2, RING), self.x, self.c)
+        self.up_side = (self.up[0], 1 - self.x, self.c)
+        self.down_side = (self.down[0], 1 - self.x, self.c)
+        self.far_side = (self.far[0], 1 - self.x, self.c)
+        self.mate = (self.z, self.x, 1 - self.c)
+
+    def when(self, block, act):
+        if self.has is None:
+            act()
+        else:
+            pl.when(self.has(*block))(act)
+
+    def copy(self, block, part, target, into, index):
+        ref = self.view(*block, part)
+        z, x, c = target
         return pltpu.make_async_remote_copy(
             src_ref=ref,
             dst_ref=ref,
-            send_sem=self.send.at[self.at, len(self.sent)],
+            send_sem=self.send.at[self.at, index],
             recv_sem=self.recv.at[self.at, into],
-            device_id=self.dev(*target),
+            device_id=(z * (SIDE * CORES) + x * CORES + c, self.f),
             device_id_type=MESH,
         )
 
-    def go(self, block, half, target, into):
-        item = self.copy(block, half, target, into)
-        item.start()
-        self.sent.append(item)
-
-    def wait(self, block, half, into):
-        z, x, c = block
-        ref = self.view(z, x, c, self.halves[half] if half is not None else None)
-        pltpu.make_async_remote_copy(
-            src_ref=ref,
-            dst_ref=ref,
-            send_sem=self.send.at[self.at, 0],
-            recv_sem=self.recv.at[self.at, into],
-            device_id=self.dev(self.z, 1 - self.x, self.c),
-            device_id_type=MESH,
-        ).wait_recv()
-
-    def names(self):
-        z, x, c = self.z, self.x, self.c
-        up, down, far = lax.rem(z + 1, RING), lax.rem(z + 3, RING), lax.rem(z + 2, RING)
-        return z, x, c, up, down, far
+    def go(self, block, target, into, part=None):
+        item = self.copy(block, part, target, into, len(self.sent))
+        self.when(block, item.start)
+        self.sent.append((block, item))
+
+    def wait(self, block, into, part=None):
+        self.when(block, self.copy(block, part, self.side, into, 0).wait_recv)
+
+    def finish(self):
+        for block, item in self.sent:
+            self.when(block, item.wait_send)
+
+
+class Gather(Relay):
+    def __init__(self, place, view, width, sems, at, has=None):
+        super().__init__(place, view, sems, at, has)
+        half = (width // 256) * 128
+        self.parts = ((0, half), (half, width - half))
 
     def step_one(self):
-        z, x, c, up, down, far = self.names()
-        own = (z, x, c)
-        self.go(own, None, (z, 1 - x, c), 0)
-        self.go(own, None, (up, x, c), 1)
-        self.go(own, None, (down, x, c), 2)
-        self.go(own, None, (z, x, 1 - c), 8)
+        self.go(self.own, self.up, 1)
+        self.go(self.own, self.down, 2)
+        self.go(self.own, self.side, 0)
+        self.go(self.own, self.mate, 8)
 
     def step_two(self):
-        z, x, c, up, down, far = self.names()
-        mate = (z, x, 1 - c)
-        self.wait((z, 1 - x, c), None, 0)
-        self.go((z, 1 - x, c), None, (up, x, c), 5)
-        self.go((z, 1 - x, c), None, (down, x, c), 6)
-        self.go((z, 1 - x, c), None, mate, 9)
-        self.wait((down, x, c), None, 1)
-        self.go((down, x, c), 0, (up, x, c), 3)
-        self.go((down, x, c), None, mate, 10)
-        self.wait((up, x, c), None, 2)
-        self.go((up, x, c), 1, (down, x, c), 4)
-        self.go((up, x, c), None, mate, 11)
+        low, high = self.parts
+        self.wait(self.down, 1)
+        self.go(self.down, self.up, 3, low)
+        self.wait(self.up, 2)
+        self.go(self.up, self.down, 4, high)
+        self.wait(self.side, 0)
+        self.go(self.side, self.up, 5)
+        self.go(self.side, self.down, 6)
+        self.go(self.down, self.mate, 10)
+        self.go(self.up, self.mate, 11)
+        self.go(self.side, self.mate, 9)
 
     def step_three(self):
-        z, x, c, up, down, far = self.names()
-        mate = (z, x, 1 - c)
-        self.wait((far, x, c), 0, 3)
-        self.wait((far, x, c), 1, 4)
-        self.go((far, x, c), None, (z, 1 - x, c), 7)
-        self.go((far, x, c), None, mate, 12)
-        self.wait((down, 1 - x, c), None, 5)
-        self.go((down, 1 - x, c), None, mate, 13)
-        self.wait((up, 1 - x, c), None, 6)
-        self.go((up, 1 - x, c), None, mate, 14)
+        low, high = self.parts
+        self.wait(self.far, 3, low)
+        self.wait(self.far, 4, high)
+        self.go(self.far, self.side, 7)
+        self.go(self.far, self.mate, 12)
+        self.wait(self.down_side, 5)
+        self.go(self.down_side, self.mate, 13)
+        self.wait(self.up_side, 6)
+        self.go(self.up_side, self.mate, 14)
 
     def step_four(self):
-        z, x, c, up, down, far = self.names()
-        mate = (z, x, 1 - c)
-        self.wait((far, 1 - x, c), None, 7)
-        self.go((far, 1 - x, c), None, mate, 15)
-        o = 1 - c
-        self.wait((z, x, o), None, 8)
-        self.wait((z, 1 - x, o), None, 9)
-        self.wait((down, x, o), None, 10)
-        self.wait((up, x, o), None, 11)
-        self.wait((far, x, o), None, 12)
-        self.wait((down, 1 - x, o), None, 13)
-        self.wait((up, 1 - x, o), None, 14)
-        self.wait((far, 1 - x, o), None, 15)
+        self.wait(self.far_side, 7)
+        self.go(self.far_side, self.mate, 15)
+
+    def step_five(self):
+        z, x, c = self.mate
+        order = (self.own, self.side, self.down, self.up, self.far, self.down_side, self.up_side, self.far_side)
+        for n, block in enumerate(order):
+            self.wait((block[0], block[1], c), 8 + n)
+
+
+class Spread(Relay):
+    def __init__(self, place, theirs, mine, sems, at):
+        super().__init__(place, theirs, sems, at)
+        self.mine = mine
+        self.columns_item = []
+
+    def push(self):
+        z, x, c = self.own
+        for n, block in enumerate((self.own, self.far)):
+            ref = self.mine(*block, None)
+            item = pltpu.make_async_remote_copy(
+                src_ref=ref, dst_ref=ref, send_sem=self.send.at[self.at, 14 + n], recv_sem=self.recv.at[self.at, 14 + n],
+                device_id=(z * (SIDE * CORES) + x * CORES + c, 1 - self.f), device_id_type=MESH,
+            )
+            item.start()
+            self.columns_item.append(item)
+
+    def step_one(self):
+        self.wait(self.own, 14)
+        self.go(self.own, self.side, 0)
+        self.go(self.own, self.up, 1)
+        self.go(self.own, self.down, 2)
+        self.go(self.own, self.mate, 6)
+        self.wait(self.far, 15)
+        self.go(self.far, self.side, 3)
+        self.go(self.far, self.mate, 7)
+
+    def step_two(self):
+        self.wait(self.side, 0)
+        self.go(self.side, self.up, 4)
+        self.go(self.side, self.down, 5)
+        self.go(self.side, self.mate, 8)
+        self.wait(self.down, 1)
+        self.go(self.down, self.mate, 9)
+        self.wait(self.up, 2)
+        self.go(self.up, self.mate, 10)
+
+    def step_three(self):
+        self.wait(self.far_side, 3)
+        self.go(self.far_side, self.mate, 11)
+        self.wait(self.down_side, 4)
+        self.go(self.down_side, self.mate, 12)
+        self.wait(self.up_side, 5)
+        self.go(self.up_side, self.mate, 13)
+
+    def step_four(self):
+        c = self.mate[2]
+        order = (self.own, self.far, self.side, self.down, self.up, self.far_side, self.down_side, self.up_side)
+        for n, block in enumerate(order):
+            self.wait((block[0], block[1], c), 6 + n)
 
     def finish(self):
-        for item in self.sent:
+        super().finish()
+        for item in self.columns_item:
             item.wait_send()
 
 
@@ -199,11 +251,12 @@
 
 
 SLOTS = 3
+UNITS = 16
 LANE_QKV, LANE_SO, LANE_CQ, LANE_CKV, LANE_CO, LANE_FI, LANE_FO = 0, 2304, 3072, 3840, 5376, 6144, 9216
-UNITS = 16
-KV_UNITS = (5, 6)
-TOKEN_UNITS = tuple(u for u in range(UNITS) if u not in KV_UNITS)
-GROUPS = ((0, 2304), (2304, 3072), (5376, 6912))
+CHUNKS = ((0, 2304), (2304, 1536), (3840, 1536), (5376, 2304), (7680, 2304), (9984, 2304))
+LOADS_BY_CHUNK = ((0,), (1, 2), (3,), (4, 5), (6,), (7, 8, 9))
+PIECE = 384
+HALF_UNITS = 6
 
 
 def layer_kernel(
@@ -212,9 +265,10 @@
     x_ref, cot_ref, mem_ref, res_ref, pre_ref, gains_ref,
     qkv_ref, so_ref, cq_ref, ckv_ref, co_ref, fi_ref, fo_ref,
     out_ref, grad_ref, memgrad_ref, gain_out_ref, weights_out_ref,
-    wb, gb, rb, sb, xb, cb, ob, gainb, memp, kvb, kvg, kp, kr, kc, cp,
+    wb, gb, rb, sb, xb, cb, nb, olr, ob, tb, pb, gainb, memp, kvb, kvg, kp, kr, kc, ky, cp,
+    hb, fg, fsend, frecv, ug, usend_b, urecv_b,
     cqb, qbuf, osend, ostat_send, obuf, ostat, dob, dstat_b, dobuf, dstat, dqsend, dqbuf, gmine, gpeer,
-    load_sem, gsend, grecv, ysend, yrecv, psend, precv, usend, urecv, ksend, krecv,
+    load_sem, wsend, wrecv, gsend, grecv, bsend, brecv, ysend, yrecv, psend, precv, usend, urecv, ksend, krecv,
 ):
     me = lax.axis_index("dp")
     f = lax.axis_index("fsdp")
@@ -243,14 +297,14 @@
         item.start()
         loads.append(item)
 
-    load(qkv_ref, LANE_QKV, 2304)
-    load(so_ref, LANE_SO, 768)
-    load(cq_ref, LANE_CQ, 768)
-    load(ckv_ref, LANE_CKV, 1536)
-    load(co_ref, LANE_CO, 768)
-    load(fi_ref, LANE_FI, 3072)
+    load(qkv_ref, LANE_QKV, 3 * D)
+    load(so_ref, LANE_SO, D)
+    load(cq_ref, LANE_CQ, D)
+    load(ckv_ref, LANE_CKV, 2 * D)
+    load(co_ref, LANE_CO, D)
+    load(fi_ref, LANE_FI, 4 * D)
     for j in range(4):
-        load(fo_ref.at[pl.ds(j * half_rows, half_rows)], LANE_FO + 768 * j, 768)
+        load(fo_ref.at[pl.ds(j * half_rows, half_rows)], LANE_FO + D * j, D)
 
     for s in range(SLOTS):
         qbuf[s] = jnp.zeros_like(qbuf[s])
@@ -261,107 +315,152 @@
         dstat[s] = jnp.zeros_like(dstat[s])
         dqbuf[s] = jnp.zeros_like(dqbuf[s])
 
-    xb[me, 0:SUFFIX] = x_ref[...]
-    xb[me, SUFFIX : SUFFIX + 8] = jnp.full((8, D), pre_ref[0, 0].astype(F32), F32)
-    cb[me] = cot_ref[...]
+    def rows_of(device):
+        return pl.ds(pl.multiple_of(device * SUFFIX, SUFFIX), SUFFIX)
+
+    xb[me] = x_ref[...]
+    cb[me] = cot_ref[...].astype(BF16)
+    pb[me] = jnp.full((8, 128), pre_ref[0, 0].astype(F32), F32)
     gainb[f] = gains_ref[...]
 
     barrier = pltpu.get_barrier_semaphore()
 
     def greet(i, carry):
-        to = lax.rem(lin + i, everyone)
-        pl.semaphore_signal(
-            barrier, inc=1, device_id=(lax.rem(to, ranks), lax.div(to, ranks)), device_id_type=MESH
-        )
+        to = lax.rem(me + i, ranks)
+        pl.semaphore_signal(barrier, inc=1, device_id=(to, f), device_id_type=MESH)
         return carry
 
-    lax.fori_loop(1, everyone, greet, 0)
-    pl.semaphore_wait(barrier, everyone - 1)
+    lax.fori_loop(1, ranks, greet, 0)
+    pl.semaphore_signal(barrier, inc=1, device_id=(me, other), device_id_type=MESH)
+    pl.semaphore_wait(barrier, ranks)
 
     y_items = []
 
-    def push_y(ref, at):
+    def push_y(src, dst, at):
         item = pltpu.make_async_remote_copy(
-            src_ref=ref, dst_ref=ref, send_sem=ysend.at[at], recv_sem=yrecv.at[at],
+            src_ref=src, dst_ref=dst, send_sem=ysend.at[at], recv_sem=yrecv.at[at],
             device_id=(me, other), device_id_type=MESH,
         )
         item.start()
         y_items.append(item)
         return item
 
-    def slab_view(first, width, mine):
+    class Tell:
+        def __init__(self, ref, at):
+            self.ref, self.at = ref, at
+
+        def copy(self, source, index, to):
+            return pltpu.make_async_remote_copy(
+                src_ref=self.ref.at[source], dst_ref=self.ref.at[source], send_sem=bsend.at[self.at, index],
+                recv_sem=brecv.at[self.at, source], device_id=(to, f), device_id_type=MESH,
+            )
+
+        def start(self):
+            def one(i, carry):
+                self.copy(me, i, lax.rem(me + i, ranks)).start()
+                return carry
+
+            lax.fori_loop(1, ranks, one, 0)
+
+        def wait(self):
+            def one(i, carry):
+                source = lax.rem(me + i, ranks)
+                self.copy(source, i, source).wait_recv()
+                return carry
+
+            lax.fori_loop(1, ranks, one, 0)
+
+        def finish(self):
+            def one(i, carry):
+                self.copy(me, i, lax.rem(me + i, ranks)).wait_send()
+                return carry
+
+            lax.fori_loop(1, ranks, one, 0)
+
+    def slab_view(first, width, rows_from):
         half = width // CORES
-        rows_from = f if mine else other
 
         def view(zz, xx, cc, part):
-            low, size = part if part is not None else (0, half)
             row = pl.multiple_of(rows_from * half_rows + (zz * SIDE + xx) * slab, 16)
-            lane = pl.multiple_of(first + cc * half + low, 128)
-            return wb.at[pl.ds(row, slab), pl.ds(lane, size)]
+            lane = pl.multiple_of(first + cc * half, 128)
+            return wb.at[pl.ds(row, slab), pl.ds(lane, half)]
 
         return view
 
+    def block_view(ref):
+        def view(zz, xx, cc, part):
+            row = ref.at[zz * (SIDE * CORES) + xx * CORES + cc]
+            return row if part is None else row.at[:, pl.ds(*part)]
+
+        return view
+
+    def token_view(ref):
+        def view(zz, xx, cc, part):
+            rows = rows_of(zz * (SIDE * CORES) + xx * CORES + cc)
+            return ref.at[rows] if part is None else ref.at[rows, pl.ds(*part)]
+
+        return view
+
     sems = (gsend, grecv)
-    ag_x = Gather(place, lambda zz, xx, cc, part: xb.at[zz * 4 + xx * 2 + cc] if part is None else xb.at[zz * 4 + xx * 2 + cc, :, pl.ds(*part)], D, sems, 0)
-    ag_w = [
-        Gather(place, slab_view(first, width, False), width // CORES, sems, 1 + n)
-        for n, (first, width) in enumerate(GROUPS)
+    ag_x = Gather(place, block_view(xb), D, sems, 0)
+    ag_c = Gather(place, block_view(cb), D, sems, 1)
+    ag_n = Gather(place, token_view(nb), D, sems, 2)
+    tell_p = Tell(pb, 0)
+    spread = [
+        Spread(place, slab_view(first, width, other), slab_view(first, width, f), (wsend, wrecv), n)
+        for n, (first, width) in enumerate(CHUNKS)
     ]
-    ag_c = Gather(place, lambda zz, xx, cc, part: cb.at[zz * 4 + xx * 2 + cc] if part is None else cb.at[zz * 4 + xx * 2 + cc, :, pl.ds(*part)], D, sems, 4)
+
+    def push_chunk(n):
+        for i in LOADS_BY_CHUNK[n]:
+            loads[i].wait()
+        spread[n].push()
 
     ag_x.step_one()
-    gain_item = push_y(gainb.at[f], 3)
-    y_w = []
-    waits = ((0,), (1, 2, 3), tuple(range(4, 10)))
-    for n, (first, width) in enumerate(GROUPS):
-        for i in waits[n]:
-            loads[i].wait()
-        y_w.append(push_y(slab_view(first, width, True)(z, x, c, None), n))
+    push_chunk(0)
+    gain_item = push_y(gainb.at[f], gainb.at[f], 0)
+    tell_p.start()
+    push_chunk(1)
     ag_x.step_two()
-    y_w[0].wait_recv()
-    ag_w[0].step_one()
+    spread[0].step_one()
+    push_chunk(2)
     ag_x.step_three()
-    ag_w[0].step_two()
+    spread[0].step_two()
     ag_x.step_four()
-    y_w[1].wait_recv()
-    ag_w[1].step_one()
-    ag_w[0].step_three()
-    ag_c.step_one()
-    ag_w[1].step_two()
+    spread[1].step_one()
+    push_chunk(3)
+    spread[0].step_three()
+    ag_x.step_five()
+    spread[1].step_two()
+    spread[2].step_one()
+    push_chunk(4)
     gain_item.wait_recv()
 
     memp[0:own_rows] = mem_ref[...]
     memp[own_rows:padded] = jnp.zeros((padded - own_rows, D), BF16)
 
+    positions = []
+    before_large = jnp.int32(0)
+    mine_rank = jnp.int32(0)
+    for i in range(ranks):
+        group = res_ref[0, i]
+        spot = jnp.where(group == 1, lay.half + before_large, i - before_large)
+        positions.append(spot)
+        mine_rank = jnp.where(me == i, spot, mine_rank)
+        before_large = before_large + group
+
     def example_of(rank):
-        small = jnp.int32(0)
-        large = jnp.int32(0)
         found = jnp.int32(0)
         for i in range(ranks):
-            group = res_ref[0, i]
-            where = jnp.where(group == 1, lay.half + large, small)
-            found = jnp.where(where == rank, i, found)
-            large = large + group
-            small = small + (1 - group)
+            found = jnp.where(positions[i] == rank, i, found)
         return found
 
-    def rank_of_example(example):
-        before_large = jnp.int32(0)
-        mine = jnp.int32(0)
-        for i in range(ranks):
-            group = res_ref[0, i]
-            before_large = before_large + jnp.where(i < example, group, 0)
-            mine = jnp.where(i == example, group, mine)
-        return jnp.where(mine == 1, lay.half + before_large, example - before_large)
-
     gain = [jnp.concatenate([gainb[i, n : n + 1] for i in range(columns)], axis=1) for n in range(3)]
 
     mine = example_of(me)
-    resid = xb[mine, 0:SUFFIX]
+    resid = xb[mine]
     hat_one, rs_one = normed(resid)
     n1 = (hat_one * gain[0]).astype(BF16)
-
-    ag_w[0].step_four()
 
     lanes = lax.broadcasted_iota(jnp.int32, (1, 256), 1)
     head_f32 = [(lax.div(lanes, HEAD_DIM) == h).astype(F32) for h in range(4)]
@@ -377,9 +476,14 @@
             total = total + value[h * rows : (h + 1) * rows] * head_f32[h]
         return total
 
-    q = (mm(n1, wb[:, 0:768])).astype(BF16)
-    k = (mm(n1, wb[:, 768:1536])).astype(BF16)
-    v = (mm(n1, wb[:, 1536:2304])).astype(BF16)
+    spread[0].step_four()
+    q = mm(n1, wb[:, 0:D]).astype(BF16)
+    k = mm(n1, wb[:, D : 2 * D]).astype(BF16)
+    v = mm(n1, wb[:, 2 * D : 3 * D]).astype(BF16)
+    spread[1].step_three()
+    spread[2].step_two()
+    spread[3].step_one()
+    push_chunk(5)
     scale = HEAD_DIM**-0.5
     qs = (q.astype(F32) * scale).astype(BF16)
     row_at = lax.broadcasted_iota(jnp.int32, (SUFFIX, SUFFIX), 0)
@@ -397,20 +501,21 @@
         mixed.append(unstack(mm(p.astype(BF16), v[:, sl])))
     sm = jnp.concatenate(mixed, axis=1).astype(BF16)
 
-    ag_w[1].step_three()
-    ag_w[1].step_four()
-    y_w[2].wait_recv()
-    ag_w[2].step_one()
-    ag_c.step_two()
-
-    after_self = resid + mm(sm, wb[:, LANE_SO : LANE_SO + 768])
+    spread[1].step_four()
+    after_self = resid + mm(sm, wb[:, LANE_SO : LANE_SO + D])
     hat_two, rs_two = normed(after_self)
     n2 = (hat_two * gain[1]).astype(BF16)
-    cq = mm(n2, wb[:, LANE_CQ : LANE_CQ + 768]).astype(BF16)
+    cq = mm(n2, wb[:, LANE_CQ : LANE_CQ + D]).astype(BF16)
     cqb[...] = cq
 
     my_first, my_last = lay.first_device(me), lay.last_device(me)
     held_first, held_last = lay.first_rank(me), lay.last_rank(me)
+
+    def piece_copy(src, dst, at, sent, landed, target):
+        return pltpu.make_async_remote_copy(
+            src_ref=src, dst_ref=dst, send_sem=psend.at[at, sent], recv_sem=precv.at[at, landed],
+            device_id=(target, f), device_id_type=MESH,
+        )
 
     def to_holders(pairs):
         for i in range(SLOTS):
@@ -426,10 +531,7 @@
             @pl.when(there & (target != me))
             def _():
                 for src, dst, at in pairs:
-                    pltpu.make_async_remote_copy(
-                        src_ref=src, dst_ref=dst.at[slot], send_sem=psend.at[at, i],
-                        recv_sem=precv.at[at, slot], device_id=(target, f), device_id_type=MESH,
-                    ).start()
+                    piece_copy(src, dst.at[slot], at, i, slot, target).start()
 
     def to_holders_sent(pairs):
         for i in range(SLOTS):
@@ -438,10 +540,7 @@
             @pl.when((target <= my_last) & (target != me))
             def _():
                 for src, dst, at in pairs:
-                    pltpu.make_async_remote_copy(
-                        src_ref=src, dst_ref=dst.at[0], send_sem=psend.at[at, i],
-                        recv_sem=precv.at[at, 0], device_id=(target, f), device_id_type=MESH,
-                    ).wait_send()
+                    piece_copy(src, dst.at[0], at, i, 0, target).wait_send()
 
     def at_holders(pairs):
         for s in range(SLOTS):
@@ -450,10 +549,7 @@
             @pl.when((rank <= held_last) & (rank != me))
             def _():
                 for src, dst, at in pairs:
-                    pltpu.make_async_remote_copy(
-                        src_ref=src, dst_ref=dst.at[s], send_sem=psend.at[at, 0],
-                        recv_sem=precv.at[at, s], device_id=(rank, f), device_id_type=MESH,
-                    ).wait_recv()
+                    piece_copy(src, dst.at[s], at, 0, s, rank).wait_recv()
 
     def to_owners(pairs):
         for s in range(SLOTS):
@@ -469,10 +565,7 @@
             @pl.when(there & (rank != me))
             def _():
                 for src, dst, at in pairs:
-                    pltpu.make_async_remote_copy(
-                        src_ref=src.at[s], dst_ref=dst.at[index], send_sem=psend.at[at, s],
-                        recv_sem=precv.at[at, index], device_id=(rank, f), device_id_type=MESH,
-                    ).start()
+                    piece_copy(src.at[s], dst.at[index], at, s, index, rank).start()
 
     def to_owners_sent(pairs):
         for s in range(SLOTS):
@@ -481,10 +574,7 @@
             @pl.when((rank <= held_last) & (rank != me))
             def _():
                 for src, dst, at in pairs:
-                    pltpu.make_async_remote_copy(
-                        src_ref=src.at[s], dst_ref=dst.at[0], send_sem=psend.at[at, s],
-                        recv_sem=precv.at[at, 0], device_id=(rank, f), device_id_type=MESH,
-                    ).wait_send()
+                    piece_copy(src.at[s], dst.at[0], at, s, 0, rank).wait_send()
 
     def at_owners(pairs):
         for i in range(SLOTS):
@@ -493,10 +583,7 @@
             @pl.when((target <= my_last) & (target != me))
             def _():
                 for src, dst, at in pairs:
-                    pltpu.make_async_remote_copy(
-                        src_ref=src.at[0], dst_ref=dst.at[i], send_sem=psend.at[at, 0],
-                        recv_sem=precv.at[at, i], device_id=(target, f), device_id_type=MESH,
-                    ).wait_recv()
+                    piece_copy(src.at[0], dst.at[i], at, 0, i, target).wait_recv()
 
     q_pairs = [(cqb, qbuf, 0)]
     o_pairs = [(osend, obuf, 1), (ostat_send, ostat, 2)]
@@ -505,6 +592,11 @@
 
     to_holders(q_pairs)
 
+    spread[2].step_three()
+    spread[3].step_two()
+    spread[4].step_one()
+    spread[2].step_four()
+
     def kv_step(i, carry):
         lane = pl.multiple_of(i * 256, 256)
         kvb[:, pl.ds(lane, 256)] = mm(memp[...], wb[:, pl.ds(LANE_CKV + lane, 256)]).astype(BF16)
@@ -512,13 +604,14 @@
 
     lax.fori_loop(0, 6, kv_step, 0)
 
+    tell_p.wait()
     lane_f = lax.broadcasted_iota(jnp.int32, (SUFFIX, padded), 1).astype(F32)
     allowed = []
     for s in range(SLOTS):
         rank = held_first + s
         ok = rank <= held_last
         example = example_of(jnp.minimum(rank, ranks - 1))
-        prefix = xb[example, SUFFIX : SUFFIX + 8, 0:128][0:1, 0:1]
+        prefix = pb[example][0:1, 0:1]
         low = (lay.start(rank) - me * own_rows).astype(F32)
         patches = jnp.where(rank < lay.half, PATCH_S, PATCH_L).astype(F32)
         high = jnp.minimum(low + patches + prefix, jnp.float32(own_rows))
@@ -527,7 +620,6 @@
     allowed = jnp.concatenate(allowed * 4, axis=0) > 0.0
 
     at_holders(q_pairs)
-    to_holders_sent(q_pairs)
     qh = jnp.concatenate([qbuf[s] for s in range(SLOTS)], axis=0)
     qh = (qh.astype(F32) * scale).astype(BF16)
     lane_c = lax.broadcasted_iota(jnp.int32, (SUFFIX, 128), 1)
@@ -540,7 +632,7 @@
         top = jnp.max(s, axis=-1, keepdims=True)
         e = jnp.where(allowed, jnp.exp(s - top), 0.0)
         total = jnp.sum(e, axis=-1, keepdims=True)
-        o = mm(e.astype(BF16), kvb[:, 768 + 256 * g : 1024 + 256 * g])
+        o = mm(e.astype(BF16), kvb[:, D + 256 * g : D + 256 * g + 256])
         o = o * jnp.where(total > 0.0, 1.0 / jnp.where(total > 0.0, total, 1.0), 0.0)
         o = unstack(o).astype(BF16)
         for n in range(SLOTS):
@@ -555,11 +647,12 @@
         ostat_send[n, 1] = sum_c[n]
     to_owners(o_pairs)
 
-    ag_w[2].step_two()
-    ag_c.step_three()
-
+    spread[3].step_three()
+    spread[4].step_two()
+    spread[5].step_one()
+    ag_c.step_one()
+    spread[3].step_four()
     at_owners(o_pairs)
-    to_owners_sent(o_pairs)
 
     def expand(compact):
         low = lane_c < HEAD_DIM
@@ -579,44 +672,49 @@
         cross = cross + expand(shares[i] / whole) * obuf[i].astype(F32)
     cm = cross.astype(BF16)
 
-    ag_c.step_four()
-    ag_w[2].step_three()
-    ag_w[2].step_four()
-
-    after_cross = after_self + mm(cm, wb[:, LANE_CO : LANE_CO + 768])
+    after_cross = after_self + mm(cm, wb[:, LANE_CO : LANE_CO + D])
     hat_three, rs_three = normed(after_cross)
     n3 = (hat_three * gain[2]).astype(BF16)
-
-    cot = cb[mine]
-    out_low = cot.astype(BF16)
+    nb[rows_of(me)] = n3
+    ag_n.step_one()
+
+    spread[4].step_three()
+    spread[5].step_two()
+    ag_c.step_two()
+    spread[4].step_four()
+    spread[5].step_three()
+    ag_c.step_three()
+    ag_n.step_two()
+    ag_c.step_four()
+    ag_c.step_five()
+    spread[5].step_four()
+
+    out_low = cb[mine]
+    cot = out_low.astype(F32)
     acts, up_grads = [], []
-    hidden_grad = [mm_nt(out_low, wb[:, LANE_FO + 768 * j : LANE_FO + 768 * (j + 1)]) for j in range(4)]
+    hidden_grad = [mm_nt(out_low, wb[:, LANE_FO + D * j : LANE_FO + D * (j + 1)]) for j in range(4)]
 
     def by_hidden(j):
         parts = []
-        for t in range(768 // half_rows):
-            at = 768 * j + t * half_rows
+        for t in range(D // half_rows):
+            at = D * j + t * half_rows
             col, unit = at // (4 * half_rows), (at % (4 * half_rows)) // half_rows
             parts.append(hidden_grad[unit][:, col * half_rows : (col + 1) * half_rows])
         return jnp.concatenate(parts, axis=1)
 
     n3_grad = jnp.zeros((SUFFIX, D), F32)
     for j in range(4):
-        weight = wb[:, LANE_FI + 768 * j : LANE_FI + 768 * (j + 1)]
+        weight = wb[:, LANE_FI + D * j : LANE_FI + D * (j + 1)]
         value, slope = gelu_parts(mm(n3, weight))
         acts.append(value.astype(BF16))
-        ug = (by_hidden(j) * slope).astype(BF16)
-        up_grads.append(ug)
-        n3_grad = n3_grad + mm_nt(ug, weight)
+        part = (by_hidden(j) * slope).astype(BF16)
+        n3_grad = n3_grad + mm_nt(part, weight)
     act = jnp.concatenate(acts, axis=1)
-
-    def act_unit(j):
-        return [act[:, i * 4 * half_rows + j * half_rows : i * 4 * half_rows + (j + 1) * half_rows] for i in range(columns)]
 
     part, ffn_gain_grad = norm_back(n3_grad, hat_three, rs_three, gain[2])
     cross_res = cot + part
     cross_low = cross_res.astype(BF16)
-    d_mixed = mm_nt(cross_low, wb[:, LANE_CO : LANE_CO + 768]).astype(BF16)
+    d_mixed = mm_nt(cross_low, wb[:, LANE_CO : LANE_CO + D]).astype(BF16)
     dob[...] = d_mixed
     prod = d_mixed.astype(F32) * cross
     delta = jnp.zeros((SUFFIX, 128), F32)
@@ -629,57 +727,54 @@
     dstat_b[0] = lse
     dstat_b[1] = delta
     to_holders(d_pairs)
+    ag_n.step_three()
 
     down = jnp.zeros((SUFFIX, D), F32)
     for j in range(4):
-        down = down + mm(
-            jnp.concatenate(act_unit(j), axis=1), wb[:, LANE_FO + 768 * j : LANE_FO + 768 * (j + 1)]
+        lhs = jnp.concatenate(
+            [act[:, i * 4 * half_rows + j * half_rows : i * 4 * half_rows + (j + 1) * half_rows] for i in range(columns)],
+            axis=1,
         )
-    ob[me, 0:SUFFIX] = after_cross + down
-
-    def unit_device(u):
-        return 2 * u + 1 if u < 8 else 2 * (u - 8)
+        down = down + mm(lhs, wb[:, LANE_FO + D * j : LANE_FO + D * (j + 1)])
+    ob[me, 0:SUFFIX] = (after_cross + down).astype(BF16)
+
+    def unit_device(h):
+        return CORES * h if h < HALF_UNITS else CORES * (h - HALF_UNITS) + 1
 
     unit_items = []
 
-    def push_unit(u, left_parts, right):
-        to = unit_device(u)
-        for col in range(columns):
-            at = u * columns + col
-            sb[at, :, 0:half_rows] = left_parts[col]
-            sb[at, :, half_rows : half_rows + D] = right
-            self_hit = (me == to) & (f == col)
-            row = pl.multiple_of(lin * SUFFIX, SUFFIX)
-
-            @pl.when(self_hit)
-            def _():
-                rb[pl.ds(row, SUFFIX)] = sb[at]
-
-            @pl.when(jnp.logical_not(self_hit))
-            def _():
-                pltpu.make_async_remote_copy(
-                    src_ref=sb.at[at], dst_ref=rb.at[pl.ds(row, SUFFIX)], send_sem=usend.at[at],
-                    recv_sem=urecv.at[lin], device_id=(to, col), device_id_type=MESH,
-                ).start()
-
-            unit_items.append((at, to, col))
-
-    def halves(value):
-        return [value[:, i * half_rows : (i + 1) * half_rows] for i in range(columns)]
-
-    for j in range(4):
-        push_unit(8 + j, halves(n3), up_grads[j])
-        push_unit(12 + j, act_unit(j), out_low)
-    push_unit(7, halves(cm), cross_low)
+    def push_unit(h, left, right):
+        to = unit_device(h)
+        sb[h, :, 0:D] = left
+        sb[h, :, D : D + PIECE] = right
+
+        @pl.when(me == to)
+        def _():
+            rb[rows_of(me)] = sb[h]
+
+        @pl.when(me != to)
+        def _():
+            pltpu.make_async_remote_copy(
+                src_ref=sb.at[h], dst_ref=rb.at[rows_of(me)], send_sem=usend.at[h],
+                recv_sem=urecv.at[me], device_id=(to, f), device_id_type=MESH,
+            ).start()
+
+        unit_items.append((h, to))
+
+    ag_n.step_four()
+    push_unit(HALF_UNITS + 4, cm, cross_low[:, 0:PIECE])
+    push_unit(HALF_UNITS + 5, cm, cross_low[:, PIECE:])
+
+    for r in range(ranks):
+        olr[r * SUFFIX : (r + 1) * SUFFIX] = cb[example_of(r)]
 
     at_holders(d_pairs)
-    to_holders_sent(d_pairs)
 
     doh = jnp.concatenate([dobuf[s] for s in range(SLOTS)], axis=0)
     for g in range(3):
         sl = slice(256 * g, 256 * g + 256)
         kg = kvb[:, sl]
-        vg = kvb[:, 768 + 256 * g : 1024 + 256 * g]
+        vg = kvb[:, D + 256 * g : D + 256 * g + 256]
         q4 = stack(qh[:, sl])
         do4 = stack(doh[:, sl])
         lse_col = jnp.concatenate([dstat[n, 0][:, 4 * g + h : 4 * g + h + 1] for h in range(4) for n in range(SLOTS)], axis=0)
@@ -688,36 +783,60 @@
         p = jnp.where(allowed, jnp.exp(jnp.where(allowed, s - lse_col, 0.0)), 0.0)
         dp = mm_nt(do4, vg)
         ds = (p * (dp - del_col)).astype(BF16)
-        kvg[:, 768 + 256 * g : 1024 + 256 * g] = mm_tn(p.astype(BF16), do4).astype(BF16)
+        kvg[:, D + 256 * g : D + 256 * g + 256] = mm_tn(p.astype(BF16), do4).astype(BF16)
         kvg[:, sl] = mm_tn(ds, q4).astype(BF16)
         dq = unstack(mm(ds, kg)) * scale
         for n in range(SLOTS):
             dqsend[n, :, sl] = dq[n * SUFFIX : (n + 1) * SUFFIX]
     to_owners(dq_pairs)
 
-    def kp_step(i, carry):
-        lane = pl.multiple_of(i * 256, 256)
-        kp[:, pl.ds(lane, 256)] = mm_tn(memp[...], kvg[:, pl.ds(lane, 256)]).astype(BF16)
-        return carry
-
-    lax.fori_loop(0, 6, kp_step, 0)
-    mate = (z * 4 + x * 2 + (1 - c), f)
-    kr_item = pltpu.make_async_remote_copy(
-        src_ref=kp.at[pl.ds(pl.multiple_of((1 - c) * half_rows, 128), half_rows)], dst_ref=kr,
-        send_sem=ksend.at[2 * chips], recv_sem=krecv.at[2 * chips], device_id=mate, device_id_type=MESH,
-    )
-    kr_item.start()
+    ag_n.step_five()
+    rows_step = 128
+    steps = ranks * SUFFIX // rows_step
+
+    @pl.when(c == 0)
+    def _():
+        lane = pl.multiple_of(LANE_FI + PIECE * chip, 128)
+        row = pl.multiple_of(lax.div(chip, 4) * half_rows, 128)
+        lane_o = pl.multiple_of(LANE_FO + D * lax.rem(chip, 4), 128)
+
+        def one(i, carry):
+            at = pl.ds(pl.multiple_of(i * rows_step, rows_step), rows_step)
+            value, slope = gelu_parts(mm(nb[at], wb[:, pl.ds(lane, PIECE)]))
+            back = mm_nt(olr[at], wb[pl.ds(row, half_rows), pl.ds(lane_o, D)])
+            hb[0, at] = (back * slope).astype(BF16)
+            return carry
+
+        lax.fori_loop(0, steps, one, 0)
+        for col in range(columns):
+            fg[col] = mm_tn(nb[:, col * half_rows : (col + 1) * half_rows], hb[0])
+
+    @pl.when(c == 1)
+    def _():
+        side = pl.ds(pl.multiple_of(PIECE * lax.div(chip, 4), 128), PIECE)
+
+        def one(i, carry):
+            at = pl.ds(pl.multiple_of(i * rows_step, rows_step), rows_step)
+            for col in range(columns):
+                lane = pl.multiple_of(LANE_FI + col * 4 * half_rows + PIECE * lax.rem(chip, 4), 128)
+                value, slope = gelu_parts(mm(nb[at], wb[:, pl.ds(lane, PIECE)]))
+                hb[col, at] = value.astype(BF16)
+            return carry
+
+        lax.fori_loop(0, steps, one, 0)
+        for col in range(columns):
+            fg[col] = mm_tn(hb[col], olr[:, side])
+
+    fsend[...] = fg[other].astype(BF16)
+    f_item = push_y(fsend, frecv, 1)
 
     at_owners(dq_pairs)
-    to_owners_sent(dq_pairs)
     cqg = (dqbuf[0] + dqbuf[1] + dqbuf[2]).astype(BF16)
-    n2_grad = mm_nt(cqg, wb[:, LANE_CQ : LANE_CQ + 768])
+    n2_grad = mm_nt(cqg, wb[:, LANE_CQ : LANE_CQ + D])
     part, cross_gain_grad = norm_back(n2_grad, hat_two, rs_two, gain[1])
     self_res = cross_res + part
     self_low = self_res.astype(BF16)
-    push_unit(4, halves(n2), cqg)
-    push_unit(3, halves(sm), self_low)
-    dmix = mm_nt(self_low, wb[:, LANE_SO : LANE_SO + 768]).astype(BF16)
+    dmix = mm_nt(self_low, wb[:, LANE_SO : LANE_SO + D]).astype(BF16)
     dqs, dks, dvs = [], [], []
     for g in range(3):
         sl = slice(256 * g, 256 * g + 256)
@@ -730,105 +849,173 @@
         dks.append(mm_tn(ds, q4))
         dqs.append(unstack(mm(ds, k[:, sl])) * scale)
     packed_grad = [jnp.concatenate(parts, axis=1).astype(BF16) for parts in (dqs, dks, dvs)]
+    for h in range(HALF_UNITS):
+        push_unit(h, n1, packed_grad[h // 2][:, (h % 2) * PIECE : (h % 2 + 1) * PIECE])
+    for h in range(2):
+        push_unit(HALF_UNITS + 2 + h, n2, cqg[:, h * PIECE : (h + 1) * PIECE])
+        push_unit(HALF_UNITS + h, sm, self_low[:, h * PIECE : (h + 1) * PIECE])
+
+    f_item.wait_recv()
+    f_lane = jnp.where(
+        c == 0, LANE_FI + PIECE * chip, LANE_FO + D * lax.rem(chip, 4) + PIECE * lax.div(chip, 4)
+    )
+    gb[:, pl.ds(pl.multiple_of(f_lane, 128), PIECE)] = (fg[f] + frecv[...].astype(F32)).astype(BF16)
+
+    def gb_view(lane_of):
+        def view(zz, xx, cc, part):
+            low, size = part if part is not None else (0, PIECE)
+            return gb.at[:, pl.ds(pl.multiple_of(lane_of(zz * SIDE + xx, cc) + low, 128), size)]
+
+        return view
+
+    ag_f = Gather(
+        place,
+        gb_view(lambda n, cc: jnp.where(cc == 0, LANE_FI + PIECE * n, LANE_FO + D * lax.rem(n, 4) + PIECE * lax.div(n, 4))),
+        PIECE, sems, 3,
+    )
+    ag_f.step_one()
+
     n1_grad = jnp.zeros((SUFFIX, D), F32)
     for j in range(3):
-        push_unit(j, halves(n1), packed_grad[j])
-    for j in range(3):
-        n1_grad = n1_grad + mm_nt(packed_grad[j], wb[:, 768 * j : 768 * (j + 1)])
+        n1_grad = n1_grad + mm_nt(packed_grad[j], wb[:, D * j : D * (j + 1)])
     part, self_gain_grad = norm_back(n1_grad, hat_one, rs_one, gain[0])
-    ob[me, SUFFIX : 2 * SUFFIX] = self_res + part
+    ob[me, SUFFIX : 2 * SUFFIX] = (self_res + part).astype(BF16)
     gmine[...] = jnp.concatenate(
         [self_gain_grad, cross_gain_grad, ffn_gain_grad, jnp.zeros((5, D), F32)], axis=0
     )
-    g_item = pltpu.make_async_remote_copy(
-        src_ref=gmine, dst_ref=gpeer, send_sem=ysend.at[4], recv_sem=yrecv.at[4],
-        device_id=(me, other), device_id_type=MESH,
-    )
-    g_item.start()
+    g_item = push_y(gmine, gpeer, 2)
+
+    def kp_step(i, carry):
+        lane = pl.multiple_of(i * 256, 256)
+        kp[:, pl.ds(lane, 256)] = mm_tn(memp[...], kvg[:, pl.ds(lane, 256)]).astype(BF16)
+        return carry
+
+    lax.fori_loop(0, 6, kp_step, 0)
+    mate = (z * (SIDE * CORES) + x * CORES + (1 - c), f)
+    kr_item = pltpu.make_async_remote_copy(
+        src_ref=kp.at[pl.ds(pl.multiple_of((1 - c) * half_rows, 128), half_rows)], dst_ref=kr,
+        send_sem=ksend.at[2 * chips], recv_sem=krecv.at[chips], device_id=mate, device_id_type=MESH,
+    )
+    kr_item.start()
+
+    ag_f.step_two()
+
+    has_unit = chip < HALF_UNITS
+
+    def unit_lane(n, cc):
+        kind = lax.div(n, 2)
+        base = jnp.where(kind == 0, LANE_SO, jnp.where(kind == 1, LANE_CQ, LANE_CO))
+        return jnp.where(cc == 0, PIECE * n, base + PIECE * lax.rem(n, 2))
+
+    u_items = []
+
+    def unit_sum(pred, at):
+        @pl.when(pred)
+        def _():
+            def take(i, carry):
+                @pl.when(i != me)
+                def _():
+                    pltpu.make_async_remote_copy(
+                        src_ref=sb.at[0], dst_ref=rb.at[rows_of(i)], send_sem=usend.at[0],
+                        recv_sem=urecv.at[i], device_id=mate, device_id_type=MESH,
+                    ).wait_recv()
+
+                return carry
+
+            lax.fori_loop(0, ranks, take, 0)
+            for col in range(columns):
+                ug[col] = mm_tn(rb[:, col * half_rows : (col + 1) * half_rows], rb[:, D : D + PIECE])
+            usend_b[...] = ug[other].astype(BF16)
+            pltpu.make_async_remote_copy(
+                src_ref=usend_b, dst_ref=urecv_b, send_sem=ysend.at[at], recv_sem=yrecv.at[at],
+                device_id=(me, other), device_id_type=MESH,
+            ).start()
+
+    def unit_join(pred, at):
+        @pl.when(pred)
+        def _():
+            item = pltpu.make_async_remote_copy(
+                src_ref=usend_b, dst_ref=urecv_b, send_sem=ysend.at[at], recv_sem=yrecv.at[at],
+                device_id=(me, other), device_id_type=MESH,
+            )
+            item.wait_recv()
+            gb[:, pl.ds(pl.multiple_of(unit_lane(chip, c), 128), PIECE)] = (
+                ug[f] + urecv_b[...].astype(F32)
+            ).astype(BF16)
+            item.wait_send()
+
+    def has_block(zz, xx, cc):
+        return zz * SIDE + xx < HALF_UNITS
+
+    ag_u = Gather(place, gb_view(unit_lane), PIECE, sems, 4, has_block)
+    unit_sum(has_unit, 3)
 
     kr_item.wait_recv()
     kc[...] = (
         kp[pl.ds(pl.multiple_of(c * half_rows, 128), half_rows)].astype(F32) + kr[...].astype(F32)
     ).astype(BF16)
+    ky_item = pltpu.make_async_remote_copy(
+        src_ref=kc, dst_ref=ky, send_sem=ksend.at[2 * chips + 1], recv_sem=krecv.at[chips + 1],
+        device_id=(me, other), device_id_type=MESH,
+    )
+
+    @pl.when(c != f)
+    def _():
+        ky_item.start()
+
+    unit_join(has_unit, 3)
+    ag_u.step_one()
+    ag_f.step_three()
     k_items = []
+
+    def k_copy(t, j, src):
+        return pltpu.make_async_remote_copy(
+            src_ref=src, dst_ref=cp.at[chip], send_sem=ksend.at[t * CORES + j], recv_sem=krecv.at[chip],
+            device_id=(t * CORES + j, f), device_id_type=MESH,
+        )
+
+    @pl.when(c == f)
+    def _():
+        ky_item.wait_recv()
+        kc[...] = (kc[...].astype(F32) + ky[...].astype(F32)).astype(BF16)
+
     for t in range(chips):
         for j in range(CORES):
-            at = t * CORES + j
-            self_hit = (f == c) & (chip == t) & (c == j)
             src = kc.at[pl.ds(t * slab, slab), pl.ds(j * D, D)]
-            slot = f * chips + chip
-
-            @pl.when(self_hit)
+            here = (chip == t) & (c == j)
+
+            @pl.when((c == f) & here)
             def _():
-                cp[slot] = kc[pl.ds(t * slab, slab), pl.ds(j * D, D)]
-
-            @pl.when(jnp.logical_not(self_hit))
+                cp[chip] = kc[t * slab : (t + 1) * slab, j * D : (j + 1) * D]
+
+            @pl.when((c == f) & jnp.logical_not(here))
             def _():
-                pltpu.make_async_remote_copy(
-                    src_ref=src, dst_ref=cp.at[slot], send_sem=ksend.at[at], recv_sem=krecv.at[slot],
-                    device_id=(t * CORES + j, c), device_id_type=MESH,
-                ).start()
-
-            k_items.append((at, src, self_hit))
+                k_copy(t, j, src).start()
+
+            k_items.append((t, j, src, here))
 
     g_item.wait_recv()
-    ob[me, 2 * SUFFIX : 2 * SUFFIX + 8] = gmine[...] + gpeer[...]
-    ag_o = Gather(place, lambda zz, xx, cc, part: ob.at[zz * 4 + xx * 2 + cc] if part is None else ob.at[zz * 4 + xx * 2 + cc, :, pl.ds(*part)], D, sems, 5)
+    tb[me] = gmine[...] + gpeer[...]
+    tell_g = Tell(tb, 1)
+    tell_g.start()
+    ag_o = Gather(place, block_view(ob), D, sems, 5)
     ag_o.step_one()
-
-    unit = jnp.where(c == 1, chip, chip + 8)
-    has_unit = (unit != KV_UNITS[0]) & (unit != KV_UNITS[1])
-
-    def unit_lane(zz, xx, cc):
-        n = zz * SIDE + xx
-        u = jnp.where(cc == 1, n, n + 8)
-        spare = (u == KV_UNITS[0]) | (u == KV_UNITS[1])
-        return jnp.where(spare, UNITS + u - KV_UNITS[0], u) * D
-
-    @pl.when(has_unit)
-    def _():
-        def take(i, carry):
-            @pl.when(i != lin)
-            def _():
-                pltpu.make_async_remote_copy(
-                    src_ref=sb.at[0], dst_ref=rb.at[pl.ds(pl.multiple_of(i * SUFFIX, SUFFIX), SUFFIX)],
-                    send_sem=usend.at[0], recv_sem=urecv.at[i], device_id=mate, device_id_type=MESH,
-                ).wait_recv()
-            return carry
-
-        lax.fori_loop(0, everyone, take, 0)
-
-        def sum_step(i, carry):
-            lane = pl.multiple_of(i * 256, 256)
-            total = mm_tn(rb[:, 0:half_rows], rb[:, pl.ds(half_rows + lane, 256)])
-            gb[:, pl.ds(pl.multiple_of(unit_lane(z, x, c) + lane, 256), 256)] = total.astype(BF16)
-            return carry
-
-        lax.fori_loop(0, 3, sum_step, 0)
-
-    @pl.when(jnp.logical_not(has_unit))
-    def _():
-        gb[:, pl.ds(pl.multiple_of(unit_lane(z, x, c), 256), D)] = jnp.zeros((half_rows, D), BF16)
-
-    def unit_view(zz, xx, cc, part):
-        low, size = part if part is not None else (0, D)
-        return gb.at[:, pl.ds(pl.multiple_of(unit_lane(zz, xx, cc) + low, 128), size)]
-
-    ag_g = Gather(place, unit_view, D, sems, 6)
-    ag_g.step_one()
+    ag_u.step_two()
+    ag_f.step_four()
 
     def take_k(i, carry):
-        @pl.when((i != f * chips + chip) | (c != f))
+        @pl.when((i != chip) | (c != f))
         def _():
             pltpu.make_async_remote_copy(
                 src_ref=kc.at[pl.ds(0, slab), pl.ds(0, D)], dst_ref=cp.at[i], send_sem=ksend.at[0],
                 recv_sem=krecv.at[i], device_id=mate, device_id_type=MESH,
             ).wait_recv()
+
         return carry
 
-    lax.fori_loop(0, 2 * chips, take_k, 0)
+    lax.fori_loop(0, chips, take_k, 0)
     total = cp[0].astype(F32)
-    for i in range(1, 2 * chips):
+    for i in range(1, chips):
         total = total + cp[i].astype(F32)
     k_lane = pl.multiple_of(LANE_CKV + c * D, 128)
     gb[pl.ds(pl.multiple_of(chip * slab, 16), slab), pl.ds(k_lane, D)] = total.astype(BF16)
@@ -838,15 +1025,11 @@
         row = pl.multiple_of((zz * SIDE + xx) * slab, 16)
         return gb.at[pl.ds(row, slab), pl.ds(pl.multiple_of(LANE_CKV + cc * D + low, 128), size)]
 
-    ag_k = Gather(place, kv_view, D, sems, 7)
+    ag_k = Gather(place, kv_view, D, sems, 6)
     ag_k.step_one()
+    ag_u.step_three()
     ag_o.step_two()
     ag_k.step_two()
-    ag_o.step_three()
-    ag_k.step_three()
-    ag_o.step_four()
-    ag_k.step_four()
-    ag_g.step_two()
 
     def mg_step(i, carry):
         row = pl.multiple_of(i * 128, 128)
@@ -859,40 +1042,54 @@
         tail = mm_nt(kvg[full * 128 : (full + 1) * 128], wb[:, LANE_CKV : LANE_CKV + 2 * D])
         memgrad_ref[full * 128 : own_rows] = tail[0 : own_rows - full * 128]
 
-    mine_rank = rank_of_example(me)
-    out_ref[...] = ob[mine_rank, 0:SUFFIX]
-    grad_ref[...] = ob[mine_rank, SUFFIX : 2 * SUFFIX]
-    gains_all = ob[0, 2 * SUFFIX : 2 * SUFFIX + 8]
+    ag_u.step_four()
+    ag_o.step_three()
+    ag_k.step_three()
+    ag_o.step_four()
+    ag_k.step_four()
+    tell_g.wait()
+    gains_all = tb[0]
     for i in range(1, ranks):
-        gains_all = gains_all + ob[i, 2 * SUFFIX : 2 * SUFFIX + 8]
+        gains_all = gains_all + tb[i]
     own_gain = gains_all[:, 0:half_rows]
     for i in range(1, columns):
         own_gain = jnp.where(f == i, gains_all[:, i * half_rows : (i + 1) * half_rows], own_gain)
     gain_out_ref[...] = own_gain
-
-    ag_g.step_three()
-    ag_g.step_four()
-    done = pltpu.make_async_copy(gb.at[:, pl.ds(0, UNITS * D)], weights_out_ref, load_sem.at[0])
+    ag_f.step_five()
+    ag_o.step_five()
+    out_ref[...] = ob[mine_rank, 0:SUFFIX].astype(F32)
+    grad_ref[...] = ob[mine_rank, SUFFIX : 2 * SUFFIX].astype(F32)
+    ag_k.step_five()
+    ag_u.step_five()
+    done = pltpu.make_async_copy(gb, weights_out_ref, load_sem.at[0])
     done.start()
 
-    for at, to, col in unit_items:
-        @pl.when(jnp.logical_not((me == to) & (f == col)))
+    to_holders_sent(q_pairs)
+    to_owners_sent(o_pairs)
+    to_holders_sent(d_pairs)
+    to_owners_sent(dq_pairs)
+    for h, to in unit_items:
+        @pl.when(me != to)
         def _():
             pltpu.make_async_remote_copy(
-                src_ref=sb.at[at], dst_ref=rb.at[pl.ds(0, SUFFIX)], send_sem=usend.at[at],
-                recv_sem=urecv.at[0], device_id=(to, col), device_id_type=MESH,
+                src_ref=sb.at[h], dst_ref=rb.at[rows_of(me)], send_sem=usend.at[h],
+                recv_sem=urecv.at[0], device_id=(to, f), device_id_type=MESH,
             ).wait_send()
-    for at, src, self_hit in k_items:
-        @pl.when(jnp.logical_not(self_hit))
+    for t, j, src, here in k_items:
+        @pl.when((c == f) & jnp.logical_not(here))
         def _():
-            pltpu.make_async_remote_copy(
-                src_ref=src, dst_ref=cp.at[0], send_sem=ksend.at[at], recv_sem=krecv.at[0],
-                device_id=mate, device_id_type=MESH,
-            ).wait_send()
+            k_copy(t, j, src).wait_send()
     kr_item.wait_send()
-    for item in y_items + [g_item]:
+
+    @pl.when(c != f)
+    def _():
+        ky_item.wait_send()
+
+    for item in y_items:
         item.wait_send()
-    for item in [ag_x, *ag_w, ag_c, ag_o, ag_g, ag_k]:
+    tell_p.finish()
+    tell_g.finish()
+    for item in [ag_x, *spread, ag_c, ag_n, ag_f, ag_u, ag_o, ag_k]:
         item.finish()
     done.wait()
 
@@ -907,7 +1104,7 @@
     slab = half_rows // chips
     own_rows = memory.shape[1]
     padded = -(-own_rows // 128) * 128
-    everyone = ranks * columns
+    tokens = ranks * SUFFIX
     gains = jnp.stack([self_gain, cross_gain, ffn_gain]).astype(F32)
     gains = jnp.pad(gains, ((0, 5), (0, 0)))
     vm = pl.BlockSpec(memory_space=pltpu.VMEM)
@@ -916,12 +1113,16 @@
     dma = pltpu.SemaphoreType.DMA
     scratch = [
         pltpu.VMEM((D, UNITS * D), BF16),
-        pltpu.VMEM((half_rows, (UNITS + 2) * D), BF16),
-        pltpu.VMEM((everyone * SUFFIX, half_rows + D), BF16),
-        pltpu.VMEM((UNITS * columns, SUFFIX, half_rows + D), BF16),
-        pltpu.VMEM((ranks, SUFFIX + 8, D), F32),
+        pltpu.VMEM((half_rows, UNITS * D), BF16),
+        pltpu.VMEM((tokens, D + PIECE), BF16),
+        pltpu.VMEM((2 * HALF_UNITS, SUFFIX, D + PIECE), BF16),
         pltpu.VMEM((ranks, SUFFIX, D), F32),
-        pltpu.VMEM((ranks, 2 * SUFFIX + 8, D), F32),
+        pltpu.VMEM((ranks, SUFFIX, D), BF16),
+        pltpu.VMEM((tokens, D), BF16),
+        pltpu.VMEM((tokens, D), BF16),
+        pltpu.VMEM((ranks, 2 * SUFFIX, D), BF16),
+        pltpu.VMEM((ranks, 8, D), F32),
+        pltpu.VMEM((ranks, 8, 128), F32),
         pltpu.VMEM((columns, 8, half_rows), F32),
         pltpu.VMEM((padded, D), BF16),
         pltpu.VMEM((padded, 2 * D), BF16),
@@ -929,7 +1130,15 @@
         pltpu.VMEM((D, 2 * D), BF16),
         pltpu.VMEM((half_rows, 2 * D), BF16),
         pltpu.VMEM((half_rows, 2 * D), BF16),
-        pltpu.VMEM((columns * chips, slab, D), BF16),
+        pltpu.VMEM((half_rows, 2 * D), BF16),
+        pltpu.VMEM((chips, slab, D), BF16),
+        pltpu.VMEM((columns, tokens, PIECE), BF16),
+        pltpu.VMEM((columns, half_rows, PIECE), F32),
+        pltpu.VMEM((half_rows, PIECE), BF16),
+        pltpu.VMEM((half_rows, PIECE), BF16),
+        pltpu.VMEM((columns, half_rows, PIECE), F32),
+        pltpu.VMEM((half_rows, PIECE), BF16),
+        pltpu.VMEM((half_rows, PIECE), BF16),
         pltpu.VMEM((SUFFIX, D), BF16),
         pltpu.VMEM((SLOTS, SUFFIX, D), BF16),
         pltpu.VMEM((SLOTS, SUFFIX, D), BF16),
@@ -945,16 +1154,20 @@
         pltpu.VMEM((8, D), F32),
         pltpu.VMEM((8, D), F32),
         dma((10,)),
-        dma((8, 16)),
-        dma((8, 16)),
-        dma((5,)),
-        dma((5,)),
+        dma((len(CHUNKS), 16)),
+        dma((len(CHUNKS), 16)),
+        dma((7, 16)),
+        dma((7, 16)),
+        dma((2, ranks)),
+        dma((2, ranks)),
+        dma((4,)),
+        dma((4,)),
         dma((6, SLOTS)),
         dma((6, SLOTS)),
-        dma((UNITS * columns,)),
-        dma((everyone,)),
-        dma((2 * chips + 1,)),
-        dma((2 * chips + 1,)),
+        dma((2 * HALF_UNITS,)),
+        dma((ranks,)),
+        dma((2 * chips + 2,)),
+        dma((chips + 2,)),
     ]
     out, grad, memgrad, gain_grads, weight_grads = pl.pallas_call(
         partial(layer_kernel, ranks, columns),

time: 382 us -> 273 us (0.71)
  the two profiles are of different devices: /device:TPU:21 before, /device:TPU:19 now
where the time goes in v2:
time: 273 us
  Pallas kernels  249 us (91%)
  other arithmetic  14.2 us (5%)
  local copies, waits for them, and re-layouts  8.59 us (3%)
    pallas_call x1, Pallas kernels, fused_body(): pl.pallas_call(partial(layer_kernel, ranks, columns), out_shape=(jax.Shap...  249 us
    convert_element_type x3, other arithmetic, lanes(): return weight_grads[:, low:low + width].astype(F32)  9.22 us

profile of v2, /device:TPU:19, one launch (start us, length us, event | category | flops | bytes accessed | tf_op | source)
XLA Modules:
  0.0 273.1 jit_solution(3091175368073150326)
XLA Ops:
  1.3 0.7 stack.12
  2.0 0.7 stack.13
  2.7 0.7 stack.14
  3.3 0.6 fusion.5.gains_ref
  3.9 249.0 %layer.1 = (f32[32,768]{1,0:T(8,128)}, f32[32,768]{1,0:T(8,128)}, f32[418,768]{1,0:T(8,128)}, f32[8,384]{1,0:T(8,128)}, bf16[384,12288]{1,0:T(8,128)(2,1)}) custom-call(f32[32,768]{1,0:T(8,128)} %bitcast.8, f32[32,768]{1,0:T(8,128)} %bitcast.9, bf16[418,768]{1,0:T(8,128)(2,1)} %bitcast.7, s32[1,16]{1,0:T(1,128)} %res_ref.1, s32[1,1]{1,0:T(1,128)S(6)} %copy.31.pre_ref, ...), custom_call_target="tpu_custom_call" | custom-call | tf_op jit(solution)/shard_map/layer/pallas_call | solution.py:1172
  252.9 1.4 slice_reduce_fusion
  254.4 0.0 copy-start
  254.4 3.8 %copy.28 = f32[1,418,768]{2,0,1:T(1,128)} copy(f32[1,418,768]{2,1,0:T(8,128)} %bitcast.6) | data formatting | bytes 2568192
  258.2 3.0 %slice_convert_fusion.2 = f32[384,1536]{1,0:T(8,128)} fusion(bf16[384,12288]{1,0:T(8,128)(2,1)} %get-tuple-element.22), kind=kLoop, calls=%fused_computation.3 | loop fusion | flops 589824 | bytes 3538944 | tf_op jit(solution)/shard_map/convert_element_type | solution.py:1194
  261.2 3.5 %slice_convert_fusion.1 = f32[384,2304]{1,0:T(8,128)} fusion(bf16[384,12288]{1,0:T(8,128)(2,1)} %get-tuple-element.22), kind=kLoop, calls=%fused_computation.2 | loop fusion | flops 884736 | bytes 5308416 | tf_op jit(solution)/shard_map/convert_element_type | solution.py:1194
  264.7 0.0 copy-done
  264.7 2.8 %slice_convert_fusion = f32[384,3072]{1,0:T(8,128)} fusion(bf16[384,12288]{1,0:T(8,128)(2,1)S(1)} %copy-done), kind=kLoop, calls=%fused_computation.1 | loop fusion | flops 1179648 | bytes 7077888 | tf_op jit(solution)/shard_map/convert_element_type | solution.py:1194
  267.4 1.9 fusion.6
  269.3 0.0 copy-start.2
  269.3 0.0 copy-start.1
  269.3 2.5 maximum_convert_fusion
  271.8 0.0 copy-done.2
  271.8 0.6 copy.32
  272.5 0.0 copy-done.1
  272.5 0.6 copy.33
Async XLA Ops:
  254.4 10.3 %copy-start = (bf16[384,12288]{1,0:T(8,128)(2,1)S(1)}, bf16[384,12288]{1,0:T(8,128)(2,1)}, u32[]{:S(2)}) copy-start(bf16[384,12288]{1,0:T(8,128)(2,1)} %get-tuple-element.22) | copy-start | bytes 28311556
  269.3 2.6 copy-start.2
  269.3 3.2 %copy-start.1 = (f32[32,768]{1,0:T(8,128)S(1)}, f32[32,768]{1,0:T(8,128)}, u32[]{:S(2)}) copy-start(f32[32,768]{1,0:T(8,128)} %get-tuple-element.19) | copy-start | bytes 294916

commit v3 on v2

--- a/solution.py
+++ b/solution.py
@@ -62,7 +62,7 @@
     return value, grad
 
 
-class Relay:
+class Gather:
     def __init__(self, place, view, sems, at, has=None):
         self.z, self.x, self.c, self.f = place
         self.view = view
@@ -70,24 +70,9 @@
         self.at = at
         self.has = has
         self.sent = []
-        self.own = (self.z, self.x, self.c)
-        self.side = (self.z, 1 - self.x, self.c)
-        self.up = (lax.rem(self.z + 1, RING), self.x, self.c)
-        self.down = (lax.rem(self.z + 3, RING), self.x, self.c)
-        self.far = (lax.rem(self.z + 2, RING), self.x, self.c)
-        self.up_side = (self.up[0], 1 - self.x, self.c)
-        self.down_side = (self.down[0], 1 - self.x, self.c)
-        self.far_side = (self.far[0], 1 - self.x, self.c)
-        self.mate = (self.z, self.x, 1 - self.c)
-
-    def when(self, block, act):
-        if self.has is None:
-            act()
-        else:
-            pl.when(self.has(*block))(act)
-
-    def copy(self, block, part, target, into, index):
-        ref = self.view(*block, part)
+
+    def copy(self, block, target, into, index):
+        ref = self.view(*block)
         z, x, c = target
         return pltpu.make_async_remote_copy(
             src_ref=ref,
@@ -98,120 +83,112 @@
             device_id_type=MESH,
         )
 
-    def go(self, block, target, into, part=None):
-        item = self.copy(block, part, target, into, len(self.sent))
-        self.when(block, item.start)
-        self.sent.append((block, item))
-
-    def wait(self, block, into, part=None):
-        self.when(block, self.copy(block, part, self.side, into, 0).wait_recv)
+    def place_at(self, k):
+        return lax.rem(self.z + k + RING, RING)
+
+    def holds(self, block, cond):
+        return cond if self.has is None else cond & self.has(*block)
+
+    def go(self, block, target, into, cond):
+        item = self.copy(block, target, into, len(self.sent))
+        cond = self.holds(block, cond)
+        pl.when(cond)(item.start)
+        self.sent.append((cond, item))
+
+    def wait(self, block, into, cond):
+        pl.when(self.holds(block, cond))(self.copy(block, (self.z, 1 - self.x, self.c), into, 0).wait_recv)
+
+    def line(self, block, up, down, cond):
+        z, x, c = self.z, self.x, self.c
+        at = block[0]
+        if up:
+            self.go(block, (self.place_at(1), x, c), at, cond & (z < RING - 1))
+        if down:
+            self.go(block, (self.place_at(-1), x, c), at, cond & (z > 0))
+
+    def spread(self, block, cond):
+        z, x, c = self.z, self.x, self.c
+        self.go(block, (z, 1 - x, c), RING + block[0], cond)
+        self.go(block, (z, x, 1 - c), 2 * RING + block[0], cond)
+
+    def step_one(self):
+        own = (self.z, self.x, self.c)
+        self.line(own, True, True, self.z >= 0)
+        self.spread(own, self.z >= 0)
+
+    def arrive(self, k):
+        low, high = (self.place_at(-k), self.x, self.c), (self.place_at(k), self.x, self.c)
+        self.wait(low, low[0], self.z >= k)
+        self.line(low, True, False, self.z >= k)
+        self.wait(high, high[0], self.z < RING - k)
+        self.line(high, False, True, self.z < RING - k)
+        self.spread(low, self.z >= k)
+        self.spread(high, self.z < RING - k)
+
+    def side(self, k):
+        z, x, c = self.z, self.x, self.c
+        for at, cond in ((self.place_at(-k), z >= k), (self.place_at(k), z < RING - k))[: 1 if k == 0 else 2]:
+            block = (at, 1 - x, c)
+            self.wait(block, RING + at, cond)
+            self.go(block, (z, x, 1 - c), 3 * RING + at, cond)
+
+    def step_two(self):
+        self.arrive(1)
+        self.side(0)
+
+    def step_three(self):
+        self.arrive(2)
+        self.side(1)
+
+    def step_four(self):
+        self.arrive(3)
+        self.side(2)
+
+    def step_five(self):
+        self.side(3)
+        always = self.z >= 0
+        for at in range(RING):
+            self.wait((at, self.x, 1 - self.c), 2 * RING + at, always)
+            self.wait((at, 1 - self.x, 1 - self.c), 3 * RING + at, always)
 
     def finish(self):
-        for block, item in self.sent:
-            self.when(block, item.wait_send)
-
-
-class Gather(Relay):
-    def __init__(self, place, view, width, sems, at, has=None):
-        super().__init__(place, view, sems, at, has)
-        half = (width // 256) * 128
-        self.parts = ((0, half), (half, width - half))
-
-    def step_one(self):
-        self.go(self.own, self.up, 1)
-        self.go(self.own, self.down, 2)
-        self.go(self.own, self.side, 0)
-        self.go(self.own, self.mate, 8)
-
-    def step_two(self):
-        low, high = self.parts
-        self.wait(self.down, 1)
-        self.go(self.down, self.up, 3, low)
-        self.wait(self.up, 2)
-        self.go(self.up, self.down, 4, high)
-        self.wait(self.side, 0)
-        self.go(self.side, self.up, 5)
-        self.go(self.side, self.down, 6)
-        self.go(self.down, self.mate, 10)
-        self.go(self.up, self.mate, 11)
-        self.go(self.side, self.mate, 9)
-
-    def step_three(self):
-        low, high = self.parts
-        self.wait(self.far, 3, low)
-        self.wait(self.far, 4, high)
-        self.go(self.far, self.side, 7)
-        self.go(self.far, self.mate, 12)
-        self.wait(self.down_side, 5)
-        self.go(self.down_side, self.mate, 13)
-        self.wait(self.up_side, 6)
-        self.go(self.up_side, self.mate, 14)
-
-    def step_four(self):
-        self.wait(self.far_side, 7)
-        self.go(self.far_side, self.mate, 15)
-
-    def step_five(self):
-        z, x, c = self.mate
-        order = (self.own, self.side, self.down, self.up, self.far, self.down_side, self.up_side, self.far_side)
-        for n, block in enumerate(order):
-            self.wait((block[0], block[1], c), 8 + n)
-
-
-class Spread(Relay):
+        for cond, item in self.sent:
+            pl.when(cond)(item.wait_send)
+
+
+class Spread(Gather):
     def __init__(self, place, theirs, mine, sems, at):
         super().__init__(place, theirs, sems, at)
         self.mine = mine
-        self.columns_item = []
+        self.pushed = []
 
     def push(self):
-        z, x, c = self.own
-        for n, block in enumerate((self.own, self.far)):
-            ref = self.mine(*block, None)
+        z, x, c = self.z, self.x, self.c
+        for n, block in enumerate(((z, x, c), (z, 1 - x, c))):
+            ref = self.mine(*block)
             item = pltpu.make_async_remote_copy(
-                src_ref=ref, dst_ref=ref, send_sem=self.send.at[self.at, 14 + n], recv_sem=self.recv.at[self.at, 14 + n],
+                src_ref=ref, dst_ref=ref, send_sem=self.send.at[self.at, 28 + n], recv_sem=self.recv.at[self.at, 16 + n],
                 device_id=(z * (SIDE * CORES) + x * CORES + c, 1 - self.f), device_id_type=MESH,
             )
             item.start()
-            self.columns_item.append(item)
+            self.pushed.append(item)
 
     def step_one(self):
-        self.wait(self.own, 14)
-        self.go(self.own, self.side, 0)
-        self.go(self.own, self.up, 1)
-        self.go(self.own, self.down, 2)
-        self.go(self.own, self.mate, 6)
-        self.wait(self.far, 15)
-        self.go(self.far, self.side, 3)
-        self.go(self.far, self.mate, 7)
+        z, x, c = self.z, self.x, self.c
+        always = z >= 0
+        own, side = (z, x, c), (z, 1 - x, c)
+        self.wait(own, 16, always)
+        self.line(own, True, True, always)
+        self.go(own, (z, x, 1 - c), 2 * RING + z, always)
+        self.wait(side, 17, always)
+        self.go(side, (z, x, 1 - c), 3 * RING + z, always)
 
     def step_two(self):
-        self.wait(self.side, 0)
-        self.go(self.side, self.up, 4)
-        self.go(self.side, self.down, 5)
-        self.go(self.side, self.mate, 8)
-        self.wait(self.down, 1)
-        self.go(self.down, self.mate, 9)
-        self.wait(self.up, 2)
-        self.go(self.up, self.mate, 10)
-
-    def step_three(self):
-        self.wait(self.far_side, 3)
-        self.go(self.far_side, self.mate, 11)
-        self.wait(self.down_side, 4)
-        self.go(self.down_side, self.mate, 12)
-        self.wait(self.up_side, 5)
-        self.go(self.up_side, self.mate, 13)
-
-    def step_four(self):
-        c = self.mate[2]
-        order = (self.own, self.far, self.side, self.down, self.up, self.far_side, self.down_side, self.up_side)
-        for n, block in enumerate(order):
-            self.wait((block[0], block[1], c), 6 + n)
+        self.arrive(1)
 
     def finish(self):
         super().finish()
-        for item in self.columns_item:
+        for item in self.pushed:
             item.wait_send()
 
 
@@ -266,9 +243,10 @@
     qkv_ref, so_ref, cq_ref, ckv_ref, co_ref, fi_ref, fo_ref,
     out_ref, grad_ref, memgrad_ref, gain_out_ref, weights_out_ref,
     wb, gb, rb, sb, xb, cb, nb, olr, ob, tb, pb, gainb, memp, kvb, kvg, kp, kr, kc, ky, cp,
-    hb, fg, fsend, frecv, ug, usend_b, urecv_b,
+    kx, ks, hb, ab, ug, usend_b, urecv_b,
     cqb, qbuf, osend, ostat_send, obuf, ostat, dob, dstat_b, dobuf, dstat, dqsend, dqbuf, gmine, gpeer,
-    load_sem, wsend, wrecv, gsend, grecv, bsend, brecv, ysend, yrecv, psend, precv, usend, urecv, ksend, krecv,
+    load_sem, wsend, wrecv, gsend, grecv, bsend, brecv, asend, arecv, fsend, frecv, ysend, yrecv, psend, precv, usend, urecv,
+    ksend, krecv,
 ):
     me = lax.axis_index("dp")
     f = lax.axis_index("fsdp")
@@ -284,6 +262,7 @@
     padded = memp.shape[0]
     lay = Pieces(ranks, own_rows)
     other = 1 - f
+    mate = (z * (SIDE * CORES) + x * CORES + (1 - c), f)
     everyone = ranks * columns
     lin = f * ranks + me
 
@@ -380,7 +359,7 @@
     def slab_view(first, width, rows_from):
         half = width // CORES
 
-        def view(zz, xx, cc, part):
+        def view(zz, xx, cc):
             row = pl.multiple_of(rows_from * half_rows + (zz * SIDE + xx) * slab, 16)
             lane = pl.multiple_of(first + cc * half, 128)
             return wb.at[pl.ds(row, slab), pl.ds(lane, half)]
@@ -388,23 +367,53 @@
         return view
 
     def block_view(ref):
-        def view(zz, xx, cc, part):
-            row = ref.at[zz * (SIDE * CORES) + xx * CORES + cc]
-            return row if part is None else row.at[:, pl.ds(*part)]
+        def view(zz, xx, cc):
+            return ref.at[zz * (SIDE * CORES) + xx * CORES + cc]
 
         return view
 
+    def token_rows(col, cc, at):
+        return pl.ds(pl.multiple_of(((col * CORES + cc) * chips + at) * SUFFIX, SUFFIX), SUFFIX)
+
     def token_view(ref):
-        def view(zz, xx, cc, part):
-            rows = rows_of(zz * (SIDE * CORES) + xx * CORES + cc)
-            return ref.at[rows] if part is None else ref.at[rows, pl.ds(*part)]
+        def view(zz, xx, cc):
+            return ref.at[token_rows(f, cc, zz * SIDE + xx)]
 
         return view
 
+    plane = pl.ds(pl.multiple_of((f * CORES + c) * chips * SUFFIX, SUFFIX), chips * SUFFIX)
+    plane_in = pl.ds(pl.multiple_of((other * CORES + c) * chips * SUFFIX, SUFFIX), chips * SUFFIX)
+    plane_mate = pl.ds(pl.multiple_of((other * CORES + 1 - c) * chips * SUFFIX, SUFFIX), chips * SUFFIX)
+
+    class Across:
+        def __init__(self, ref, at):
+            self.ref, self.at = ref, at
+
+        def copy(self, rows, n, to):
+            ref = self.ref.at[rows]
+            return pltpu.make_async_remote_copy(
+                src_ref=ref, dst_ref=ref, send_sem=asend.at[self.at, n], recv_sem=arecv.at[self.at, n],
+                device_id=to, device_id_type=MESH,
+            )
+
+        def start(self):
+            self.copy(plane, 0, (me, other)).start()
+
+        def relay(self):
+            self.copy(plane_in, 0, (me, other)).wait_recv()
+            self.copy(plane_in, 1, mate).start()
+
+        def wait(self):
+            self.copy(plane_mate, 1, mate).wait_recv()
+
+        def finish(self):
+            self.copy(plane, 0, (me, other)).wait_send()
+            self.copy(plane_in, 1, mate).wait_send()
+
     sems = (gsend, grecv)
-    ag_x = Gather(place, block_view(xb), D, sems, 0)
-    ag_c = Gather(place, block_view(cb), D, sems, 1)
-    ag_n = Gather(place, token_view(nb), D, sems, 2)
+    ag_x = Gather(place, block_view(xb), sems, 0)
+    ag_c = Gather(place, block_view(cb), sems, 1)
+    ag_n = Gather(place, token_view(nb), sems, 2)
     tell_p = Tell(pb, 0)
     spread = [
         Spread(place, slab_view(first, width, other), slab_view(first, width, f), (wsend, wrecv), n)
@@ -421,19 +430,22 @@
     gain_item = push_y(gainb.at[f], gainb.at[f], 0)
     tell_p.start()
     push_chunk(1)
+
+    def tick(n):
+        for age, act in ((4, "step_five"), (3, "step_four"), (2, "step_three"), (1, "step_two"), (0, "step_one")):
+            if 0 <= n - age < len(spread):
+                getattr(spread[n - age], act)()
+        if n + 2 < len(spread):
+            push_chunk(n + 2)
+
     ag_x.step_two()
-    spread[0].step_one()
-    push_chunk(2)
+    tick(0)
     ag_x.step_three()
-    spread[0].step_two()
+    tick(1)
     ag_x.step_four()
-    spread[1].step_one()
-    push_chunk(3)
-    spread[0].step_three()
+    tick(2)
     ag_x.step_five()
-    spread[1].step_two()
-    spread[2].step_one()
-    push_chunk(4)
+    tick(3)
     gain_item.wait_recv()
 
     memp[0:own_rows] = mem_ref[...]
@@ -476,14 +488,10 @@
             total = total + value[h * rows : (h + 1) * rows] * head_f32[h]
         return total
 
-    spread[0].step_four()
+    tick(4)
     q = mm(n1, wb[:, 0:D]).astype(BF16)
     k = mm(n1, wb[:, D : 2 * D]).astype(BF16)
     v = mm(n1, wb[:, 2 * D : 3 * D]).astype(BF16)
-    spread[1].step_three()
-    spread[2].step_two()
-    spread[3].step_one()
-    push_chunk(5)
     scale = HEAD_DIM**-0.5
     qs = (q.astype(F32) * scale).astype(BF16)
     row_at = lax.broadcasted_iota(jnp.int32, (SUFFIX, SUFFIX), 0)
@@ -501,7 +509,7 @@
         mixed.append(unstack(mm(p.astype(BF16), v[:, sl])))
     sm = jnp.concatenate(mixed, axis=1).astype(BF16)
 
-    spread[1].step_four()
+    tick(5)
     after_self = resid + mm(sm, wb[:, LANE_SO : LANE_SO + D])
     hat_two, rs_two = normed(after_self)
     n2 = (hat_two * gain[1]).astype(BF16)
@@ -592,10 +600,8 @@
 
     to_holders(q_pairs)
 
-    spread[2].step_three()
-    spread[3].step_two()
-    spread[4].step_one()
-    spread[2].step_four()
+    tick(6)
+    ag_c.step_one()
 
     def kv_step(i, carry):
         lane = pl.multiple_of(i * 256, 256)
@@ -647,11 +653,8 @@
         ostat_send[n, 1] = sum_c[n]
     to_owners(o_pairs)
 
-    spread[3].step_three()
-    spread[4].step_two()
-    spread[5].step_one()
-    ag_c.step_one()
-    spread[3].step_four()
+    tick(7)
+    ag_c.step_two()
     at_owners(o_pairs)
 
     def expand(compact):
@@ -675,20 +678,16 @@
     after_cross = after_self + mm(cm, wb[:, LANE_CO : LANE_CO + D])
     hat_three, rs_three = normed(after_cross)
     n3 = (hat_three * gain[2]).astype(BF16)
-    nb[rows_of(me)] = n3
+    nb[token_rows(f, c, chip)] = n3
     ag_n.step_one()
 
-    spread[4].step_three()
-    spread[5].step_two()
-    ag_c.step_two()
-    spread[4].step_four()
-    spread[5].step_three()
+    tick(8)
     ag_c.step_three()
     ag_n.step_two()
+    tick(9)
     ag_c.step_four()
+    ag_n.step_three()
     ag_c.step_five()
-    spread[5].step_four()
-
     out_low = cb[mine]
     cot = out_low.astype(F32)
     acts, up_grads = [], []
@@ -727,7 +726,11 @@
     dstat_b[0] = lse
     dstat_b[1] = delta
     to_holders(d_pairs)
-    ag_n.step_three()
+    for r in range(ranks):
+        olr[token_rows(f, r % CORES, r // CORES)] = cb[example_of(r)]
+    across_o = Across(olr, 0)
+    across_n = Across(nb, 1)
+    across_o.start()
 
     down = jnp.zeros((SUFFIX, D), F32)
     for j in range(4):
@@ -739,7 +742,7 @@
     ob[me, 0:SUFFIX] = (after_cross + down).astype(BF16)
 
     def unit_device(h):
-        return CORES * h if h < HALF_UNITS else CORES * (h - HALF_UNITS) + 1
+        return CORES * (h + 1) if h < HALF_UNITS else CORES * (h - HALF_UNITS + 1) + 1
 
     unit_items = []
 
@@ -762,11 +765,10 @@
         unit_items.append((h, to))
 
     ag_n.step_four()
+    ag_n.step_five()
+    across_n.start()
     push_unit(HALF_UNITS + 4, cm, cross_low[:, 0:PIECE])
     push_unit(HALF_UNITS + 5, cm, cross_low[:, PIECE:])
-
-    for r in range(ranks):
-        olr[r * SUFFIX : (r + 1) * SUFFIX] = cb[example_of(r)]
 
     at_holders(d_pairs)
 
@@ -789,46 +791,6 @@
         for n in range(SLOTS):
             dqsend[n, :, sl] = dq[n * SUFFIX : (n + 1) * SUFFIX]
     to_owners(dq_pairs)
-
-    ag_n.step_five()
-    rows_step = 128
-    steps = ranks * SUFFIX // rows_step
-
-    @pl.when(c == 0)
-    def _():
-        lane = pl.multiple_of(LANE_FI + PIECE * chip, 128)
-        row = pl.multiple_of(lax.div(chip, 4) * half_rows, 128)
-        lane_o = pl.multiple_of(LANE_FO + D * lax.rem(chip, 4), 128)
-
-        def one(i, carry):
-            at = pl.ds(pl.multiple_of(i * rows_step, rows_step), rows_step)
-            value, slope = gelu_parts(mm(nb[at], wb[:, pl.ds(lane, PIECE)]))
-            back = mm_nt(olr[at], wb[pl.ds(row, half_rows), pl.ds(lane_o, D)])
-            hb[0, at] = (back * slope).astype(BF16)
-            return carry
-
-        lax.fori_loop(0, steps, one, 0)
-        for col in range(columns):
-            fg[col] = mm_tn(nb[:, col * half_rows : (col + 1) * half_rows], hb[0])
-
-    @pl.when(c == 1)
-    def _():
-        side = pl.ds(pl.multiple_of(PIECE * lax.div(chip, 4), 128), PIECE)
-
-        def one(i, carry):
-            at = pl.ds(pl.multiple_of(i * rows_step, rows_step), rows_step)
-            for col in range(columns):
-                lane = pl.multiple_of(LANE_FI + col * 4 * half_rows + PIECE * lax.rem(chip, 4), 128)
-                value, slope = gelu_parts(mm(nb[at], wb[:, pl.ds(lane, PIECE)]))
-                hb[col, at] = value.astype(BF16)
-            return carry
-
-        lax.fori_loop(0, steps, one, 0)
-        for col in range(columns):
-            fg[col] = mm_tn(hb[col], olr[:, side])
-
-    fsend[...] = fg[other].astype(BF16)
-    f_item = push_y(fsend, frecv, 1)
 
     at_owners(dq_pairs)
     cqg = (dqbuf[0] + dqbuf[1] + dqbuf[2]).astype(BF16)
@@ -855,25 +817,11 @@
         push_unit(HALF_UNITS + 2 + h, n2, cqg[:, h * PIECE : (h + 1) * PIECE])
         push_unit(HALF_UNITS + h, sm, self_low[:, h * PIECE : (h + 1) * PIECE])
 
-    f_item.wait_recv()
-    f_lane = jnp.where(
-        c == 0, LANE_FI + PIECE * chip, LANE_FO + D * lax.rem(chip, 4) + PIECE * lax.div(chip, 4)
-    )
-    gb[:, pl.ds(pl.multiple_of(f_lane, 128), PIECE)] = (fg[f] + frecv[...].astype(F32)).astype(BF16)
-
     def gb_view(lane_of):
-        def view(zz, xx, cc, part):
-            low, size = part if part is not None else (0, PIECE)
-            return gb.at[:, pl.ds(pl.multiple_of(lane_of(zz * SIDE + xx, cc) + low, 128), size)]
+        def view(zz, xx, cc):
+            return gb.at[:, pl.ds(pl.multiple_of(lane_of(zz * SIDE + xx, cc), 128), PIECE)]
 
         return view
-
-    ag_f = Gather(
-        place,
-        gb_view(lambda n, cc: jnp.where(cc == 0, LANE_FI + PIECE * n, LANE_FO + D * lax.rem(n, 4) + PIECE * lax.div(n, 4))),
-        PIECE, sems, 3,
-    )
-    ag_f.step_one()
 
     n1_grad = jnp.zeros((SUFFIX, D), F32)
     for j in range(3):
@@ -891,18 +839,77 @@
         return carry
 
     lax.fori_loop(0, 6, kp_step, 0)
-    mate = (z * (SIDE * CORES) + x * CORES + (1 - c), f)
     kr_item = pltpu.make_async_remote_copy(
         src_ref=kp.at[pl.ds(pl.multiple_of((1 - c) * half_rows, 128), half_rows)], dst_ref=kr,
         send_sem=ksend.at[2 * chips], recv_sem=krecv.at[chips], device_id=mate, device_id_type=MESH,
     )
     kr_item.start()
 
-    ag_f.step_two()
-
-    has_unit = chip < HALF_UNITS
+    across_o.relay()
+    across_n.relay()
+    across_o.wait()
+    across_n.wait()
+
+    rows_step = 128
+    hidden = [col * 4 * half_rows + D * c for col in range(columns)]
+
+    def ffn_rows(first, last):
+        def one(i, carry):
+            at = pl.ds(pl.multiple_of(i * rows_step, rows_step), rows_step)
+            for col in range(columns):
+                lane = pl.multiple_of(LANE_FI + hidden[col], 128)
+                value, slope = gelu_parts(mm(nb[at], wb[:, pl.ds(lane, D)]))
+
+                @pl.when(f == col)
+                def _():
+                    ab[at] = value.astype(BF16)
+
+                back = []
+                for t in range(CORES):
+                    lane_o = pl.multiple_of(LANE_FO + D * (2 * c + t), 128)
+                    back.append(mm_nt(olr[at], wb[col * half_rows : (col + 1) * half_rows, pl.ds(lane_o, D)]))
+                hb[col, at] = (jnp.concatenate(back, axis=1) * slope).astype(BF16)
+            return carry
+
+        lax.fori_loop(first, last, one, 0)
+
+    own_lanes = pl.ds(pl.multiple_of(f * half_rows, 128), half_rows)
+
+    def ffn_in_sum(col):
+        lane = pl.multiple_of(LANE_FI + hidden[col], 128)
+        for part in range(0, D, PIECE):
+            total = mm_tn(nb[:, own_lanes], hb[col, :, part : part + PIECE])
+            gb[:, pl.ds(lane + part, PIECE)] = total.astype(BF16)
+
+    def ffn_out_sum(t):
+        lane = pl.multiple_of(LANE_FO + D * (2 * c + t), 128)
+        for part in range(0, D, PIECE):
+            total = mm_tn(ab[:, t * half_rows : (t + 1) * half_rows], olr[:, part : part + PIECE])
+            gb[:, pl.ds(lane + part, PIECE)] = total.astype(BF16)
+
+    f_items = []
+
+    def to_mate(lane, width):
+        ref = gb.at[:, pl.ds(pl.multiple_of(lane, 128), width)]
+        item = pltpu.make_async_remote_copy(
+            src_ref=ref, dst_ref=ref, send_sem=fsend.at[len(f_items)], recv_sem=frecv.at[len(f_items)],
+            device_id=mate, device_id_type=MESH,
+        )
+        item.start()
+        f_items.append(item)
+
+    ffn_rows(0, columns * ranks * SUFFIX // rows_step)
+    for col in range(columns):
+        ffn_in_sum(col)
+        to_mate(LANE_FI + hidden[col], D)
+    for t in range(CORES):
+        ffn_out_sum(t)
+    to_mate(LANE_FO + CORES * D * c, CORES * D)
+
+    has_unit = (chip >= 1) & (chip <= HALF_UNITS)
 
     def unit_lane(n, cc):
+        n = n - 1
         kind = lax.div(n, 2)
         base = jnp.where(kind == 0, LANE_SO, jnp.where(kind == 1, LANE_CQ, LANE_CO))
         return jnp.where(cc == 0, PIECE * n, base + PIECE * lax.rem(n, 2))
@@ -945,9 +952,10 @@
             item.wait_send()
 
     def has_block(zz, xx, cc):
-        return zz * SIDE + xx < HALF_UNITS
-
-    ag_u = Gather(place, gb_view(unit_lane), PIECE, sems, 4, has_block)
+        n = zz * SIDE + xx
+        return (n >= 1) & (n <= HALF_UNITS)
+
+    ag_u = Gather(place, gb_view(unit_lane), sems, 3, has_block)
     unit_sum(has_unit, 3)
 
     kr_item.wait_recv()
@@ -965,67 +973,79 @@
 
     unit_join(has_unit, 3)
     ag_u.step_one()
-    ag_f.step_three()
-    k_items = []
-
-    def k_copy(t, j, src):
-        return pltpu.make_async_remote_copy(
-            src_ref=src, dst_ref=cp.at[chip], send_sem=ksend.at[t * CORES + j], recv_sem=krecv.at[chip],
-            device_id=(t * CORES + j, f), device_id_type=MESH,
-        )
+    half_slabs = half_rows // SIDE
+    kx_item = pltpu.make_async_remote_copy(
+        src_ref=kc.at[pl.ds(pl.multiple_of((1 - x) * half_slabs, 16), half_slabs)], dst_ref=kx,
+        send_sem=ksend.at[2 * chips + 2], recv_sem=krecv.at[chips + 2],
+        device_id=(z * (SIDE * CORES) + (1 - x) * CORES + c, f), device_id_type=MESH,
+    )
 
     @pl.when(c == f)
     def _():
         ky_item.wait_recv()
         kc[...] = (kc[...].astype(F32) + ky[...].astype(F32)).astype(BF16)
-
-    for t in range(chips):
-        for j in range(CORES):
-            src = kc.at[pl.ds(t * slab, slab), pl.ds(j * D, D)]
-            here = (chip == t) & (c == j)
-
-            @pl.when((c == f) & here)
-            def _():
-                cp[chip] = kc[t * slab : (t + 1) * slab, j * D : (j + 1) * D]
-
-            @pl.when((c == f) & jnp.logical_not(here))
-            def _():
-                k_copy(t, j, src).start()
-
-            k_items.append((t, j, src, here))
+        kx_item.start()
 
     g_item.wait_recv()
     tb[me] = gmine[...] + gpeer[...]
     tell_g = Tell(tb, 1)
     tell_g.start()
-    ag_o = Gather(place, block_view(ob), D, sems, 5)
+    ag_o = Gather(place, block_view(ob), sems, 4)
     ag_o.step_one()
     ag_u.step_two()
-    ag_f.step_four()
+    k_items = []
+
+    def k_copy(t, j):
+        return pltpu.make_async_remote_copy(
+            src_ref=ks.at[pl.ds(t * slab, slab), pl.ds(j * D, D)], dst_ref=cp.at[z],
+            send_sem=ksend.at[t * CORES + j], recv_sem=krecv.at[z],
+            device_id=(t * (SIDE * CORES) + x * CORES + j, f), device_id_type=MESH,
+        )
+
+    @pl.when(c == f)
+    def _():
+        kx_item.wait_recv()
+        ks[...] = (
+            kc[pl.ds(pl.multiple_of(x * half_slabs, 16), half_slabs)].astype(F32) + kx[...].astype(F32)
+        ).astype(BF16)
+
+    for t in range(RING):
+        for j in range(CORES):
+            here = (z == t) & (c == j)
+
+            @pl.when((c == f) & here)
+            def _():
+                cp[z] = ks[t * slab : (t + 1) * slab, j * D : (j + 1) * D]
+
+            @pl.when((c == f) & jnp.logical_not(here))
+            def _():
+                k_copy(t, j).start()
+
+            k_items.append((t, j, here))
+
 
     def take_k(i, carry):
-        @pl.when((i != chip) | (c != f))
+        @pl.when((i != z) | (c != f))
         def _():
             pltpu.make_async_remote_copy(
-                src_ref=kc.at[pl.ds(0, slab), pl.ds(0, D)], dst_ref=cp.at[i], send_sem=ksend.at[0],
+                src_ref=ks.at[pl.ds(0, slab), pl.ds(0, D)], dst_ref=cp.at[i], send_sem=ksend.at[0],
                 recv_sem=krecv.at[i], device_id=mate, device_id_type=MESH,
             ).wait_recv()
 
         return carry
 
-    lax.fori_loop(0, chips, take_k, 0)
+    lax.fori_loop(0, RING, take_k, 0)
     total = cp[0].astype(F32)
-    for i in range(1, chips):
+    for i in range(1, RING):
         total = total + cp[i].astype(F32)
     k_lane = pl.multiple_of(LANE_CKV + c * D, 128)
-    gb[pl.ds(pl.multiple_of(chip * slab, 16), slab), pl.ds(k_lane, D)] = total.astype(BF16)
-
-    def kv_view(zz, xx, cc, part):
-        low, size = part if part is not None else (0, D)
-        row = pl.multiple_of((zz * SIDE + xx) * slab, 16)
-        return gb.at[pl.ds(row, slab), pl.ds(pl.multiple_of(LANE_CKV + cc * D + low, 128), size)]
-
-    ag_k = Gather(place, kv_view, D, sems, 6)
+    gb[pl.ds(pl.multiple_of(x * half_slabs + z * slab, 16), slab), pl.ds(k_lane, D)] = total.astype(BF16)
+
+    def kv_view(zz, xx, cc):
+        row = pl.multiple_of(xx * half_slabs + zz * slab, 16)
+        return gb.at[pl.ds(row, slab), pl.ds(pl.multiple_of(LANE_CKV + cc * D, 128), D)]
+
+    ag_k = Gather(place, kv_view, sems, 5)
     ag_k.step_one()
     ag_u.step_three()
     ag_o.step_two()
@@ -1055,12 +1075,18 @@
     for i in range(1, columns):
         own_gain = jnp.where(f == i, gains_all[:, i * half_rows : (i + 1) * half_rows], own_gain)
     gain_out_ref[...] = own_gain
-    ag_f.step_five()
     ag_o.step_five()
     out_ref[...] = ob[mine_rank, 0:SUFFIX].astype(F32)
     grad_ref[...] = ob[mine_rank, SUFFIX : 2 * SUFFIX].astype(F32)
     ag_k.step_five()
     ag_u.step_five()
+    for n, (lane, width) in enumerate(
+        [(LANE_FI + col * 4 * half_rows + D * (1 - c), D) for col in range(columns)] + [(LANE_FO + CORES * D * (1 - c), CORES * D)]
+    ):
+        ref = gb.at[:, pl.ds(pl.multiple_of(lane, 128), width)]
+        pltpu.make_async_remote_copy(
+            src_ref=ref, dst_ref=ref, send_sem=fsend.at[n], recv_sem=frecv.at[n], device_id=mate, device_id_type=MESH,
+        ).wait_recv()
     done = pltpu.make_async_copy(gb, weights_out_ref, load_sem.at[0])
     done.start()
 
@@ -1075,10 +1101,19 @@
                 src_ref=sb.at[h], dst_ref=rb.at[rows_of(me)], send_sem=usend.at[h],
                 recv_sem=urecv.at[0], device_id=(to, f), device_id_type=MESH,
             ).wait_send()
-    for t, j, src, here in k_items:
+    for t, j, here in k_items:
         @pl.when((c == f) & jnp.logical_not(here))
         def _():
-            k_copy(t, j, src).wait_send()
+            k_copy(t, j).wait_send()
+
+    @pl.when(c == f)
+    def _():
+        kx_item.wait_send()
+
+    across_o.finish()
+    across_n.finish()
+    for item in f_items:
+        item.wait_send()
     kr_item.wait_send()
 
     @pl.when(c != f)
@@ -1089,7 +1124,7 @@
         item.wait_send()
     tell_p.finish()
     tell_g.finish()
-    for item in [ag_x, *spread, ag_c, ag_n, ag_f, ag_u, ag_o, ag_k]:
+    for item in [ag_x, *spread, ag_c, ag_n, ag_u, ag_o, ag_k]:
         item.finish()
     done.wait()
 
@@ -1118,8 +1153,8 @@
         pltpu.VMEM((2 * HALF_UNITS, SUFFIX, D + PIECE), BF16),
         pltpu.VMEM((ranks, SUFFIX, D), F32),
         pltpu.VMEM((ranks, SUFFIX, D), BF16),
-        pltpu.VMEM((tokens, D), BF16),
-        pltpu.VMEM((tokens, D), BF16),
+        pltpu.VMEM((columns * tokens, D), BF16),
+        pltpu.VMEM((columns * tokens, D), BF16),
         pltpu.VMEM((ranks, 2 * SUFFIX, D), BF16),
         pltpu.VMEM((ranks, 8, D), F32),
         pltpu.VMEM((ranks, 8, 128), F32),
@@ -1131,11 +1166,11 @@
         pltpu.VMEM((half_rows, 2 * D), BF16),
         pltpu.VMEM((half_rows, 2 * D), BF16),
         pltpu.VMEM((half_rows, 2 * D), BF16),
-        pltpu.VMEM((chips, slab, D), BF16),
-        pltpu.VMEM((columns, tokens, PIECE), BF16),
-        pltpu.VMEM((columns, half_rows, PIECE), F32),
-        pltpu.VMEM((half_rows, PIECE), BF16),
-        pltpu.VMEM((half_rows, PIECE), BF16),
+        pltpu.VMEM((RING, slab, D), BF16),
+        pltpu.VMEM((half_rows // SIDE, 2 * D), BF16),
+        pltpu.VMEM((half_rows // SIDE, 2 * D), BF16),
+        pltpu.VMEM((columns, columns * tokens, D), BF16),
+        pltpu.VMEM((columns * tokens, D), BF16),
         pltpu.VMEM((columns, half_rows, PIECE), F32),
         pltpu.VMEM((half_rows, PIECE), BF16),
         pltpu.VMEM((half_rows, PIECE), BF16),
@@ -1154,20 +1189,24 @@
         pltpu.VMEM((8, D), F32),
         pltpu.VMEM((8, D), F32),
         dma((10,)),
-        dma((len(CHUNKS), 16)),
-        dma((len(CHUNKS), 16)),
-        dma((7, 16)),
-        dma((7, 16)),
+        dma((len(CHUNKS), 30)),
+        dma((len(CHUNKS), 18)),
+        dma((6, 29)),
+        dma((6, 16)),
         dma((2, ranks)),
         dma((2, ranks)),
+        dma((2, 2)),
+        dma((2, 2)),
+        dma((3,)),
+        dma((3,)),
         dma((4,)),
         dma((4,)),
         dma((6, SLOTS)),
         dma((6, SLOTS)),
         dma((2 * HALF_UNITS,)),
         dma((ranks,)),
-        dma((2 * chips + 2,)),
-        dma((chips + 2,)),
+        dma((2 * chips + 3,)),
+        dma((chips + 3,)),
     ]
     out, grad, memgrad, gain_grads, weight_grads = pl.pallas_call(
         partial(layer_kernel, ranks, columns),
@@ -1182,7 +1221,7 @@
         out_specs=(vm, vm, vm, vm, hbm),
         scratch_shapes=scratch,
         compiler_params=pltpu.CompilerParams(
-            collective_id=0, has_side_effects=True, vmem_limit_bytes=62 * 2**20
+            collective_id=0, has_side_effects=True, vmem_limit_bytes=63 * 2**20
         ),
         name="layer",
     )(

time: 273 us -> 222 us (0.81)
  the two profiles are of different devices: /device:TPU:19 before, /device:TPU:3 now
where the time goes in v3:
time: 222 us; the launch traced here: 220 us
  Pallas kernels  196 us (88%)
  other arithmetic  14.3 us (6%)
  local copies, waits for them, and re-layouts  8.59 us (4%)
    pallas_call x1, Pallas kernels, fused_body(): pl.pallas_call(partial(layer_kernel, ranks, columns), out_shape=(jax.Shap...  196 us
    convert_element_type x3, other arithmetic, lanes(): return weight_grads[:, low:low + width].astype(F32)  9.23 us
    unnamed x9, local copies, waits for them, and re-layouts  5.12 us

profile of v3, /device:TPU:3, one launch (start us, length us, event | category | flops | bytes accessed | tf_op | source)
XLA Modules:
  0.0 220.2 jit_solution(5850263012188135908)
XLA Ops:
  1.3 0.7 stack.12
  2.0 0.7 stack.13
  2.7 0.7 stack.14
  3.3 0.6 fusion.5.gains_ref
  3.9 196.0 %layer.1 = (f32[32,768]{1,0:T(8,128)}, f32[32,768]{1,0:T(8,128)}, f32[418,768]{1,0:T(8,128)}, f32[8,384]{1,0:T(8,128)}, bf16[384,12288]{1,0:T(8,128)(2,1)}) custom-call(f32[32,768]{1,0:T(8,128)} %bitcast.8, f32[32,768]{1,0:T(8,128)} %bitcast.9, bf16[418,768]{1,0:T(8,128)(2,1)} %bitcast.7, s32[1,16]{1,0:T(1,128)} %res_ref.1, s32[1,1]{1,0:T(1,128)S(6)} %copy.31.pre_ref, ...), custom_call_target="tpu_custom_call" | custom-call | tf_op jit(solution)/shard_map/layer/pallas_call | solution.py:1211
  200.0 1.4 slice_reduce_fusion
  201.4 0.0 copy-start
  201.4 3.8 %copy.28 = f32[1,418,768]{2,0,1:T(1,128)} copy(f32[1,418,768]{2,1,0:T(8,128)} %bitcast.6) | data formatting | bytes 2568192
  205.2 3.0 %slice_convert_fusion.2 = f32[384,1536]{1,0:T(8,128)} fusion(bf16[384,12288]{1,0:T(8,128)(2,1)} %get-tuple-element.22), kind=kLoop, calls=%fused_computation.3 | loop fusion | flops 589824 | bytes 3538944 | tf_op jit(solution)/shard_map/convert_element_type | solution.py:1233
  208.2 3.5 %slice_convert_fusion.1 = f32[384,2304]{1,0:T(8,128)} fusion(bf16[384,12288]{1,0:T(8,128)(2,1)} %get-tuple-element.22), kind=kLoop, calls=%fused_computation.2 | loop fusion | flops 884736 | bytes 5308416 | tf_op jit(solution)/shard_map/convert_element_type | solution.py:1233
  211.7 0.0 copy-done
  211.7 2.8 %slice_convert_fusion = f32[384,3072]{1,0:T(8,128)} fusion(bf16[384,12288]{1,0:T(8,128)(2,1)S(1)} %copy-done), kind=kLoop, calls=%fused_computation.1 | loop fusion | flops 1179648 | bytes 7077888 | tf_op jit(solution)/shard_map/convert_element_type | solution.py:1233
  214.4 1.9 fusion.6
  216.3 0.0 copy-start.2
  216.3 0.0 copy-start.1
  216.3 2.5 %maximum_convert_fusion = f32[1536,768]{1,0:T(8,128)} fusion(bf16[384,768]{1,0:T(8,128)(2,1)S(1)} %get-tuple-element.40, bf16[384,768]{1,0:T(8,128)(2,1)S(1)} %get-tuple-element.41, bf16[384,768]{1,0:T(8,128)(2,1)S(1)} %get-tuple-element.42, bf16[384,768]{1,0:T(8,128)(2,1)S(1)} %get-tuple-element.39), kind=kLoop, calls=%fused_computation | loop fusion | flops 9437184 | bytes 7077888 | tf_op jit(solution)/shard_map/concatenate | solution.py:1235
  218.9 0.0 copy-done.2
  218.9 0.6 copy.32
  219.5 0.0 copy-done.1
  219.5 0.6 copy.33
Async XLA Ops:
  201.4 10.3 %copy-start = (bf16[384,12288]{1,0:T(8,128)(2,1)S(1)}, bf16[384,12288]{1,0:T(8,128)(2,1)}, u32[]{:S(2)}) copy-start(bf16[384,12288]{1,0:T(8,128)(2,1)} %get-tuple-element.22) | copy-start | bytes 28311556
  216.3 2.6 %copy-start.2 = (f32[32,768]{1,0:T(8,128)S(1)}, f32[32,768]{1,0:T(8,128)}, u32[]{:S(2)}) copy-start(f32[32,768]{1,0:T(8,128)} %get-tuple-element.18) | copy-start | bytes 294916
  216.3 3.2 %copy-start.1 = (f32[32,768]{1,0:T(8,128)S(1)}, f32[32,768]{1,0:T(8,128)}, u32[]{:S(2)}) copy-start(f32[32,768]{1,0:T(8,128)} %get-tuple-element.19) | copy-start | bytes 294916

commit v4 on v3

--- a/solution.py
+++ b/solution.py
@@ -63,16 +63,18 @@
 
 
 class Gather:
-    def __init__(self, place, view, sems, at, has=None):
+    def __init__(self, place, view, bulk, sems, at, has=None):
         self.z, self.x, self.c, self.f = place
-        self.view = view
+        self.view, self.bulk = view, bulk
         self.send, self.recv = sems
         self.at = at
         self.has = has
         self.sent = []
 
-    def copy(self, block, target, into, index):
-        ref = self.view(*block)
+    def place_at(self, k):
+        return lax.rem(self.z + k + RING, RING)
+
+    def copy(self, ref, target, into, index):
         z, x, c = target
         return pltpu.make_async_remote_copy(
             src_ref=ref,
@@ -83,38 +85,33 @@
             device_id_type=MESH,
         )
 
-    def place_at(self, k):
-        return lax.rem(self.z + k + RING, RING)
-
     def holds(self, block, cond):
         return cond if self.has is None else cond & self.has(*block)
 
     def go(self, block, target, into, cond):
-        item = self.copy(block, target, into, len(self.sent))
+        item = self.copy(self.view(*block), target, into, len(self.sent))
         cond = self.holds(block, cond)
         pl.when(cond)(item.start)
         self.sent.append((cond, item))
 
     def wait(self, block, into, cond):
-        pl.when(self.holds(block, cond))(self.copy(block, (self.z, 1 - self.x, self.c), into, 0).wait_recv)
+        item = self.copy(self.view(*block), (self.z, 1 - self.x, self.c), into, 0)
+        pl.when(self.holds(block, cond))(item.wait_recv)
 
     def line(self, block, up, down, cond):
         z, x, c = self.z, self.x, self.c
-        at = block[0]
         if up:
-            self.go(block, (self.place_at(1), x, c), at, cond & (z < RING - 1))
+            self.go(block, (self.place_at(1), x, c), block[0], cond & (z < RING - 1))
         if down:
-            self.go(block, (self.place_at(-1), x, c), at, cond & (z > 0))
-
-    def spread(self, block, cond):
-        z, x, c = self.z, self.x, self.c
-        self.go(block, (z, 1 - x, c), RING + block[0], cond)
-        self.go(block, (z, x, 1 - c), 2 * RING + block[0], cond)
+            self.go(block, (self.place_at(-1), x, c), block[0], cond & (z > 0))
+
+    def across(self, block, cond):
+        self.go(block, (self.z, 1 - self.x, self.c), RING + block[0], cond)
 
     def step_one(self):
         own = (self.z, self.x, self.c)
         self.line(own, True, True, self.z >= 0)
-        self.spread(own, self.z >= 0)
+        self.across(own, self.z >= 0)
 
     def arrive(self, k):
         low, high = (self.place_at(-k), self.x, self.c), (self.place_at(k), self.x, self.c)
@@ -122,22 +119,19 @@
         self.line(low, True, False, self.z >= k)
         self.wait(high, high[0], self.z < RING - k)
         self.line(high, False, True, self.z < RING - k)
-        self.spread(low, self.z >= k)
-        self.spread(high, self.z < RING - k)
+        self.across(low, self.z >= k)
+        self.across(high, self.z < RING - k)
 
     def side(self, k):
-        z, x, c = self.z, self.x, self.c
-        for at, cond in ((self.place_at(-k), z >= k), (self.place_at(k), z < RING - k))[: 1 if k == 0 else 2]:
-            block = (at, 1 - x, c)
-            self.wait(block, RING + at, cond)
-            self.go(block, (z, x, 1 - c), 3 * RING + at, cond)
+        for at, cond in ((self.place_at(-k), self.z >= k), (self.place_at(k), self.z < RING - k))[: 1 if k == 0 else 2]:
+            self.wait((at, 1 - self.x, self.c), RING + at, cond)
 
     def step_two(self):
         self.arrive(1)
-        self.side(0)
 
     def step_three(self):
         self.arrive(2)
+        self.side(0)
         self.side(1)
 
     def step_four(self):
@@ -146,19 +140,24 @@
 
     def step_five(self):
         self.side(3)
-        always = self.z >= 0
-        for at in range(RING):
-            self.wait((at, self.x, 1 - self.c), 2 * RING + at, always)
-            self.wait((at, 1 - self.x, 1 - self.c), 3 * RING + at, always)
+        item = self.copy(self.bulk(self.c), (self.z, self.x, 1 - self.c), 2 * RING, len(self.sent))
+        item.start()
+        self.sent.append((None, item))
+
+    def step_six(self):
+        self.copy(self.bulk(1 - self.c), (self.z, self.x, 1 - self.c), 2 * RING, 0).wait_recv()
 
     def finish(self):
         for cond, item in self.sent:
-            pl.when(cond)(item.wait_send)
+            if cond is None:
+                item.wait_send()
+            else:
+                pl.when(cond)(item.wait_send)
 
 
 class Spread(Gather):
-    def __init__(self, place, theirs, mine, sems, at):
-        super().__init__(place, theirs, sems, at)
+    def __init__(self, place, theirs, mine, bulk, sems, at):
+        super().__init__(place, theirs, bulk, sems, at)
         self.mine = mine
         self.pushed = []
 
@@ -167,24 +166,25 @@
         for n, block in enumerate(((z, x, c), (z, 1 - x, c))):
             ref = self.mine(*block)
             item = pltpu.make_async_remote_copy(
-                src_ref=ref, dst_ref=ref, send_sem=self.send.at[self.at, 28 + n], recv_sem=self.recv.at[self.at, 16 + n],
+                src_ref=ref, dst_ref=ref, send_sem=self.send.at[self.at, 15 + n], recv_sem=self.recv.at[self.at, 9 + n],
                 device_id=(z * (SIDE * CORES) + x * CORES + c, 1 - self.f), device_id_type=MESH,
             )
             item.start()
             self.pushed.append(item)
 
     def step_one(self):
-        z, x, c = self.z, self.x, self.c
-        always = z >= 0
-        own, side = (z, x, c), (z, 1 - x, c)
-        self.wait(own, 16, always)
+        always = self.z >= 0
+        own = (self.z, self.x, self.c)
+        self.wait(own, 9, always)
         self.line(own, True, True, always)
-        self.go(own, (z, x, 1 - c), 2 * RING + z, always)
-        self.wait(side, 17, always)
-        self.go(side, (z, x, 1 - c), 3 * RING + z, always)
-
-    def step_two(self):
-        self.arrive(1)
+
+    def step_three(self):
+        self.arrive(2)
+        self.side(1)
+
+    def step_five(self):
+        self.wait((self.z, 1 - self.x, self.c), 10, self.z >= 0)
+        super().step_five()
 
     def finish(self):
         super().finish()
@@ -229,9 +229,9 @@
 
 SLOTS = 3
 UNITS = 16
-LANE_QKV, LANE_SO, LANE_CQ, LANE_CKV, LANE_CO, LANE_FI, LANE_FO = 0, 2304, 3072, 3840, 5376, 6144, 9216
-CHUNKS = ((0, 2304), (2304, 1536), (3840, 1536), (5376, 2304), (7680, 2304), (9984, 2304))
-LOADS_BY_CHUNK = ((0,), (1, 2), (3,), (4, 5), (6,), (7, 8, 9))
+LANE_QKV, LANE_SO, LANE_CQ, LANE_CO, LANE_CKV, LANE_FI, LANE_FO = 0, 2304, 3072, 3840, 4608, 6144, 9216
+CHUNKS = ((0, 2304), (2304, 2304), (4608, 1536), (6144, 2048), (8192, 2048), (10240, 2048))
+LOADS_BY_CHUNK = ((0,), (1, 2, 3), (4,), (5,), (6, 7), (8, 9))
 PIECE = 384
 HALF_UNITS = 6
 
@@ -279,8 +279,8 @@
     load(qkv_ref, LANE_QKV, 3 * D)
     load(so_ref, LANE_SO, D)
     load(cq_ref, LANE_CQ, D)
+    load(co_ref, LANE_CO, D)
     load(ckv_ref, LANE_CKV, 2 * D)
-    load(co_ref, LANE_CO, D)
     load(fi_ref, LANE_FI, 4 * D)
     for j in range(4):
         load(fo_ref.at[pl.ds(j * half_rows, half_rows)], LANE_FO + D * j, D)
@@ -297,9 +297,13 @@
     def rows_of(device):
         return pl.ds(pl.multiple_of(device * SUFFIX, SUFFIX), SUFFIX)
 
-    xb[me] = x_ref[...]
-    cb[me] = cot_ref[...].astype(BF16)
-    pb[me] = jnp.full((8, 128), pre_ref[0, 0].astype(F32), F32)
+    def slot_of(device):
+        return lax.rem(device, CORES) * chips + lax.div(device, CORES)
+
+    my_slot = slot_of(me)
+    xb[my_slot] = x_ref[...]
+    cb[my_slot] = cot_ref[...].astype(BF16)
+    pb[my_slot] = jnp.full((8, 128), pre_ref[0, 0].astype(F32), F32)
     gainb[f] = gains_ref[...]
 
     barrier = pltpu.get_barrier_semaphore()
@@ -330,7 +334,7 @@
 
         def copy(self, source, index, to):
             return pltpu.make_async_remote_copy(
-                src_ref=self.ref.at[source], dst_ref=self.ref.at[source], send_sem=bsend.at[self.at, index],
+                src_ref=self.ref.at[slot_of(source)], dst_ref=self.ref.at[slot_of(source)], send_sem=bsend.at[self.at, index],
                 recv_sem=brecv.at[self.at, source], device_id=(to, f), device_id_type=MESH,
             )
 
@@ -368,9 +372,12 @@
 
     def block_view(ref):
         def view(zz, xx, cc):
-            return ref.at[zz * (SIDE * CORES) + xx * CORES + cc]
+            return ref.at[cc * chips + zz * SIDE + xx]
 
         return view
+
+    def block_bulk(ref):
+        return lambda cc: ref.at[pl.ds(cc * chips, chips)]
 
     def token_rows(col, cc, at):
         return pl.ds(pl.multiple_of(((col * CORES + cc) * chips + at) * SUFFIX, SUFFIX), SUFFIX)
@@ -380,6 +387,15 @@
             return ref.at[token_rows(f, cc, zz * SIDE + xx)]
 
         return view
+
+    def token_bulk(ref):
+        rows = chips * SUFFIX
+        return lambda cc: ref.at[pl.ds(pl.multiple_of((f * CORES + cc) * rows, rows), rows)]
+
+    def chunk_bulk(first, width):
+        half = width // CORES
+        rows = pl.ds(pl.multiple_of(other * half_rows, 128), half_rows)
+        return lambda cc: wb.at[rows, pl.ds(pl.multiple_of(first + cc * half, 128), half)]
 
     plane = pl.ds(pl.multiple_of((f * CORES + c) * chips * SUFFIX, SUFFIX), chips * SUFFIX)
     plane_in = pl.ds(pl.multiple_of((other * CORES + c) * chips * SUFFIX, SUFFIX), chips * SUFFIX)
@@ -411,12 +427,12 @@
             self.copy(plane_in, 1, mate).wait_send()
 
     sems = (gsend, grecv)
-    ag_x = Gather(place, block_view(xb), sems, 0)
-    ag_c = Gather(place, block_view(cb), sems, 1)
-    ag_n = Gather(place, token_view(nb), sems, 2)
+    ag_x = Gather(place, block_view(xb), block_bulk(xb), sems, 0)
+    ag_c = Gather(place, block_view(cb), block_bulk(cb), sems, 1)
+    ag_n = Gather(place, token_view(nb), token_bulk(nb), sems, 2)
     tell_p = Tell(pb, 0)
     spread = [
-        Spread(place, slab_view(first, width, other), slab_view(first, width, f), (wsend, wrecv), n)
+        Spread(place, slab_view(first, width, other), slab_view(first, width, f), chunk_bulk(first, width), (wsend, wrecv), n)
         for n, (first, width) in enumerate(CHUNKS)
     ]
 
@@ -440,12 +456,17 @@
 
     ag_x.step_two()
     tick(0)
+    ag_c.step_one()
     ag_x.step_three()
     tick(1)
+    ag_c.step_two()
     ag_x.step_four()
     tick(2)
+    ag_c.step_three()
     ag_x.step_five()
+    ag_x.step_six()
     tick(3)
+    ag_c.step_four()
     gain_item.wait_recv()
 
     memp[0:own_rows] = mem_ref[...]
@@ -461,13 +482,23 @@
         mine_rank = jnp.where(me == i, spot, mine_rank)
         before_large = before_large + group
 
+    slots = [(i % CORES) * chips + i // CORES for i in range(ranks)]
+
     def example_of(rank):
         found = jnp.int32(0)
         for i in range(ranks):
-            found = jnp.where(positions[i] == rank, i, found)
+            found = jnp.where(positions[i] == rank, slots[i], found)
         return found
 
-    gain = [jnp.concatenate([gainb[i, n : n + 1] for i in range(columns)], axis=1) for n in range(3)]
+    out_slot = jnp.int32(0)
+    for i in range(ranks):
+        out_slot = jnp.where(mine_rank == i, slots[i], out_slot)
+
+    tiles = half_rows // 128
+    gain = [
+        jnp.concatenate([gainb[i, tiles * n + j : tiles * n + j + 1] for i in range(columns) for j in range(tiles)], axis=1)
+        for n in range(3)
+    ]
 
     mine = example_of(me)
     resid = xb[mine]
@@ -489,6 +520,8 @@
         return total
 
     tick(4)
+    ag_c.step_five()
+    spread[0].step_six()
     q = mm(n1, wb[:, 0:D]).astype(BF16)
     k = mm(n1, wb[:, D : 2 * D]).astype(BF16)
     v = mm(n1, wb[:, 2 * D : 3 * D]).astype(BF16)
@@ -510,6 +543,8 @@
     sm = jnp.concatenate(mixed, axis=1).astype(BF16)
 
     tick(5)
+    ag_c.step_six()
+    spread[1].step_six()
     after_self = resid + mm(sm, wb[:, LANE_SO : LANE_SO + D])
     hat_two, rs_two = normed(after_self)
     n2 = (hat_two * gain[1]).astype(BF16)
@@ -601,7 +636,14 @@
     to_holders(q_pairs)
 
     tick(6)
-    ag_c.step_one()
+    spread[2].step_six()
+
+    for r in range(ranks):
+        olr[token_rows(f, r % CORES, r // CORES)] = cb[example_of(r)]
+    across_o = Across(olr, 0)
+    across_n = Across(nb, 1)
+    across_o.start()
+
 
     def kv_step(i, carry):
         lane = pl.multiple_of(i * 256, 256)
@@ -654,7 +696,6 @@
     to_owners(o_pairs)
 
     tick(7)
-    ag_c.step_two()
     at_owners(o_pairs)
 
     def expand(compact):
@@ -682,12 +723,9 @@
     ag_n.step_one()
 
     tick(8)
-    ag_c.step_three()
-    ag_n.step_two()
     tick(9)
-    ag_c.step_four()
-    ag_n.step_three()
-    ag_c.step_five()
+    for n in (3, 4, 5):
+        spread[n].step_six()
     out_low = cb[mine]
     cot = out_low.astype(F32)
     acts, up_grads = [], []
@@ -710,6 +748,7 @@
         n3_grad = n3_grad + mm_nt(part, weight)
     act = jnp.concatenate(acts, axis=1)
 
+    ag_n.step_two()
     part, ffn_gain_grad = norm_back(n3_grad, hat_three, rs_three, gain[2])
     cross_res = cot + part
     cross_low = cross_res.astype(BF16)
@@ -726,12 +765,6 @@
     dstat_b[0] = lse
     dstat_b[1] = delta
     to_holders(d_pairs)
-    for r in range(ranks):
-        olr[token_rows(f, r % CORES, r // CORES)] = cb[example_of(r)]
-    across_o = Across(olr, 0)
-    across_n = Across(nb, 1)
-    across_o.start()
-
     down = jnp.zeros((SUFFIX, D), F32)
     for j in range(4):
         lhs = jnp.concatenate(
@@ -739,7 +772,10 @@
             axis=1,
         )
         down = down + mm(lhs, wb[:, LANE_FO + D * j : LANE_FO + D * (j + 1)])
-    ob[me, 0:SUFFIX] = (after_cross + down).astype(BF16)
+    ob[0, my_slot] = (after_cross + down).astype(BF16)
+    ag_out = Gather(place, block_view(ob.at[0]), block_bulk(ob.at[0]), sems, 4)
+    ag_out.step_one()
+    ag_n.step_three()
 
     def unit_device(h):
         return CORES * (h + 1) if h < HALF_UNITS else CORES * (h - HALF_UNITS + 1) + 1
@@ -764,9 +800,6 @@
 
         unit_items.append((h, to))
 
-    ag_n.step_four()
-    ag_n.step_five()
-    across_n.start()
     push_unit(HALF_UNITS + 4, cm, cross_low[:, 0:PIECE])
     push_unit(HALF_UNITS + 5, cm, cross_low[:, PIECE:])
 
@@ -789,11 +822,27 @@
         kvg[:, sl] = mm_tn(ds, q4).astype(BF16)
         dq = unstack(mm(ds, kg)) * scale
         for n in range(SLOTS):
-            dqsend[n, :, sl] = dq[n * SUFFIX : (n + 1) * SUFFIX]
+            dqsend[n, :, sl] = dq[n * SUFFIX : (n + 1) * SUFFIX].astype(BF16)
     to_owners(dq_pairs)
-
+    ag_n.step_four()
+    def kp_step(i, carry):
+        lane = pl.multiple_of(i * 256, 256)
+        kp[:, pl.ds(lane, 256)] = mm_tn(memp[...], kvg[:, pl.ds(lane, 256)]).astype(BF16)
+        return carry
+
+    lax.fori_loop(0, 6, kp_step, 0)
+    kr_item = pltpu.make_async_remote_copy(
+        src_ref=kp.at[pl.ds(pl.multiple_of((1 - c) * half_rows, 128), half_rows)], dst_ref=kr,
+        send_sem=ksend.at[2 * chips], recv_sem=krecv.at[chips], device_id=mate, device_id_type=MESH,
+    )
+    kr_item.start()
+
+    ag_n.step_five()
+    across_n.start()
+    across_o.relay()
+    ag_out.step_two()
     at_owners(dq_pairs)
-    cqg = (dqbuf[0] + dqbuf[1] + dqbuf[2]).astype(BF16)
+    cqg = (dqbuf[0].astype(F32) + dqbuf[1].astype(F32) + dqbuf[2].astype(F32)).astype(BF16)
     n2_grad = mm_nt(cqg, wb[:, LANE_CQ : LANE_CQ + D])
     part, cross_gain_grad = norm_back(n2_grad, hat_two, rs_two, gain[1])
     self_res = cross_res + part
@@ -827,26 +876,32 @@
     for j in range(3):
         n1_grad = n1_grad + mm_nt(packed_grad[j], wb[:, D * j : D * (j + 1)])
     part, self_gain_grad = norm_back(n1_grad, hat_one, rs_one, gain[0])
-    ob[me, SUFFIX : 2 * SUFFIX] = (self_res + part).astype(BF16)
+    ob[1, my_slot] = (self_res + part).astype(BF16)
+    ag_grad = Gather(place, block_view(ob.at[1]), block_bulk(ob.at[1]), sems, 6)
     gmine[...] = jnp.concatenate(
         [self_gain_grad, cross_gain_grad, ffn_gain_grad, jnp.zeros((5, D), F32)], axis=0
     )
-    g_item = push_y(gmine, gpeer, 2)
-
-    def kp_step(i, carry):
-        lane = pl.multiple_of(i * 256, 256)
-        kp[:, pl.ds(lane, 256)] = mm_tn(memp[...], kvg[:, pl.ds(lane, 256)]).astype(BF16)
-        return carry
-
-    lax.fori_loop(0, 6, kp_step, 0)
-    kr_item = pltpu.make_async_remote_copy(
-        src_ref=kp.at[pl.ds(pl.multiple_of((1 - c) * half_rows, 128), half_rows)], dst_ref=kr,
-        send_sem=ksend.at[2 * chips], recv_sem=krecv.at[chips], device_id=mate, device_id_type=MESH,
-    )
-    kr_item.start()
-
-    across_o.relay()
+    tb[my_slot] = gmine[...]
+    tell_g = Tell(tb, 1)
+    tell_g.start()
+    kr_item.wait_recv()
+    kc[...] = (
+        kp[pl.ds(pl.multiple_of(c * half_rows, 128), half_rows)].astype(F32) + kr[...].astype(F32)
+    ).astype(BF16)
+    ky_item = pltpu.make_async_remote_copy(
+        src_ref=kc, dst_ref=ky, send_sem=ksend.at[2 * chips + 1], recv_sem=krecv.at[chips + 1],
+        device_id=(me, other), device_id_type=MESH,
+    )
+
+    @pl.when(c != f)
+    def _():
+        ky_item.start()
+
+    ag_grad.step_one()
+    ag_out.step_three()
+
     across_n.relay()
+    ag_n.step_six()
     across_o.wait()
     across_n.wait()
 
@@ -898,23 +953,10 @@
         item.start()
         f_items.append(item)
 
-    ffn_rows(0, columns * ranks * SUFFIX // rows_step)
-    for col in range(columns):
-        ffn_in_sum(col)
-        to_mate(LANE_FI + hidden[col], D)
-    for t in range(CORES):
-        ffn_out_sum(t)
-    to_mate(LANE_FO + CORES * D * c, CORES * D)
-
     has_unit = (chip >= 1) & (chip <= HALF_UNITS)
 
     def unit_lane(n, cc):
-        n = n - 1
-        kind = lax.div(n, 2)
-        base = jnp.where(kind == 0, LANE_SO, jnp.where(kind == 1, LANE_CQ, LANE_CO))
-        return jnp.where(cc == 0, PIECE * n, base + PIECE * lax.rem(n, 2))
-
-    u_items = []
+        return PIECE * (n - 1) + HALF_UNITS * PIECE * cc
 
     def unit_sum(pred, at):
         @pl.when(pred)
@@ -955,24 +997,12 @@
         n = zz * SIDE + xx
         return (n >= 1) & (n <= HALF_UNITS)
 
-    ag_u = Gather(place, gb_view(unit_lane), sems, 3, has_block)
-    unit_sum(has_unit, 3)
-
-    kr_item.wait_recv()
-    kc[...] = (
-        kp[pl.ds(pl.multiple_of(c * half_rows, 128), half_rows)].astype(F32) + kr[...].astype(F32)
-    ).astype(BF16)
-    ky_item = pltpu.make_async_remote_copy(
-        src_ref=kc, dst_ref=ky, send_sem=ksend.at[2 * chips + 1], recv_sem=krecv.at[chips + 1],
-        device_id=(me, other), device_id_type=MESH,
-    )
-
-    @pl.when(c != f)
-    def _():
-        ky_item.start()
-
-    unit_join(has_unit, 3)
-    ag_u.step_one()
+    def unit_bulk(cc):
+        return gb.at[:, pl.ds(pl.multiple_of(HALF_UNITS * PIECE * cc, 128), HALF_UNITS * PIECE)]
+
+    ag_u = Gather(place, gb_view(unit_lane), unit_bulk, sems, 3, has_block)
+
+    ffn_rows(0, 4)
     half_slabs = half_rows // SIDE
     kx_item = pltpu.make_async_remote_copy(
         src_ref=kc.at[pl.ds(pl.multiple_of((1 - x) * half_slabs, 16), half_slabs)], dst_ref=kx,
@@ -986,13 +1016,9 @@
         kc[...] = (kc[...].astype(F32) + ky[...].astype(F32)).astype(BF16)
         kx_item.start()
 
-    g_item.wait_recv()
-    tb[me] = gmine[...] + gpeer[...]
-    tell_g = Tell(tb, 1)
-    tell_g.start()
-    ag_o = Gather(place, block_view(ob), sems, 4)
-    ag_o.step_one()
-    ag_u.step_two()
+    ffn_rows(4, 6)
+    unit_sum(has_unit, 3)
+    ffn_rows(6, 8)
     k_items = []
 
     def k_copy(t, j):
@@ -1023,6 +1049,15 @@
 
             k_items.append((t, j, here))
 
+    unit_join(has_unit, 3)
+    ag_u.step_one()
+    ag_grad.step_two()
+    ag_out.step_four()
+    ffn_in_sum(0)
+    to_mate(LANE_FI + hidden[0], D)
+    ffn_in_sum(1)
+    to_mate(LANE_FI + hidden[1], D)
+    ag_u.step_two()
 
     def take_k(i, carry):
         @pl.when((i != z) | (c != f))
@@ -1045,11 +1080,17 @@
         row = pl.multiple_of(xx * half_slabs + zz * slab, 16)
         return gb.at[pl.ds(row, slab), pl.ds(pl.multiple_of(LANE_CKV + cc * D, 128), D)]
 
-    ag_k = Gather(place, kv_view, sems, 5)
+    ag_k = Gather(place, kv_view, lambda cc: gb.at[:, pl.ds(pl.multiple_of(LANE_CKV + cc * D, 128), D)], sems, 5)
     ag_k.step_one()
+    ag_grad.step_three()
+    ag_out.step_five()
+    ffn_out_sum(0)
+    ffn_out_sum(1)
+    to_mate(LANE_FO + CORES * D * c, CORES * D)
     ag_u.step_three()
-    ag_o.step_two()
     ag_k.step_two()
+    ag_grad.step_four()
+    ag_out.step_six()
 
     def mg_step(i, carry):
         row = pl.multiple_of(i * 128, 128)
@@ -1062,24 +1103,15 @@
         tail = mm_nt(kvg[full * 128 : (full + 1) * 128], wb[:, LANE_CKV : LANE_CKV + 2 * D])
         memgrad_ref[full * 128 : own_rows] = tail[0 : own_rows - full * 128]
 
+
     ag_u.step_four()
-    ag_o.step_three()
     ag_k.step_three()
-    ag_o.step_four()
-    ag_k.step_four()
+    ag_grad.step_five()
     tell_g.wait()
-    gains_all = tb[0]
+    gmine[...] = tb[0]
     for i in range(1, ranks):
-        gains_all = gains_all + tb[i]
-    own_gain = gains_all[:, 0:half_rows]
-    for i in range(1, columns):
-        own_gain = jnp.where(f == i, gains_all[:, i * half_rows : (i + 1) * half_rows], own_gain)
-    gain_out_ref[...] = own_gain
-    ag_o.step_five()
-    out_ref[...] = ob[mine_rank, 0:SUFFIX].astype(F32)
-    grad_ref[...] = ob[mine_rank, SUFFIX : 2 * SUFFIX].astype(F32)
-    ag_k.step_five()
-    ag_u.step_five()
+        gmine[...] += tb[i]
+    g_item = push_y(gmine, gpeer, 2)
     for n, (lane, width) in enumerate(
         [(LANE_FI + col * 4 * half_rows + D * (1 - c), D) for col in range(columns)] + [(LANE_FO + CORES * D * (1 - c), CORES * D)]
     ):
@@ -1087,8 +1119,31 @@
         pltpu.make_async_remote_copy(
             src_ref=ref, dst_ref=ref, send_sem=fsend.at[n], recv_sem=frecv.at[n], device_id=mate, device_id_type=MESH,
         ).wait_recv()
-    done = pltpu.make_async_copy(gb, weights_out_ref, load_sem.at[0])
-    done.start()
+    outs = []
+
+    def write(lane, width):
+        lanes = pl.ds(lane, width)
+        item = pltpu.make_async_copy(gb.at[:, lanes], weights_out_ref.at[:, lanes], load_sem.at[len(outs)])
+        item.start()
+        outs.append(item)
+
+    write(LANE_FI, 8 * D)
+    ag_u.step_five()
+    ag_k.step_four()
+    ag_k.step_five()
+    ag_grad.step_six()
+    out_ref[...] = ob[0, out_slot].astype(F32)
+    grad_ref[...] = ob[1, out_slot].astype(F32)
+    g_item.wait_recv()
+    gains_all = gmine[...] + gpeer[...]
+    own_gain = gains_all[:, 0:half_rows]
+    for i in range(1, columns):
+        own_gain = jnp.where(f == i, gains_all[:, i * half_rows : (i + 1) * half_rows], own_gain)
+    gain_out_ref[...] = own_gain
+    ag_u.step_six()
+    write(0, LANE_CKV)
+    ag_k.step_six()
+    write(LANE_CKV, 2 * D)
 
     to_holders_sent(q_pairs)
     to_owners_sent(o_pairs)
@@ -1124,9 +1179,10 @@
         item.wait_send()
     tell_p.finish()
     tell_g.finish()
-    for item in [ag_x, *spread, ag_c, ag_n, ag_u, ag_o, ag_k]:
+    for item in [ag_x, *spread, ag_c, ag_n, ag_u, ag_out, ag_grad, ag_k]:
         item.finish()
-    done.wait()
+    for item in outs:
+        item.wait()
 
 
 def fused_body(
@@ -1140,8 +1196,8 @@
     own_rows = memory.shape[1]
     padded = -(-own_rows // 128) * 128
     tokens = ranks * SUFFIX
-    gains = jnp.stack([self_gain, cross_gain, ffn_gain]).astype(F32)
-    gains = jnp.pad(gains, ((0, 5), (0, 0)))
+    gains = jnp.concatenate([self_gain, cross_gain, ffn_gain]).astype(F32)
+    gains = jnp.pad(gains, (0, 16 * 128 - gains.shape[0])).reshape(16, 128)
     vm = pl.BlockSpec(memory_space=pltpu.VMEM)
     sm = pl.BlockSpec(memory_space=pltpu.SMEM)
     hbm = pl.BlockSpec(memory_space=pl.ANY)
@@ -1155,10 +1211,10 @@
         pltpu.VMEM((ranks, SUFFIX, D), BF16),
         pltpu.VMEM((columns * tokens, D), BF16),
         pltpu.VMEM((columns * tokens, D), BF16),
-        pltpu.VMEM((ranks, 2 * SUFFIX, D), BF16),
+        pltpu.VMEM((2, ranks, SUFFIX, D), BF16),
         pltpu.VMEM((ranks, 8, D), F32),
         pltpu.VMEM((ranks, 8, 128), F32),
-        pltpu.VMEM((columns, 8, half_rows), F32),
+        pltpu.VMEM((columns, 16, 128), F32),
         pltpu.VMEM((padded, D), BF16),
         pltpu.VMEM((padded, 2 * D), BF16),
         pltpu.VMEM((padded, 2 * D), BF16),
@@ -1184,15 +1240,15 @@
         pltpu.VMEM((2, SUFFIX, 128), F32),
         pltpu.VMEM((SLOTS, SUFFIX, D), BF16),
         pltpu.VMEM((SLOTS, 2, SUFFIX, 128), F32),
-        pltpu.VMEM((SLOTS, SUFFIX, D), F32),
-        pltpu.VMEM((SLOTS, SUFFIX, D), F32),
+        pltpu.VMEM((SLOTS, SUFFIX, D), BF16),
+        pltpu.VMEM((SLOTS, SUFFIX, D), BF16),
         pltpu.VMEM((8, D), F32),
         pltpu.VMEM((8, D), F32),
         dma((10,)),
-        dma((len(CHUNKS), 30)),
-        dma((len(CHUNKS), 18)),
-        dma((6, 29)),
-        dma((6, 16)),
+        dma((len(CHUNKS), 17)),
+        dma((len(CHUNKS), 11)),
+        dma((7, 16)),
+        dma((7, 9)),
         dma((2, ranks)),
         dma((2, ranks)),
         dma((2, 2)),
@@ -1229,15 +1285,57 @@
         self_qkv, self_out, cross_query, cross_kv, cross_out, ffn_in, ffn_out,
     )
 
-    def lanes(low, width):
-        return weight_grads[:, low : low + width].astype(F32)
-
-    ffn_out_grad = jnp.concatenate([lanes(LANE_FO + D * j, D) for j in range(4)], axis=0)
+    return unpack(half_rows, columns, weight_grads, memgrad, out, grad, gain_grads)
+
+
+SPLIT = (
+    (LANE_QKV, 3 * D), (LANE_SO, D), (LANE_CQ, D), (LANE_CKV, 2 * D), (LANE_CO, D), (LANE_FI, 4 * D)
+)
+
+
+def unpack_kernel(w_ref, m_ref, o_ref, g_ref, *refs):
+    *weights, ffn_out_ref, mem_ref, out_ref, grad_ref = refs
+    for (low, width), ref in zip(SPLIT, weights):
+        ref[...] = w_ref[:, low : low + width].astype(F32)
+    for j in range(4):
+        ffn_out_ref[j] = w_ref[:, LANE_FO + D * j : LANE_FO + D * (j + 1)].astype(F32)
+    mem_ref[:, 0, :] = m_ref[...]
+    out_ref[...] = o_ref[...]
+    grad_ref[...] = g_ref[...]
+
+
+def unpack(half_rows, columns, weight_grads, memgrad, out, grad, gain_grads):
+    steps = 2
+    rows = half_rows // steps
+    own_rows = memgrad.shape[0]
+    mem_rows = -(-own_rows // (8 * steps)) * 8
+    tokens = out.shape[0] // steps
+    block = lambda height, width: pl.BlockSpec((height, width), lambda i: (i, 0))
+    results = pl.pallas_call(
+        unpack_kernel,
+        grid=(steps,),
+        out_shape=[jax.ShapeDtypeStruct((half_rows, width), F32) for low, width in SPLIT]
+        + [
+            jax.ShapeDtypeStruct((4, half_rows, D), F32),
+            jax.ShapeDtypeStruct((own_rows, 1, D), F32),
+            jax.ShapeDtypeStruct(out.shape, F32),
+            jax.ShapeDtypeStruct(grad.shape, F32),
+        ],
+        in_specs=[block(rows, UNITS * D), block(mem_rows, D), block(tokens, D), block(tokens, D)],
+        out_specs=[block(rows, width) for low, width in SPLIT]
+        + [
+            pl.BlockSpec((4, rows, D), lambda i: (0, i, 0)),
+            pl.BlockSpec((mem_rows, 1, D), lambda i: (i, 0, 0)),
+            block(tokens, D),
+            block(tokens, D),
+        ],
+        compiler_params=pltpu.CompilerParams(vmem_limit_bytes=63 * 2**20),
+        name="unpack",
+    )(weight_grads, memgrad, out, grad)
+    qkv, so, cq, ckv, co, fi, fo, mem, out, grad = results
     return (
-        out[None], grad[None], memgrad[None],
-        gain_grads[0], lanes(LANE_QKV, 3 * D), lanes(LANE_SO, D),
-        gain_grads[1], lanes(LANE_CQ, D), lanes(LANE_CKV, 2 * D), lanes(LANE_CO, D),
-        gain_grads[2], lanes(LANE_FI, 4 * D), ffn_out_grad,
+        out[None], grad[None], mem.reshape(1, own_rows, D),
+        gain_grads[0], qkv, so, gain_grads[1], cq, ckv, co, gain_grads[2], fi, fo.reshape(4 * half_rows, D),
     )
 
 

time: 222 us -> 185 us (0.83)
  Pallas kernels: 196 us -> 179 us
  other arithmetic: 14.3 us -> 1.32 us
  local copies, waits for them, and re-layouts: 8.59 us -> 1.42 us
    pallas_call x1, Pallas kernels: 196 us -> 169 us  [fused_body(): pl.pallas_call(partial(layer_kernel, ranks, columns), out_shape=(jax.Shap...]
    pallas_call x0 -> x1, Pallas kernels: none -> 9.72 us  [unpack(): pl.pallas_call(unpack_kernel, grid=(steps,), out_shape=[jax.ShapeDtypeStr...]
    convert_element_type x3 -> x0, other arithmetic: 9.23 us -> none  [lanes(): return weight_grads[:, low:low + width].astype(F32)]
    unnamed x9 -> x0, local copies, waits for them, and re-layouts: 5.12 us -> none
    concatenate x1 -> x0, other arithmetic: 2.54 us -> none  [fused_body(): jnp.concatenate([lanes(LANE_FO + D * j, D) for j in range(4)], axis=0)]
where the time goes in v4:
time: 185 us; the launch traced here: 183 us
  Pallas kernels  179 us (97%)
    pallas_call x1, Pallas kernels, fused_body(): pl.pallas_call(partial(layer_kernel, ranks, columns), out_shape=(jax.Shap...  169 us
    pallas_call x1, Pallas kernels, unpack(): pl.pallas_call(unpack_kernel, grid=(steps,), out_shape=[jax.ShapeDtypeStr...  9.72 us

profile of v4, /device:TPU:3, one launch (start us, length us, event | category | flops | bytes accessed | tf_op | source)
XLA Modules:
  0.0 183.1 jit_solution(10437500750190105489)
XLA Ops:
  1.3 1.3 fusion.6.gains_ref
  2.6 169.1 %layer.1 = (f32[32,768]{1,0:T(8,128)}, f32[32,768]{1,0:T(8,128)}, f32[418,768]{1,0:T(8,128)}, f32[8,384]{1,0:T(8,128)}, bf16[384,12288]{1,0:T(8,128)(2,1)}) custom-call(f32[32,768]{1,0:T(8,128)} %bitcast.13, f32[32,768]{1,0:T(8,128)} %bitcast.14, bf16[418,768]{1,0:T(8,128)(2,1)} %bitcast.12, s32[1,16]{1,0:T(1,128)} %res_ref.1, s32[1,1]{1,0:T(1,128)S(6)} %copy.28.pre_ref, ...), custom_call_target="tpu_custom_call" | custom-call | tf_op jit(solution)/shard_map/layer/pallas_call | solution.py:1267
  171.7 1.4 slice_reduce_fusion
  173.2 9.7 %unpack.1 = (f32[384,2304]{1,0:T(8,128)}, f32[384,768]{1,0:T(8,128)}, f32[384,768]{1,0:T(8,128)}, f32[384,1536]{1,0:T(8,128)}, f32[384,768]{1,0:T(8,128)}, /*ind...) custom-call(bf16[384,12288]{1,0:T(8,128)(2,1)} %get-tuple-element.28, ...), custom_call_target="tpu_custom_call" | custom-call | tf_op jit(solution)/shard_map/unpack/pallas_call | solution.py:1314

commit v5 on v4

--- a/solution.py
+++ b/solution.py
@@ -63,8 +63,9 @@
 
 
 class Gather:
-    def __init__(self, place, view, bulk, sems, at, has=None):
+    def __init__(self, place, view, bulk, sems, at, has=None, plane=None):
         self.z, self.x, self.c, self.f = place
+        self.plane = plane
         self.view, self.bulk = view, bulk
         self.send, self.recv = sems
         self.at = at
@@ -140,56 +141,113 @@
 
     def step_five(self):
         self.side(3)
+        self.hand_over()
+
+    def hand_over(self):
         item = self.copy(self.bulk(self.c), (self.z, self.x, 1 - self.c), 2 * RING, len(self.sent))
-        item.start()
-        self.sent.append((None, item))
+        mine = self.c >= 0 if self.plane is None else self.c == self.plane
+        pl.when(mine)(item.start)
+        self.sent.append((mine, item))
 
     def step_six(self):
-        self.copy(self.bulk(1 - self.c), (self.z, self.x, 1 - self.c), 2 * RING, 0).wait_recv()
+        theirs = self.c >= 0 if self.plane is None else self.c != self.plane
+        item = self.copy(self.bulk(1 - self.c), (self.z, self.x, 1 - self.c), 2 * RING, 0)
+        pl.when(theirs)(item.wait_recv)
 
     def finish(self):
         for cond, item in self.sent:
-            if cond is None:
-                item.wait_send()
-            else:
-                pl.when(cond)(item.wait_send)
+            pl.when(cond)(item.wait_send)
+
+
+class ShortGather(Gather):
+    def step_one(self):
+        own = (self.z, self.x, self.c)
+        for k in range(1, RING):
+            self.go(own, (self.place_at(k), self.x, self.c), self.z, self.z >= 0)
+        self.across(own, self.z >= 0)
+
+    def step_two(self):
+        for k in range(1, RING):
+            block = (self.place_at(k), self.x, self.c)
+            self.wait(block, block[0], self.z >= 0)
+            self.across(block, self.z >= 0)
+
+    def step_three(self):
+        for k in range(RING):
+            at = self.place_at(k)
+            self.wait((at, 1 - self.x, self.c), RING + at, self.z >= 0)
+        self.hand_over()
 
 
 class Spread(Gather):
     def __init__(self, place, theirs, mine, bulk, sems, at):
         super().__init__(place, theirs, bulk, sems, at)
         self.mine = mine
+        z, x, c = self.z, self.x, self.c
+        always, end = z >= 0, (z == 0) | (z == RING - 1)
+        self.opposite = RING - 1 - z
+        self.over = (
+            ((z, x, c), None, always),
+            ((z, 1 - x, c), None, always),
+            ((self.opposite, x, c), 1, end),
+            ((self.opposite, 1 - x, c), 1, end),
+        )
         self.pushed = []
 
+    def over_copy(self, n, view):
+        block, part, cond = self.over[n]
+        ref = view(*block, part)
+        return pltpu.make_async_remote_copy(
+            src_ref=ref, dst_ref=ref, send_sem=self.send.at[self.at, 15 + n], recv_sem=self.recv.at[self.at, 9 + n],
+            device_id=(self.z * (SIDE * CORES) + self.x * CORES + self.c, 1 - self.f), device_id_type=MESH,
+        )
+
     def push(self):
-        z, x, c = self.z, self.x, self.c
-        for n, block in enumerate(((z, x, c), (z, 1 - x, c))):
-            ref = self.mine(*block)
-            item = pltpu.make_async_remote_copy(
-                src_ref=ref, dst_ref=ref, send_sem=self.send.at[self.at, 15 + n], recv_sem=self.recv.at[self.at, 9 + n],
-                device_id=(z * (SIDE * CORES) + x * CORES + c, 1 - self.f), device_id_type=MESH,
-            )
-            item.start()
-            self.pushed.append(item)
+        for n in range(4):
+            item, cond = self.over_copy(n, self.mine), self.over[n][2]
+            pl.when(cond)(item.start)
+            self.pushed.append((cond, item))
+
+    def landed(self, n):
+        pl.when(self.over[n][2])(self.over_copy(n, self.view).wait_recv)
 
     def step_one(self):
         always = self.z >= 0
         own = (self.z, self.x, self.c)
-        self.wait(own, 9, always)
+        self.landed(0)
         self.line(own, True, True, always)
 
     def step_three(self):
-        self.arrive(2)
+        z, x, c = self.z, self.x, self.c
+        low, high = (self.place_at(-2), x, c), (self.place_at(2), x, c)
+        self.wait(low, low[0], z >= 2)
+        self.go((*low, 0), (self.place_at(1), x, c), low[0], z == RING - 2)
+        self.wait(high, high[0], z < RING - 2)
+        self.go((*high, 0), (self.place_at(-1), x, c), high[0], z == 1)
+        self.across(low, z >= 2)
+        self.across(high, z < RING - 2)
         self.side(1)
 
+    def step_four(self):
+        z, x, c = self.z, self.x, self.c
+        end = (z == 0) | (z == RING - 1)
+        block = (self.opposite, x, c, 0)
+        self.wait(block, self.opposite, end)
+        self.across(block, end)
+        self.side(2)
+
     def step_five(self):
-        self.wait((self.z, 1 - self.x, self.c), 10, self.z >= 0)
-        super().step_five()
+        z, x, c = self.z, self.x, self.c
+        self.landed(1)
+        self.landed(2)
+        self.landed(3)
+        self.wait((self.opposite, 1 - x, c, 0), RING + self.opposite, (z == 0) | (z == RING - 1))
+        self.hand_over()
 
     def finish(self):
         super().finish()
-        for item in self.pushed:
-            item.wait_send()
+        for cond, item in self.pushed:
+            pl.when(cond)(item.wait_send)
 
 
 class Pieces:
@@ -229,11 +287,12 @@
 
 SLOTS = 3
 UNITS = 16
-LANE_QKV, LANE_SO, LANE_CQ, LANE_CO, LANE_CKV, LANE_FI, LANE_FO = 0, 2304, 3072, 3840, 4608, 6144, 9216
-CHUNKS = ((0, 2304), (2304, 2304), (4608, 1536), (6144, 2048), (8192, 2048), (10240, 2048))
-LOADS_BY_CHUNK = ((0,), (1, 2, 3), (4,), (5,), (6, 7), (8, 9))
+LANE_QKV, LANE_SO, LANE_CQ, LANE_CKV, LANE_CO, LANE_FI, LANE_FO = 0, 2304, 3072, 3840, 5376, 6144, 9216
+OUT_CO, OUT_CKV = 3840, 4608
+CHUNKS = ((0, 2304), (2304, 1536), (3840, 1536), (5376, 3072), (8448, 2304), (10752, 1536))
+LOADS_BY_CHUNK = ((0,), (1, 2), (3,), (4, 5), (6, 7), (8, 9))
 PIECE = 384
-HALF_UNITS = 6
+UNIT_CHIPS = 6
 
 
 def layer_kernel(
@@ -242,7 +301,7 @@
     x_ref, cot_ref, mem_ref, res_ref, pre_ref, gains_ref,
     qkv_ref, so_ref, cq_ref, ckv_ref, co_ref, fi_ref, fo_ref,
     out_ref, grad_ref, memgrad_ref, gain_out_ref, weights_out_ref,
-    wb, gb, rb, sb, xb, cb, nb, olr, ob, tb, pb, gainb, memp, kvb, kvg, kp, kr, kc, ky, cp,
+    wb, gb, rl, rr, lb, sb, xb, cb, nb, olr, ob, tb, pb, gainb, memp, kvb, kvg, kp, kr, kc, ky, cp,
     kx, ks, hb, ab, ug, usend_b, urecv_b,
     cqb, qbuf, osend, ostat_send, obuf, ostat, dob, dstat_b, dobuf, dstat, dqsend, dqbuf, gmine, gpeer,
     load_sem, wsend, wrecv, gsend, grecv, bsend, brecv, asend, arecv, fsend, frecv, ysend, yrecv, psend, precv, usend, urecv,
@@ -279,8 +338,8 @@
     load(qkv_ref, LANE_QKV, 3 * D)
     load(so_ref, LANE_SO, D)
     load(cq_ref, LANE_CQ, D)
+    load(ckv_ref, LANE_CKV, 2 * D)
     load(co_ref, LANE_CO, D)
-    load(ckv_ref, LANE_CKV, 2 * D)
     load(fi_ref, LANE_FI, 4 * D)
     for j in range(4):
         load(fo_ref.at[pl.ds(j * half_rows, half_rows)], LANE_FO + D * j, D)
@@ -363,10 +422,13 @@
     def slab_view(first, width, rows_from):
         half = width // CORES
 
-        def view(zz, xx, cc):
+        cut = (half // 256) * 128
+
+        def view(zz, xx, cc, part=None):
+            low, size = {None: (0, half), 0: (0, half - cut), 1: (half - cut, cut)}[part]
             row = pl.multiple_of(rows_from * half_rows + (zz * SIDE + xx) * slab, 16)
-            lane = pl.multiple_of(first + cc * half, 128)
-            return wb.at[pl.ds(row, slab), pl.ds(lane, half)]
+            lane = pl.multiple_of(first + cc * half + low, 128)
+            return wb.at[pl.ds(row, slab), pl.ds(lane, size)]
 
         return view
 
@@ -429,7 +491,7 @@
     sems = (gsend, grecv)
     ag_x = Gather(place, block_view(xb), block_bulk(xb), sems, 0)
     ag_c = Gather(place, block_view(cb), block_bulk(cb), sems, 1)
-    ag_n = Gather(place, token_view(nb), token_bulk(nb), sems, 2)
+    ag_n = ShortGather(place, token_view(nb), token_bulk(nb), sems, 2)
     tell_p = Tell(pb, 0)
     spread = [
         Spread(place, slab_view(first, width, other), slab_view(first, width, f), chunk_bulk(first, width), (wsend, wrecv), n)
@@ -456,17 +518,13 @@
 
     ag_x.step_two()
     tick(0)
-    ag_c.step_one()
     ag_x.step_three()
     tick(1)
-    ag_c.step_two()
     ag_x.step_four()
     tick(2)
-    ag_c.step_three()
     ag_x.step_five()
     ag_x.step_six()
     tick(3)
-    ag_c.step_four()
     gain_item.wait_recv()
 
     memp[0:own_rows] = mem_ref[...]
@@ -490,6 +548,7 @@
             found = jnp.where(positions[i] == rank, slots[i], found)
         return found
 
+    by_rank = [example_of(r) for r in range(ranks)]
     out_slot = jnp.int32(0)
     for i in range(ranks):
         out_slot = jnp.where(mine_rank == i, slots[i], out_slot)
@@ -520,7 +579,7 @@
         return total
 
     tick(4)
-    ag_c.step_five()
+    ag_c.step_one()
     spread[0].step_six()
     q = mm(n1, wb[:, 0:D]).astype(BF16)
     k = mm(n1, wb[:, D : 2 * D]).astype(BF16)
@@ -543,7 +602,7 @@
     sm = jnp.concatenate(mixed, axis=1).astype(BF16)
 
     tick(5)
-    ag_c.step_six()
+    ag_c.step_two()
     spread[1].step_six()
     after_self = resid + mm(sm, wb[:, LANE_SO : LANE_SO + D])
     hat_two, rs_two = normed(after_self)
@@ -636,13 +695,8 @@
     to_holders(q_pairs)
 
     tick(6)
+    ag_c.step_three()
     spread[2].step_six()
-
-    for r in range(ranks):
-        olr[token_rows(f, r % CORES, r // CORES)] = cb[example_of(r)]
-    across_o = Across(olr, 0)
-    across_n = Across(nb, 1)
-    across_o.start()
 
 
     def kv_step(i, carry):
@@ -696,7 +750,9 @@
     to_owners(o_pairs)
 
     tick(7)
+    ag_c.step_four()
     at_owners(o_pairs)
+    spread[3].step_six()
 
     def expand(compact):
         low = lane_c < HEAD_DIM
@@ -723,9 +779,45 @@
     ag_n.step_one()
 
     tick(8)
+    ag_c.step_five()
     tick(9)
-    for n in (3, 4, 5):
+    for n in (4, 5):
         spread[n].step_six()
+    ag_c.step_six()
+    for r in range(ranks):
+        olr[token_rows(f, r % CORES, r // CORES)] = cb[by_rank[r]]
+    across_o = Across(olr, 0)
+    across_n = Across(nb, 1)
+    across_o.start()
+
+    unit_items = []
+
+    def push_part(which, at, to, src, dst):
+        @pl.when(me == to)
+        def _():
+            dst[...] = src[...]
+
+        @pl.when(me != to)
+        def _():
+            pltpu.make_async_remote_copy(
+                src_ref=src, dst_ref=dst, send_sem=usend.at[which, at],
+                recv_sem=urecv.at[which, me], device_id=(to, f), device_id_type=MESH,
+            ).start()
+
+        unit_items.append((which, at, to, src, dst))
+
+    def push_left(units, at, left):
+        lb[at] = left
+        for unit in units:
+            for j in range(CORES):
+                lanes = pl.ds(j * PIECE, PIECE)
+                push_part(0, CORES * unit + j, CORES * (unit + 1) + j, lb.at[at, :, lanes], rl.at[rows_of(me), lanes])
+
+    def push_right(unit, right):
+        for j in range(CORES):
+            sb[unit, j] = right[:, j * PIECE : (j + 1) * PIECE]
+            push_part(1, CORES * unit + j, CORES * (unit + 1) + j, sb.at[unit, j], rr.at[rows_of(me)])
+
     out_low = cb[mine]
     cot = out_low.astype(F32)
     acts, up_grads = [], []
@@ -765,6 +857,7 @@
     dstat_b[0] = lse
     dstat_b[1] = delta
     to_holders(d_pairs)
+    push_left((0, 1, 2), 0, n1)
     down = jnp.zeros((SUFFIX, D), F32)
     for j in range(4):
         lhs = jnp.concatenate(
@@ -773,38 +866,13 @@
         )
         down = down + mm(lhs, wb[:, LANE_FO + D * j : LANE_FO + D * (j + 1)])
     ob[0, my_slot] = (after_cross + down).astype(BF16)
-    ag_out = Gather(place, block_view(ob.at[0]), block_bulk(ob.at[0]), sems, 4)
+    ag_out = ShortGather(place, block_view(ob.at[0]), block_bulk(ob.at[0]), sems, 4)
     ag_out.step_one()
-    ag_n.step_three()
-
-    def unit_device(h):
-        return CORES * (h + 1) if h < HALF_UNITS else CORES * (h - HALF_UNITS + 1) + 1
-
-    unit_items = []
-
-    def push_unit(h, left, right):
-        to = unit_device(h)
-        sb[h, :, 0:D] = left
-        sb[h, :, D : D + PIECE] = right
-
-        @pl.when(me == to)
-        def _():
-            rb[rows_of(me)] = sb[h]
-
-        @pl.when(me != to)
-        def _():
-            pltpu.make_async_remote_copy(
-                src_ref=sb.at[h], dst_ref=rb.at[rows_of(me)], send_sem=usend.at[h],
-                recv_sem=urecv.at[me], device_id=(to, f), device_id_type=MESH,
-            ).start()
-
-        unit_items.append((h, to))
-
-    push_unit(HALF_UNITS + 4, cm, cross_low[:, 0:PIECE])
-    push_unit(HALF_UNITS + 5, cm, cross_low[:, PIECE:])
 
     at_holders(d_pairs)
 
+    push_left((4,), 2, n2)
+    push_left((3,), 1, sm)
     doh = jnp.concatenate([dobuf[s] for s in range(SLOTS)], axis=0)
     for g in range(3):
         sl = slice(256 * g, 256 * g + 256)
@@ -824,7 +892,8 @@
         for n in range(SLOTS):
             dqsend[n, :, sl] = dq[n * SUFFIX : (n + 1) * SUFFIX].astype(BF16)
     to_owners(dq_pairs)
-    ag_n.step_four()
+    ag_n.step_three()
+    across_n.start()
     def kp_step(i, carry):
         lane = pl.multiple_of(i * 256, 256)
         kp[:, pl.ds(lane, 256)] = mm_tn(memp[...], kvg[:, pl.ds(lane, 256)]).astype(BF16)
@@ -837,11 +906,37 @@
     )
     kr_item.start()
 
-    ag_n.step_five()
-    across_n.start()
     across_o.relay()
     ag_out.step_two()
     at_owners(dq_pairs)
+    push_left((5,), 3, cm)
+    push_right(5, cross_low)
+    kr_item.wait_recv()
+    kc[...] = (
+        kp[pl.ds(pl.multiple_of(c * half_rows, 128), half_rows)].astype(F32) + kr[...].astype(F32)
+    ).astype(BF16)
+    half_slabs = half_rows // SIDE
+
+    def ky_copy(j):
+        lanes = pl.ds(j * D, D)
+        return pltpu.make_async_remote_copy(
+            src_ref=kc.at[:, lanes], dst_ref=ky.at[:, lanes], send_sem=ksend.at[2 * chips + 1 + j],
+            recv_sem=krecv.at[chips + 1 + j], device_id=(me, other), device_id_type=MESH,
+        )
+
+    def kx_copy(j):
+        lanes = pl.ds(j * D, D)
+        return pltpu.make_async_remote_copy(
+            src_ref=kc.at[pl.ds(pl.multiple_of((1 - x) * half_slabs, 16), half_slabs), lanes], dst_ref=kx.at[:, lanes],
+            send_sem=ksend.at[2 * chips + 3 + j], recv_sem=krecv.at[chips + 3 + j],
+            device_id=(z * (SIDE * CORES) + (1 - x) * CORES + c, f), device_id_type=MESH,
+        )
+
+    @pl.when(c != f)
+    def _():
+        ky_copy(0).start()
+        ky_copy(1).start()
+
     cqg = (dqbuf[0].astype(F32) + dqbuf[1].astype(F32) + dqbuf[2].astype(F32)).astype(BF16)
     n2_grad = mm_nt(cqg, wb[:, LANE_CQ : LANE_CQ + D])
     part, cross_gain_grad = norm_back(n2_grad, hat_two, rs_two, gain[1])
@@ -860,48 +955,28 @@
         dks.append(mm_tn(ds, q4))
         dqs.append(unstack(mm(ds, k[:, sl])) * scale)
     packed_grad = [jnp.concatenate(parts, axis=1).astype(BF16) for parts in (dqs, dks, dvs)]
-    for h in range(HALF_UNITS):
-        push_unit(h, n1, packed_grad[h // 2][:, (h % 2) * PIECE : (h % 2 + 1) * PIECE])
-    for h in range(2):
-        push_unit(HALF_UNITS + 2 + h, n2, cqg[:, h * PIECE : (h + 1) * PIECE])
-        push_unit(HALF_UNITS + h, sm, self_low[:, h * PIECE : (h + 1) * PIECE])
-
-    def gb_view(lane_of):
-        def view(zz, xx, cc):
-            return gb.at[:, pl.ds(pl.multiple_of(lane_of(zz * SIDE + xx, cc), 128), PIECE)]
-
-        return view
+    for j in range(3):
+        push_right(j, packed_grad[j])
+    push_right(4, cqg)
+    push_right(3, self_low)
 
     n1_grad = jnp.zeros((SUFFIX, D), F32)
     for j in range(3):
         n1_grad = n1_grad + mm_nt(packed_grad[j], wb[:, D * j : D * (j + 1)])
     part, self_gain_grad = norm_back(n1_grad, hat_one, rs_one, gain[0])
     ob[1, my_slot] = (self_res + part).astype(BF16)
-    ag_grad = Gather(place, block_view(ob.at[1]), block_bulk(ob.at[1]), sems, 6)
+    ag_grad = ShortGather(place, block_view(ob.at[1]), block_bulk(ob.at[1]), sems, 6)
     gmine[...] = jnp.concatenate(
         [self_gain_grad, cross_gain_grad, ffn_gain_grad, jnp.zeros((5, D), F32)], axis=0
     )
     tb[my_slot] = gmine[...]
     tell_g = Tell(tb, 1)
     tell_g.start()
-    kr_item.wait_recv()
-    kc[...] = (
-        kp[pl.ds(pl.multiple_of(c * half_rows, 128), half_rows)].astype(F32) + kr[...].astype(F32)
-    ).astype(BF16)
-    ky_item = pltpu.make_async_remote_copy(
-        src_ref=kc, dst_ref=ky, send_sem=ksend.at[2 * chips + 1], recv_sem=krecv.at[chips + 1],
-        device_id=(me, other), device_id_type=MESH,
-    )
-
-    @pl.when(c != f)
-    def _():
-        ky_item.start()
-
     ag_grad.step_one()
     ag_out.step_three()
 
+    ag_n.step_six()
     across_n.relay()
-    ag_n.step_six()
     across_o.wait()
     across_n.wait()
 
@@ -953,72 +1028,97 @@
         item.start()
         f_items.append(item)
 
-    has_unit = (chip >= 1) & (chip <= HALF_UNITS)
+    has_unit = (chip >= 1) & (chip <= UNIT_CHIPS)
 
     def unit_lane(n, cc):
-        return PIECE * (n - 1) + HALF_UNITS * PIECE * cc
-
-    def unit_sum(pred, at):
+        return PIECE * (n - 1) + UNIT_CHIPS * PIECE * cc
+
+    def unit_take(which, src, dst):
+        def take(i, carry):
+            @pl.when(i != me)
+            def _():
+                pltpu.make_async_remote_copy(
+                    src_ref=src, dst_ref=dst(i), send_sem=usend.at[which, 0],
+                    recv_sem=urecv.at[which, i], device_id=mate, device_id_type=MESH,
+                ).wait_recv()
+
+            return carry
+
+        lax.fori_loop(0, ranks, take, 0)
+
+    def left_lanes(core):
+        return pl.ds(pl.multiple_of(core * PIECE, 128), PIECE)
+
+    def left_copy(core):
+        ref = rl.at[:, left_lanes(core)]
+        return pltpu.make_async_remote_copy(
+            src_ref=ref, dst_ref=ref, send_sem=ysend.at[1], recv_sem=yrecv.at[1], device_id=mate, device_id_type=MESH,
+        )
+
+    def unit_left(pred):
         @pl.when(pred)
         def _():
-            def take(i, carry):
-                @pl.when(i != me)
-                def _():
-                    pltpu.make_async_remote_copy(
-                        src_ref=sb.at[0], dst_ref=rb.at[rows_of(i)], send_sem=usend.at[0],
-                        recv_sem=urecv.at[i], device_id=mate, device_id_type=MESH,
-                    ).wait_recv()
-
-                return carry
-
-            lax.fori_loop(0, ranks, take, 0)
-            for col in range(columns):
-                ug[col] = mm_tn(rb[:, col * half_rows : (col + 1) * half_rows], rb[:, D : D + PIECE])
-            usend_b[...] = ug[other].astype(BF16)
-            pltpu.make_async_remote_copy(
-                src_ref=usend_b, dst_ref=urecv_b, send_sem=ysend.at[at], recv_sem=yrecv.at[at],
-                device_id=(me, other), device_id_type=MESH,
-            ).start()
-
-    def unit_join(pred, at):
+            unit_take(0, lb.at[0, :, pl.ds(0, PIECE)], lambda i: rl.at[rows_of(i), left_lanes(c)])
+            left_copy(c).start()
+
+    def unit_rows(n):
+        return pl.ds(n * (half_rows // 2), half_rows // 2)
+
+    def unit_copy(n):
+        rows = unit_rows(n)
+        return pltpu.make_async_remote_copy(
+            src_ref=usend_b.at[rows], dst_ref=urecv_b.at[rows], send_sem=ysend.at[3 + n], recv_sem=yrecv.at[3 + n],
+            device_id=(me, other), device_id_type=MESH,
+        )
+
+    def unit_sum(pred):
         @pl.when(pred)
         def _():
-            item = pltpu.make_async_remote_copy(
-                src_ref=usend_b, dst_ref=urecv_b, send_sem=ysend.at[at], recv_sem=yrecv.at[at],
-                device_id=(me, other), device_id_type=MESH,
-            )
-            item.wait_recv()
-            gb[:, pl.ds(pl.multiple_of(unit_lane(chip, c), 128), PIECE)] = (
-                ug[f] + urecv_b[...].astype(F32)
+            unit_take(1, sb.at[0, 0], lambda i: rr.at[rows_of(i)])
+            left_copy(1 - c).wait_recv()
+            for col in range(columns):
+                ug[col] = mm_tn(rl[:, col * half_rows : (col + 1) * half_rows], rr[...])
+            usend_b[...] = ug[other].astype(BF16)
+            for n in range(2):
+                unit_copy(n).start()
+
+    def unit_join(pred, n):
+        @pl.when(pred)
+        def _():
+            unit_copy(n).wait_recv()
+            rows = unit_rows(n)
+            gb[rows, pl.ds(pl.multiple_of(unit_lane(chip, c), 128), PIECE)] = (
+                ug[f, rows] + urecv_b[rows].astype(F32)
             ).astype(BF16)
-            item.wait_send()
 
     def has_block(zz, xx, cc):
         n = zz * SIDE + xx
-        return (n >= 1) & (n <= HALF_UNITS)
-
-    def unit_bulk(cc):
-        return gb.at[:, pl.ds(pl.multiple_of(HALF_UNITS * PIECE * cc, 128), HALF_UNITS * PIECE)]
-
-    ag_u = Gather(place, gb_view(unit_lane), unit_bulk, sems, 3, has_block)
-
-    ffn_rows(0, 4)
-    half_slabs = half_rows // SIDE
-    kx_item = pltpu.make_async_remote_copy(
-        src_ref=kc.at[pl.ds(pl.multiple_of((1 - x) * half_slabs, 16), half_slabs)], dst_ref=kx,
-        send_sem=ksend.at[2 * chips + 2], recv_sem=krecv.at[chips + 2],
-        device_id=(z * (SIDE * CORES) + (1 - x) * CORES + c, f), device_id_type=MESH,
-    )
-
-    @pl.when(c == f)
-    def _():
-        ky_item.wait_recv()
-        kc[...] = (kc[...].astype(F32) + ky[...].astype(F32)).astype(BF16)
-        kx_item.start()
-
-    ffn_rows(4, 6)
-    unit_sum(has_unit, 3)
-    ffn_rows(6, 8)
+        return (n >= 1) & (n <= UNIT_CHIPS)
+
+    def unit_bulk(rows):
+        width = UNIT_CHIPS * PIECE
+        return lambda cc: gb.at[rows, pl.ds(pl.multiple_of(width * cc, 128), width)]
+
+    def gb_view(lane_of, rows):
+        def view(zz, xx, cc):
+            return gb.at[rows, pl.ds(pl.multiple_of(lane_of(zz * SIDE + xx, cc), 128), PIECE)]
+
+        return view
+
+    class UnitGather:
+        def __init__(self):
+            parts = [unit_rows(n) for n in range(2)]
+            self.gathers = [
+                Gather(place, gb_view(unit_lane, rows), unit_bulk(rows), sems, at, has_block)
+                for at, rows in zip((3, 7), parts)
+            ]
+
+        def step(self, name):
+            for gather in self.gathers:
+                getattr(gather, name)()
+
+    ag_u = UnitGather()
+
     k_items = []
 
     def k_copy(t, j):
@@ -1028,15 +1128,26 @@
             device_id=(t * (SIDE * CORES) + x * CORES + j, f), device_id_type=MESH,
         )
 
-    @pl.when(c == f)
-    def _():
-        kx_item.wait_recv()
-        ks[...] = (
-            kc[pl.ds(pl.multiple_of(x * half_slabs, 16), half_slabs)].astype(F32) + kx[...].astype(F32)
-        ).astype(BF16)
-
-    for t in range(RING):
-        for j in range(CORES):
+    def k_over_x(j):
+        lanes = pl.ds(j * D, D)
+
+        @pl.when(c == f)
+        def _():
+            ky_copy(j).wait_recv()
+            kc[:, lanes] = (kc[:, lanes].astype(F32) + ky[:, lanes].astype(F32)).astype(BF16)
+            kx_copy(j).start()
+
+    def k_on_line(j):
+        lanes = pl.ds(j * D, D)
+
+        @pl.when(c == f)
+        def _():
+            kx_copy(j).wait_recv()
+            ks[:, lanes] = (
+                kc[pl.ds(pl.multiple_of(x * half_slabs, 16), half_slabs), lanes].astype(F32) + kx[:, lanes].astype(F32)
+            ).astype(BF16)
+
+        for t in range(RING):
             here = (z == t) & (c == j)
 
             @pl.when((c == f) & here)
@@ -1049,15 +1160,20 @@
 
             k_items.append((t, j, here))
 
-    unit_join(has_unit, 3)
-    ag_u.step_one()
-    ag_grad.step_two()
-    ag_out.step_four()
-    ffn_in_sum(0)
-    to_mate(LANE_FI + hidden[0], D)
-    ffn_in_sum(1)
-    to_mate(LANE_FI + hidden[1], D)
-    ag_u.step_two()
+    k_over_x(0)
+    ffn_rows(0, 2)
+    unit_left(has_unit)
+    k_on_line(0)
+    k_over_x(1)
+    unit_sum(has_unit)
+    ffn_rows(2, 4)
+    k_on_line(1)
+    unit_join(has_unit, 0)
+    ag_u.gathers[0].step_one()
+    ffn_rows(4, 5)
+    unit_join(has_unit, 1)
+    ag_u.gathers[1].step_one()
+    ffn_rows(5, 6)
 
     def take_k(i, carry):
         @pl.when((i != z) | (c != f))
@@ -1073,24 +1189,15 @@
     total = cp[0].astype(F32)
     for i in range(1, RING):
         total = total + cp[i].astype(F32)
-    k_lane = pl.multiple_of(LANE_CKV + c * D, 128)
+    k_lane = pl.multiple_of(OUT_CKV + c * D, 128)
     gb[pl.ds(pl.multiple_of(x * half_slabs + z * slab, 16), slab), pl.ds(k_lane, D)] = total.astype(BF16)
 
     def kv_view(zz, xx, cc):
         row = pl.multiple_of(xx * half_slabs + zz * slab, 16)
-        return gb.at[pl.ds(row, slab), pl.ds(pl.multiple_of(LANE_CKV + cc * D, 128), D)]
-
-    ag_k = Gather(place, kv_view, lambda cc: gb.at[:, pl.ds(pl.multiple_of(LANE_CKV + cc * D, 128), D)], sems, 5)
+        return gb.at[pl.ds(row, slab), pl.ds(pl.multiple_of(OUT_CKV + cc * D, 128), D)]
+
+    ag_k = Gather(place, kv_view, lambda cc: gb.at[:, pl.ds(pl.multiple_of(OUT_CKV + cc * D, 128), D)], sems, 5)
     ag_k.step_one()
-    ag_grad.step_three()
-    ag_out.step_five()
-    ffn_out_sum(0)
-    ffn_out_sum(1)
-    to_mate(LANE_FO + CORES * D * c, CORES * D)
-    ag_u.step_three()
-    ag_k.step_two()
-    ag_grad.step_four()
-    ag_out.step_six()
 
     def mg_step(i, carry):
         row = pl.multiple_of(i * 128, 128)
@@ -1104,9 +1211,24 @@
         memgrad_ref[full * 128 : own_rows] = tail[0 : own_rows - full * 128]
 
 
-    ag_u.step_four()
+    ag_u.step("step_two")
+    ffn_rows(6, 8)
+    ag_u.step("step_three")
+    ag_k.step_two()
+    ffn_in_sum(0)
+    to_mate(LANE_FI + hidden[0], D)
+    ag_grad.step_two()
     ag_k.step_three()
-    ag_grad.step_five()
+    ag_u.step("step_four")
+    ffn_in_sum(1)
+    to_mate(LANE_FI + hidden[1], D)
+    ag_k.step_four()
+    ag_grad.step_three()
+    ag_out.step_six()
+    ffn_out_sum(0)
+    ffn_out_sum(1)
+    to_mate(LANE_FO + CORES * D * c, CORES * D)
+    ag_u.step("step_five")
     tell_g.wait()
     gmine[...] = tb[0]
     for i in range(1, ranks):
@@ -1128,8 +1250,6 @@
         outs.append(item)
 
     write(LANE_FI, 8 * D)
-    ag_u.step_five()
-    ag_k.step_four()
     ag_k.step_five()
     ag_grad.step_six()
     out_ref[...] = ob[0, out_slot].astype(F32)
@@ -1140,22 +1260,28 @@
     for i in range(1, columns):
         own_gain = jnp.where(f == i, gains_all[:, i * half_rows : (i + 1) * half_rows], own_gain)
     gain_out_ref[...] = own_gain
-    ag_u.step_six()
-    write(0, LANE_CKV)
+    ag_u.step("step_six")
+    write(0, OUT_CKV)
     ag_k.step_six()
-    write(LANE_CKV, 2 * D)
+    write(OUT_CKV, 2 * D)
 
     to_holders_sent(q_pairs)
     to_owners_sent(o_pairs)
     to_holders_sent(d_pairs)
     to_owners_sent(dq_pairs)
-    for h, to in unit_items:
+    for which, at, to, src, dst in unit_items:
         @pl.when(me != to)
         def _():
             pltpu.make_async_remote_copy(
-                src_ref=sb.at[h], dst_ref=rb.at[rows_of(me)], send_sem=usend.at[h],
-                recv_sem=urecv.at[0], device_id=(to, f), device_id_type=MESH,
+                src_ref=src, dst_ref=dst, send_sem=usend.at[which, at],
+                recv_sem=urecv.at[which, 0], device_id=(to, f), device_id_type=MESH,
             ).wait_send()
+    @pl.when(has_unit)
+    def _():
+        for n in range(2):
+            unit_copy(n).wait_send()
+        left_copy(c).wait_send()
+
     for t, j, here in k_items:
         @pl.when((c == f) & jnp.logical_not(here))
         def _():
@@ -1163,7 +1289,8 @@
 
     @pl.when(c == f)
     def _():
-        kx_item.wait_send()
+        kx_copy(0).wait_send()
+        kx_copy(1).wait_send()
 
     across_o.finish()
     across_n.finish()
@@ -1173,13 +1300,14 @@
 
     @pl.when(c != f)
     def _():
-        ky_item.wait_send()
+        ky_copy(0).wait_send()
+        ky_copy(1).wait_send()
 
     for item in y_items:
         item.wait_send()
     tell_p.finish()
     tell_g.finish()
-    for item in [ag_x, *spread, ag_c, ag_n, ag_u, ag_out, ag_grad, ag_k]:
+    for item in [ag_x, *spread, ag_c, ag_n, *ag_u.gathers, ag_out, ag_grad, ag_k]:
         item.finish()
     for item in outs:
         item.wait()
@@ -1205,8 +1333,10 @@
     scratch = [
         pltpu.VMEM((D, UNITS * D), BF16),
         pltpu.VMEM((half_rows, UNITS * D), BF16),
-        pltpu.VMEM((tokens, D + PIECE), BF16),
-        pltpu.VMEM((2 * HALF_UNITS, SUFFIX, D + PIECE), BF16),
+        pltpu.VMEM((tokens, D), BF16),
+        pltpu.VMEM((tokens, PIECE), BF16),
+        pltpu.VMEM((4, SUFFIX, D), BF16),
+        pltpu.VMEM((UNIT_CHIPS, CORES, SUFFIX, PIECE), BF16),
         pltpu.VMEM((ranks, SUFFIX, D), F32),
         pltpu.VMEM((ranks, SUFFIX, D), BF16),
         pltpu.VMEM((columns * tokens, D), BF16),
@@ -1245,24 +1375,24 @@
         pltpu.VMEM((8, D), F32),
         pltpu.VMEM((8, D), F32),
         dma((10,)),
-        dma((len(CHUNKS), 17)),
-        dma((len(CHUNKS), 11)),
-        dma((7, 16)),
-        dma((7, 9)),
+        dma((len(CHUNKS), 19)),
+        dma((len(CHUNKS), 13)),
+        dma((8, 16)),
+        dma((8, 9)),
         dma((2, ranks)),
         dma((2, ranks)),
         dma((2, 2)),
         dma((2, 2)),
         dma((3,)),
         dma((3,)),
-        dma((4,)),
-        dma((4,)),
+        dma((5,)),
+        dma((5,)),
         dma((6, SLOTS)),
         dma((6, SLOTS)),
-        dma((2 * HALF_UNITS,)),
-        dma((ranks,)),
-        dma((2 * chips + 3,)),
-        dma((chips + 3,)),
+        dma((2, CORES * UNIT_CHIPS)),
+        dma((2, ranks)),
+        dma((2 * chips + 5,)),
+        dma((chips + 5,)),
     ]
     out, grad, memgrad, gain_grads, weight_grads = pl.pallas_call(
         partial(layer_kernel, ranks, columns),
@@ -1288,15 +1418,21 @@
     return unpack(half_rows, columns, weight_grads, memgrad, out, grad, gain_grads)
 
 
-SPLIT = (
-    (LANE_QKV, 3 * D), (LANE_SO, D), (LANE_CQ, D), (LANE_CKV, 2 * D), (LANE_CO, D), (LANE_FI, 4 * D)
-)
+SPLIT = ((0, 3), (3, 1), (4, 1), (OUT_CKV, 2 * D), (5, 1), (LANE_FI, 4 * D))
+WHOLE = (OUT_CKV, LANE_FI)
 
 
 def unpack_kernel(w_ref, m_ref, o_ref, g_ref, *refs):
     *weights, ffn_out_ref, mem_ref, out_ref, grad_ref = refs
     for (low, width), ref in zip(SPLIT, weights):
-        ref[...] = w_ref[:, low : low + width].astype(F32)
+        if low in WHOLE:
+            ref[...] = w_ref[:, low : low + width].astype(F32)
+            continue
+        for n in range(width):
+            for j in range(CORES):
+                at = (UNIT_CHIPS * j + low + n) * PIECE
+                to = (CORES * n + j) * PIECE
+                ref[:, to : to + PIECE] = w_ref[:, at : at + PIECE].astype(F32)
     for j in range(4):
         ffn_out_ref[j] = w_ref[:, LANE_FO + D * j : LANE_FO + D * (j + 1)].astype(F32)
     mem_ref[:, 0, :] = m_ref[...]
@@ -1314,7 +1450,7 @@
     results = pl.pallas_call(
         unpack_kernel,
         grid=(steps,),
-        out_shape=[jax.ShapeDtypeStruct((half_rows, width), F32) for low, width in SPLIT]
+        out_shape=[jax.ShapeDtypeStruct((half_rows, width if low in WHOLE else width * D), F32) for low, width in SPLIT]
         + [
             jax.ShapeDtypeStruct((4, half_rows, D), F32),
             jax.ShapeDtypeStruct((own_rows, 1, D), F32),
@@ -1322,7 +1458,7 @@
             jax.ShapeDtypeStruct(grad.shape, F32),
         ],
         in_specs=[block(rows, UNITS * D), block(mem_rows, D), block(tokens, D), block(tokens, D)],
-        out_specs=[block(rows, width) for low, width in SPLIT]
+        out_specs=[block(rows, width if low in WHOLE else width * D) for low, width in SPLIT]
         + [
             pl.BlockSpec((4, rows, D), lambda i: (0, i, 0)),
             pl.BlockSpec((mem_rows, 1, D), lambda i: (i, 0, 0)),

time: 185 us -> 175 us (0.946)
  Pallas kernels: 179 us -> 171 us
    pallas_call x1, Pallas kernels: 169 us -> 161 us  [fused_body(): pl.pallas_call(partial(layer_kernel, ranks, columns), out_shape=(jax.Shap...]
where the time goes in v5:
time: 175 us
  Pallas kernels  171 us (98%)
    pallas_call x1, Pallas kernels, fused_body(): pl.pallas_call(partial(layer_kernel, ranks, columns), out_shape=(jax.Shap...  161 us
    pallas_call x1, Pallas kernels, unpack(): pl.pallas_call(unpack_kernel, grid=(steps,), out_shape=[jax.ShapeDtypeStr...  9.73 us

profile of v5, /device:TPU:3, one launch (start us, length us, event | category | flops | bytes accessed | tf_op | source)
XLA Modules:
  0.0 174.8 jit_solution(12089057258124855634)
XLA Ops:
  1.3 1.3 fusion.6.gains_ref
  2.6 160.9 %layer.1 = (f32[32,768]{1,0:T(8,128)}, f32[32,768]{1,0:T(8,128)}, f32[418,768]{1,0:T(8,128)}, f32[8,384]{1,0:T(8,128)}, bf16[384,12288]{1,0:T(8,128)(2,1)}) custom-call(f32[32,768]{1,0:T(8,128)} %bitcast.13, f32[32,768]{1,0:T(8,128)} %bitcast.14, bf16[418,768]{1,0:T(8,128)(2,1)} %bitcast.12, s32[1,16]{1,0:T(1,128)} %res_ref.1, s32[1,1]{1,0:T(1,128)S(6)} %copy.28.pre_ref, ...), custom_call_target="tpu_custom_call" | custom-call | tf_op jit(solution)/shard_map/layer/pallas_call | solution.py:1397
  163.5 1.4 slice_reduce_fusion
  164.9 9.7 %unpack.1 = (f32[384,2304]{1,0:T(8,128)}, f32[384,768]{1,0:T(8,128)}, f32[384,768]{1,0:T(8,128)}, f32[384,1536]{1,0:T(8,128)}, f32[384,768]{1,0:T(8,128)}, /*ind...) custom-call(bf16[384,12288]{1,0:T(8,128)(2,1)} %get-tuple-element.28, ...), custom_call_target="tpu_custom_call" | custom-call | tf_op jit(solution)/shard_map/unpack/pallas_call | solution.py:1450

commit v6 on v5

--- a/solution.py
+++ b/solution.py
@@ -63,9 +63,8 @@
 
 
 class Gather:
-    def __init__(self, place, view, bulk, sems, at, has=None, plane=None):
+    def __init__(self, place, view, bulk, sems, at, has=None):
         self.z, self.x, self.c, self.f = place
-        self.plane = plane
         self.view, self.bulk = view, bulk
         self.send, self.recv = sems
         self.at = at
@@ -137,22 +136,22 @@
 
     def step_four(self):
         self.arrive(3)
+        self.hand_over(0)
         self.side(2)
 
     def step_five(self):
         self.side(3)
-        self.hand_over()
-
-    def hand_over(self):
-        item = self.copy(self.bulk(self.c), (self.z, self.x, 1 - self.c), 2 * RING, len(self.sent))
-        mine = self.c >= 0 if self.plane is None else self.c == self.plane
-        pl.when(mine)(item.start)
-        self.sent.append((mine, item))
+        self.hand_over(1)
+
+    def hand_over(self, n):
+        item = self.copy(self.bulk(self.c, self.x + n * (1 - 2 * self.x)), (self.z, self.x, 1 - self.c), 2 * RING + n, len(self.sent))
+        item.start()
+        self.sent.append((self.z >= 0, item))
 
     def step_six(self):
-        theirs = self.c >= 0 if self.plane is None else self.c != self.plane
-        item = self.copy(self.bulk(1 - self.c), (self.z, self.x, 1 - self.c), 2 * RING, 0)
-        pl.when(theirs)(item.wait_recv)
+        for n in range(2):
+            ref = self.bulk(1 - self.c, self.x + n * (1 - 2 * self.x))
+            self.copy(ref, (self.z, self.x, 1 - self.c), 2 * RING + n, 0).wait_recv()
 
     def finish(self):
         for cond, item in self.sent:
@@ -171,12 +170,13 @@
             block = (self.place_at(k), self.x, self.c)
             self.wait(block, block[0], self.z >= 0)
             self.across(block, self.z >= 0)
+        self.hand_over(0)
 
     def step_three(self):
         for k in range(RING):
             at = self.place_at(k)
             self.wait((at, 1 - self.x, self.c), RING + at, self.z >= 0)
-        self.hand_over()
+        self.hand_over(1)
 
 
 class Spread(Gather):
@@ -198,7 +198,7 @@
         block, part, cond = self.over[n]
         ref = view(*block, part)
         return pltpu.make_async_remote_copy(
-            src_ref=ref, dst_ref=ref, send_sem=self.send.at[self.at, 15 + n], recv_sem=self.recv.at[self.at, 9 + n],
+            src_ref=ref, dst_ref=ref, send_sem=self.send.at[self.at, 15 + n], recv_sem=self.recv.at[self.at, 10 + n],
             device_id=(self.z * (SIDE * CORES) + self.x * CORES + self.c, 1 - self.f), device_id_type=MESH,
         )
 
@@ -234,15 +234,16 @@
         block = (self.opposite, x, c, 0)
         self.wait(block, self.opposite, end)
         self.across(block, end)
+        self.landed(2)
+        self.hand_over(0)
         self.side(2)
 
     def step_five(self):
         z, x, c = self.z, self.x, self.c
         self.landed(1)
-        self.landed(2)
         self.landed(3)
         self.wait((self.opposite, 1 - x, c, 0), RING + self.opposite, (z == 0) | (z == RING - 1))
-        self.hand_over()
+        self.hand_over(1)
 
     def finish(self):
         super().finish()
@@ -298,13 +299,13 @@
 def layer_kernel(
     ranks,
     columns,
-    x_ref, cot_ref, mem_ref, res_ref, pre_ref, gains_ref,
+    x_ref, cot_ref, mem_ref, res_ref, pre_ref, gain_one_ref, gain_two_ref, gain_three_ref,
     qkv_ref, so_ref, cq_ref, ckv_ref, co_ref, fi_ref, fo_ref,
     out_ref, grad_ref, memgrad_ref, gain_out_ref, weights_out_ref,
-    wb, gb, rl, rr, lb, sb, xb, cb, nb, olr, ob, tb, pb, gainb, memp, kvb, kvg, kp, kr, kc, ky, cp,
+    wb, gb, rl, rr, lb, sb, xb, cb, nb, olr, ob, pb, gainb, memp, kvb, kvg, kp, kr, kc, ky, cp,
     kx, ks, hb, ab, ug, usend_b, urecv_b,
     cqb, qbuf, osend, ostat_send, obuf, ostat, dob, dstat_b, dobuf, dstat, dqsend, dqbuf, gmine, gpeer,
-    load_sem, wsend, wrecv, gsend, grecv, bsend, brecv, asend, arecv, fsend, frecv, ysend, yrecv, psend, precv, usend, urecv,
+    load_sem, wsend, wrecv, gsend, grecv, bsend, brecv, gain_sem, asend, arecv, fsend, frecv, ysend, yrecv, psend, precv, usend, urecv,
     ksend, krecv,
 ):
     me = lax.axis_index("dp")
@@ -312,7 +313,7 @@
     z = lax.div(me, SIDE * CORES)
     x = lax.rem(lax.div(me, CORES), SIDE)
     c = lax.rem(me, CORES)
-    chip = lax.div(me, CORES)
+    seat = x * RING + z
     chips = ranks // CORES
     place = (z, x, c, f)
     half_rows = D // columns
@@ -347,8 +348,7 @@
     for s in range(SLOTS):
         qbuf[s] = jnp.zeros_like(qbuf[s])
         obuf[s] = jnp.zeros_like(obuf[s])
-        ostat[s, 0] = jnp.full_like(ostat[s, 0], NONE)
-        ostat[s, 1] = jnp.zeros_like(ostat[s, 1])
+        ostat[s] = jnp.where(lax.broadcasted_iota(jnp.int32, ostat.shape[1:], 1) < 64, NONE, 0.0)
         dobuf[s] = jnp.zeros_like(dobuf[s])
         dstat[s] = jnp.zeros_like(dstat[s])
         dqbuf[s] = jnp.zeros_like(dqbuf[s])
@@ -357,13 +357,18 @@
         return pl.ds(pl.multiple_of(device * SUFFIX, SUFFIX), SUFFIX)
 
     def slot_of(device):
-        return lax.rem(device, CORES) * chips + lax.div(device, CORES)
+        side = lax.rem(lax.div(device, CORES), SIDE)
+        return lax.rem(device, CORES) * chips + side * RING + lax.div(device, SIDE * CORES)
 
     my_slot = slot_of(me)
     xb[my_slot] = x_ref[...]
     cb[my_slot] = cot_ref[...].astype(BF16)
     pb[my_slot] = jnp.full((8, 128), pre_ref[0, 0].astype(F32), F32)
-    gainb[f] = gains_ref[...]
+    for n, ref in enumerate((gain_one_ref, gain_two_ref, gain_three_ref)):
+        values = ref[...].astype(F32).reshape(1, half_rows)
+        for j in range(half_rows // 128):
+            at = n * (half_rows // 128) + j
+            gainb[f, at : at + 1] = values[:, 128 * j : 128 * (j + 1)]
 
     barrier = pltpu.get_barrier_semaphore()
 
@@ -426,7 +431,7 @@
 
         def view(zz, xx, cc, part=None):
             low, size = {None: (0, half), 0: (0, half - cut), 1: (half - cut, cut)}[part]
-            row = pl.multiple_of(rows_from * half_rows + (zz * SIDE + xx) * slab, 16)
+            row = pl.multiple_of(rows_from * half_rows + (xx * RING + zz) * slab, 16)
             lane = pl.multiple_of(first + cc * half + low, 128)
             return wb.at[pl.ds(row, slab), pl.ds(lane, size)]
 
@@ -434,30 +439,35 @@
 
     def block_view(ref):
         def view(zz, xx, cc):
-            return ref.at[cc * chips + zz * SIDE + xx]
+            return ref.at[cc * chips + xx * RING + zz]
 
         return view
 
     def block_bulk(ref):
-        return lambda cc: ref.at[pl.ds(cc * chips, chips)]
+        return lambda cc, xx: ref.at[pl.ds(cc * chips + xx * RING, RING)]
 
     def token_rows(col, cc, at):
         return pl.ds(pl.multiple_of(((col * CORES + cc) * chips + at) * SUFFIX, SUFFIX), SUFFIX)
 
     def token_view(ref):
         def view(zz, xx, cc):
-            return ref.at[token_rows(f, cc, zz * SIDE + xx)]
+            return ref.at[token_rows(f, cc, xx * RING + zz)]
 
         return view
 
     def token_bulk(ref):
-        rows = chips * SUFFIX
-        return lambda cc: ref.at[pl.ds(pl.multiple_of((f * CORES + cc) * rows, rows), rows)]
+        rows = RING * SUFFIX
+        return lambda cc, xx: ref.at[pl.ds(pl.multiple_of(((f * CORES + cc) * SIDE + xx) * rows, rows), rows)]
 
     def chunk_bulk(first, width):
         half = width // CORES
-        rows = pl.ds(pl.multiple_of(other * half_rows, 128), half_rows)
-        return lambda cc: wb.at[rows, pl.ds(pl.multiple_of(first + cc * half, 128), half)]
+        rows = RING * slab
+
+        def bulk(cc, xx):
+            row = pl.multiple_of(other * half_rows + xx * rows, 16)
+            return wb.at[pl.ds(row, rows), pl.ds(pl.multiple_of(first + cc * half, 128), half)]
+
+        return bulk
 
     plane = pl.ds(pl.multiple_of((f * CORES + c) * chips * SUFFIX, SUFFIX), chips * SUFFIX)
     plane_in = pl.ds(pl.multiple_of((other * CORES + c) * chips * SUFFIX, SUFFIX), chips * SUFFIX)
@@ -540,7 +550,8 @@
         mine_rank = jnp.where(me == i, spot, mine_rank)
         before_large = before_large + group
 
-    slots = [(i % CORES) * chips + i // CORES for i in range(ranks)]
+    spots = [i // CORES % SIDE * RING + i // (SIDE * CORES) for i in range(ranks)]
+    slots = [(i % CORES) * chips + spots[i] for i in range(ranks)]
 
     def example_of(rank):
         found = jnp.int32(0)
@@ -725,6 +736,9 @@
     qh = jnp.concatenate([qbuf[s] for s in range(SLOTS)], axis=0)
     qh = (qh.astype(F32) * scale).astype(BF16)
     lane_c = lax.broadcasted_iota(jnp.int32, (SUFFIX, 128), 1)
+    def swap(tile):
+        return jnp.concatenate([tile[:, 64:], tile[:, :64]], axis=1)
+
     top_c = [jnp.zeros((SUFFIX, 128), F32) for _ in range(SLOTS)]
     sum_c = [jnp.zeros((SUFFIX, 128), F32) for _ in range(SLOTS)]
     for g in range(3):
@@ -745,8 +759,7 @@
                 top_c[n] = jnp.where(hit, top[at : at + SUFFIX], top_c[n])
                 sum_c[n] = jnp.where(hit, total[at : at + SUFFIX], sum_c[n])
     for n in range(SLOTS):
-        ostat_send[n, 0] = top_c[n]
-        ostat_send[n, 1] = sum_c[n]
+        ostat_send[n] = jnp.where(lane_c < 64, top_c[n], swap(sum_c[n]))
     to_owners(o_pairs)
 
     tick(7)
@@ -761,9 +774,9 @@
             axis=1,
         )
 
-    tops = [ostat[i, 0] for i in range(SLOTS)]
+    tops = [ostat[i] for i in range(SLOTS)]
     top_all = jnp.maximum(jnp.maximum(tops[0], tops[1]), tops[2])
-    shares = [ostat[i, 1] * jnp.exp(tops[i] - top_all) for i in range(SLOTS)]
+    shares = [jnp.where(lane_c < 64, swap(tops[i]) * jnp.exp(tops[i] - top_all), 0.0) for i in range(SLOTS)]
     whole = shares[0] + shares[1] + shares[2]
     whole = jnp.where(whole > 0.0, whole, 1.0)
     lse = top_all + jnp.log(whole)
@@ -775,22 +788,31 @@
     after_cross = after_self + mm(cm, wb[:, LANE_CO : LANE_CO + D])
     hat_three, rs_three = normed(after_cross)
     n3 = (hat_three * gain[2]).astype(BF16)
-    nb[token_rows(f, c, chip)] = n3
+    nb[token_rows(f, c, seat)] = n3
     ag_n.step_one()
 
     tick(8)
     ag_c.step_five()
     tick(9)
-    for n in (4, 5):
-        spread[n].step_six()
+    spread[4].step_six()
+    acts, slopes = [], []
+    for j in range(4):
+        value, slope = gelu_parts(mm(n3, wb[:, LANE_FI + D * j : LANE_FI + D * (j + 1)]))
+        acts.append(value.astype(BF16))
+        slopes.append(slope)
+    act = jnp.concatenate(acts, axis=1)
     ag_c.step_six()
     for r in range(ranks):
-        olr[token_rows(f, r % CORES, r // CORES)] = cb[by_rank[r]]
+        olr[token_rows(f, r % CORES, spots[r])] = cb[by_rank[r]]
     across_o = Across(olr, 0)
     across_n = Across(nb, 1)
     across_o.start()
-
+    spread[5].step_six()
     unit_items = []
+
+    def unit_device(unit, j):
+        at = unit + 1
+        return at % RING * (SIDE * CORES) + at // RING * CORES + j
 
     def push_part(which, at, to, src, dst):
         @pl.when(me == to)
@@ -811,16 +833,15 @@
         for unit in units:
             for j in range(CORES):
                 lanes = pl.ds(j * PIECE, PIECE)
-                push_part(0, CORES * unit + j, CORES * (unit + 1) + j, lb.at[at, :, lanes], rl.at[rows_of(me), lanes])
+                push_part(0, CORES * unit + j, unit_device(unit, j), lb.at[at, :, lanes], rl.at[rows_of(me), lanes])
 
     def push_right(unit, right):
         for j in range(CORES):
             sb[unit, j] = right[:, j * PIECE : (j + 1) * PIECE]
-            push_part(1, CORES * unit + j, CORES * (unit + 1) + j, sb.at[unit, j], rr.at[rows_of(me)])
+            push_part(1, CORES * unit + j, unit_device(unit, j), sb.at[unit, j], rr.at[rows_of(me)])
 
     out_low = cb[mine]
     cot = out_low.astype(F32)
-    acts, up_grads = [], []
     hidden_grad = [mm_nt(out_low, wb[:, LANE_FO + D * j : LANE_FO + D * (j + 1)]) for j in range(4)]
 
     def by_hidden(j):
@@ -833,12 +854,8 @@
 
     n3_grad = jnp.zeros((SUFFIX, D), F32)
     for j in range(4):
-        weight = wb[:, LANE_FI + D * j : LANE_FI + D * (j + 1)]
-        value, slope = gelu_parts(mm(n3, weight))
-        acts.append(value.astype(BF16))
-        part = (by_hidden(j) * slope).astype(BF16)
-        n3_grad = n3_grad + mm_nt(part, weight)
-    act = jnp.concatenate(acts, axis=1)
+        part = (by_hidden(j) * slopes[j]).astype(BF16)
+        n3_grad = n3_grad + mm_nt(part, wb[:, LANE_FI + D * j : LANE_FI + D * (j + 1)])
 
     ag_n.step_two()
     part, ffn_gain_grad = norm_back(n3_grad, hat_three, rs_three, gain[2])
@@ -854,8 +871,7 @@
         right = jnp.sum(jnp.where(lane_c < HEAD_DIM, 0.0, tile), axis=-1, keepdims=True)
         delta = jnp.where(lane_c == 2 * t, left, delta)
         delta = jnp.where(lane_c == 2 * t + 1, right, delta)
-    dstat_b[0] = lse
-    dstat_b[1] = delta
+    dstat_b[...] = jnp.where(lane_c < 64, lse, swap(delta))
     to_holders(d_pairs)
     push_left((0, 1, 2), 0, n1)
     down = jnp.zeros((SUFFIX, D), F32)
@@ -880,8 +896,8 @@
         vg = kvb[:, D + 256 * g : D + 256 * g + 256]
         q4 = stack(qh[:, sl])
         do4 = stack(doh[:, sl])
-        lse_col = jnp.concatenate([dstat[n, 0][:, 4 * g + h : 4 * g + h + 1] for h in range(4) for n in range(SLOTS)], axis=0)
-        del_col = jnp.concatenate([dstat[n, 1][:, 4 * g + h : 4 * g + h + 1] for h in range(4) for n in range(SLOTS)], axis=0)
+        lse_col = jnp.concatenate([dstat[n][:, 4 * g + h : 4 * g + h + 1] for h in range(4) for n in range(SLOTS)], axis=0)
+        del_col = jnp.concatenate([dstat[n][:, 64 + 4 * g + h : 65 + 4 * g + h] for h in range(4) for n in range(SLOTS)], axis=0)
         s = mm_nt(q4, kg)
         p = jnp.where(allowed, jnp.exp(jnp.where(allowed, s - lse_col, 0.0)), 0.0)
         dp = mm_nt(do4, vg)
@@ -966,12 +982,32 @@
     part, self_gain_grad = norm_back(n1_grad, hat_one, rs_one, gain[0])
     ob[1, my_slot] = (self_res + part).astype(BF16)
     ag_grad = ShortGather(place, block_view(ob.at[1]), block_bulk(ob.at[1]), sems, 6)
-    gmine[...] = jnp.concatenate(
+    gmine[0] = jnp.concatenate(
         [self_gain_grad, cross_gain_grad, ffn_gain_grad, jnp.zeros((5, D), F32)], axis=0
     )
-    tb[my_slot] = gmine[...]
-    tell_g = Tell(tb, 1)
-    tell_g.start()
+    partners = (
+        mate,
+        (me, other),
+        (z * (SIDE * CORES) + (1 - x) * CORES + c, f),
+        ((z + 1 - 2 * lax.rem(z, 2)) * (SIDE * CORES) + x * CORES + c, f),
+        (lax.rem(z + 2, RING) * (SIDE * CORES) + x * CORES + c, f),
+    )
+
+    def gain_copy(k):
+        return pltpu.make_async_remote_copy(
+            src_ref=gmine.at[k], dst_ref=gpeer.at[k], send_sem=gain_sem.at[0, k], recv_sem=gain_sem.at[1, k],
+            device_id=partners[k], device_id_type=MESH,
+        )
+
+    def gain_step(k):
+        gain_copy(k - 1).wait_recv()
+        total = gmine[k - 1] + gpeer[k - 1]
+        if k == len(partners):
+            return total
+        gmine[k] = total
+        gain_copy(k).start()
+
+    gain_copy(0).start()
     ag_grad.step_one()
     ag_out.step_three()
 
@@ -1028,7 +1064,7 @@
         item.start()
         f_items.append(item)
 
-    has_unit = (chip >= 1) & (chip <= UNIT_CHIPS)
+    has_unit = (seat >= 1) & (seat <= UNIT_CHIPS)
 
     def unit_lane(n, cc):
         return PIECE * (n - 1) + UNIT_CHIPS * PIECE * cc
@@ -1087,21 +1123,21 @@
         def _():
             unit_copy(n).wait_recv()
             rows = unit_rows(n)
-            gb[rows, pl.ds(pl.multiple_of(unit_lane(chip, c), 128), PIECE)] = (
+            gb[rows, pl.ds(pl.multiple_of(unit_lane(seat, c), 128), PIECE)] = (
                 ug[f, rows] + urecv_b[rows].astype(F32)
             ).astype(BF16)
 
     def has_block(zz, xx, cc):
-        n = zz * SIDE + xx
+        n = xx * RING + zz
         return (n >= 1) & (n <= UNIT_CHIPS)
 
     def unit_bulk(rows):
-        width = UNIT_CHIPS * PIECE
-        return lambda cc: gb.at[rows, pl.ds(pl.multiple_of(width * cc, 128), width)]
+        width = UNIT_CHIPS * PIECE // SIDE
+        return lambda cc, xx: gb.at[rows, pl.ds(pl.multiple_of(width * (SIDE * cc + xx), 128), width)]
 
     def gb_view(lane_of, rows):
         def view(zz, xx, cc):
-            return gb.at[rows, pl.ds(pl.multiple_of(lane_of(zz * SIDE + xx, cc), 128), PIECE)]
+            return gb.at[rows, pl.ds(pl.multiple_of(lane_of(xx * RING + zz, cc), 128), PIECE)]
 
         return view
 
@@ -1162,11 +1198,13 @@
 
     k_over_x(0)
     ffn_rows(0, 2)
+    gain_step(1)
     unit_left(has_unit)
     k_on_line(0)
     k_over_x(1)
     unit_sum(has_unit)
     ffn_rows(2, 4)
+    gain_step(2)
     k_on_line(1)
     unit_join(has_unit, 0)
     ag_u.gathers[0].step_one()
@@ -1174,6 +1212,7 @@
     unit_join(has_unit, 1)
     ag_u.gathers[1].step_one()
     ffn_rows(5, 6)
+    gain_step(3)
 
     def take_k(i, carry):
         @pl.when((i != z) | (c != f))
@@ -1196,7 +1235,7 @@
         row = pl.multiple_of(xx * half_slabs + zz * slab, 16)
         return gb.at[pl.ds(row, slab), pl.ds(pl.multiple_of(OUT_CKV + cc * D, 128), D)]
 
-    ag_k = Gather(place, kv_view, lambda cc: gb.at[:, pl.ds(pl.multiple_of(OUT_CKV + cc * D, 128), D)], sems, 5)
+    ag_k = Gather(place, kv_view, lambda cc, xx: gb.at[pl.ds(pl.multiple_of(xx * half_slabs, 16), half_slabs), pl.ds(pl.multiple_of(OUT_CKV + cc * D, 128), D)], sems, 5)
     ag_k.step_one()
 
     def mg_step(i, carry):
@@ -1213,6 +1252,7 @@
 
     ag_u.step("step_two")
     ffn_rows(6, 8)
+    gain_step(4)
     ag_u.step("step_three")
     ag_k.step_two()
     ffn_in_sum(0)
@@ -1229,11 +1269,6 @@
     ffn_out_sum(1)
     to_mate(LANE_FO + CORES * D * c, CORES * D)
     ag_u.step("step_five")
-    tell_g.wait()
-    gmine[...] = tb[0]
-    for i in range(1, ranks):
-        gmine[...] += tb[i]
-    g_item = push_y(gmine, gpeer, 2)
     for n, (lane, width) in enumerate(
         [(LANE_FI + col * 4 * half_rows + D * (1 - c), D) for col in range(columns)] + [(LANE_FO + CORES * D * (1 - c), CORES * D)]
     ):
@@ -1254,8 +1289,7 @@
     ag_grad.step_six()
     out_ref[...] = ob[0, out_slot].astype(F32)
     grad_ref[...] = ob[1, out_slot].astype(F32)
-    g_item.wait_recv()
-    gains_all = gmine[...] + gpeer[...]
+    gains_all = gain_step(5)
     own_gain = gains_all[:, 0:half_rows]
     for i in range(1, columns):
         own_gain = jnp.where(f == i, gains_all[:, i * half_rows : (i + 1) * half_rows], own_gain)
@@ -1306,7 +1340,8 @@
     for item in y_items:
         item.wait_send()
     tell_p.finish()
-    tell_g.finish()
+    for k in range(len(partners)):
+        gain_copy(k).wait_send()
     for item in [ag_x, *spread, ag_c, ag_n, *ag_u.gathers, ag_out, ag_grad, ag_k]:
         item.finish()
     for item in outs:
@@ -1324,8 +1359,6 @@
     own_rows = memory.shape[1]
     padded = -(-own_rows // 128) * 128
     tokens = ranks * SUFFIX
-    gains = jnp.concatenate([self_gain, cross_gain, ffn_gain]).astype(F32)
-    gains = jnp.pad(gains, (0, 16 * 128 - gains.shape[0])).reshape(16, 128)
     vm = pl.BlockSpec(memory_space=pltpu.VMEM)
     sm = pl.BlockSpec(memory_space=pltpu.SMEM)
     hbm = pl.BlockSpec(memory_space=pl.ANY)
@@ -1342,7 +1375,6 @@
         pltpu.VMEM((columns * tokens, D), BF16),
         pltpu.VMEM((columns * tokens, D), BF16),
         pltpu.VMEM((2, ranks, SUFFIX, D), BF16),
-        pltpu.VMEM((ranks, 8, D), F32),
         pltpu.VMEM((ranks, 8, 128), F32),
         pltpu.VMEM((columns, 16, 128), F32),
         pltpu.VMEM((padded, D), BF16),
@@ -1363,24 +1395,25 @@
         pltpu.VMEM((SUFFIX, D), BF16),
         pltpu.VMEM((SLOTS, SUFFIX, D), BF16),
         pltpu.VMEM((SLOTS, SUFFIX, D), BF16),
-        pltpu.VMEM((SLOTS, 2, SUFFIX, 128), F32),
+        pltpu.VMEM((SLOTS, SUFFIX, 128), F32),
         pltpu.VMEM((SLOTS, SUFFIX, D), BF16),
-        pltpu.VMEM((SLOTS, 2, SUFFIX, 128), F32),
+        pltpu.VMEM((SLOTS, SUFFIX, 128), F32),
         pltpu.VMEM((SUFFIX, D), BF16),
-        pltpu.VMEM((2, SUFFIX, 128), F32),
+        pltpu.VMEM((SUFFIX, 128), F32),
         pltpu.VMEM((SLOTS, SUFFIX, D), BF16),
-        pltpu.VMEM((SLOTS, 2, SUFFIX, 128), F32),
+        pltpu.VMEM((SLOTS, SUFFIX, 128), F32),
         pltpu.VMEM((SLOTS, SUFFIX, D), BF16),
         pltpu.VMEM((SLOTS, SUFFIX, D), BF16),
-        pltpu.VMEM((8, D), F32),
-        pltpu.VMEM((8, D), F32),
+        pltpu.VMEM((5, 8, D), F32),
+        pltpu.VMEM((5, 8, D), F32),
         dma((10,)),
         dma((len(CHUNKS), 19)),
-        dma((len(CHUNKS), 13)),
-        dma((8, 16)),
-        dma((8, 9)),
-        dma((2, ranks)),
-        dma((2, ranks)),
+        dma((len(CHUNKS), 14)),
+        dma((8, 17)),
+        dma((8, 10)),
+        dma((1, ranks)),
+        dma((1, ranks)),
+        dma((2, 5)),
         dma((2, 2)),
         dma((2, 2)),
         dma((3,)),
@@ -1403,7 +1436,7 @@
             jax.ShapeDtypeStruct((8, half_rows), F32),
             jax.ShapeDtypeStruct((half_rows, UNITS * D), BF16),
         ),
-        in_specs=[vm, vm, vm, sm, sm, vm] + [hbm] * 7,
+        in_specs=[vm, vm, vm, sm, sm, vm, vm, vm] + [hbm] * 7,
         out_specs=(vm, vm, vm, vm, hbm),
         scratch_shapes=scratch,
         compiler_params=pltpu.CompilerParams(
@@ -1411,7 +1444,7 @@
         ),
         name="layer",
     )(
-        decoder_in[0], cotangent[0], memory[0], res_group, prefix_len, gains,
+        decoder_in[0], cotangent[0], memory[0], res_group, prefix_len, self_gain, cross_gain, ffn_gain,
         self_qkv, self_out, cross_query, cross_kv, cross_out, ffn_in, ffn_out,
     )
 
@@ -1422,8 +1455,10 @@
 WHOLE = (OUT_CKV, LANE_FI)
 
 
-def unpack_kernel(w_ref, m_ref, o_ref, g_ref, *refs):
-    *weights, ffn_out_ref, mem_ref, out_ref, grad_ref = refs
+def unpack_kernel(w_ref, m_ref, o_ref, g_ref, gains_ref, *refs):
+    *weights, ffn_out_ref, mem_ref, out_ref, grad_ref, one_ref, two_ref, three_ref = refs
+    for n, ref in enumerate((one_ref, two_ref, three_ref)):
+        ref[...] = gains_ref[n : n + 1].reshape(ref.shape)
     for (low, width), ref in zip(SPLIT, weights):
         if low in WHOLE:
             ref[...] = w_ref[:, low : low + width].astype(F32)
@@ -1456,22 +1491,24 @@
             jax.ShapeDtypeStruct((own_rows, 1, D), F32),
             jax.ShapeDtypeStruct(out.shape, F32),
             jax.ShapeDtypeStruct(grad.shape, F32),
-        ],
-        in_specs=[block(rows, UNITS * D), block(mem_rows, D), block(tokens, D), block(tokens, D)],
+        ]
+        + [jax.ShapeDtypeStruct((half_rows,), F32)] * 3,
+        in_specs=[block(rows, UNITS * D), block(mem_rows, D), block(tokens, D), block(tokens, D), pl.BlockSpec(gain_grads.shape, lambda i: (0, 0))],
         out_specs=[block(rows, width if low in WHOLE else width * D) for low, width in SPLIT]
         + [
             pl.BlockSpec((4, rows, D), lambda i: (0, i, 0)),
             pl.BlockSpec((mem_rows, 1, D), lambda i: (i, 0, 0)),
             block(tokens, D),
             block(tokens, D),
-        ],
+        ]
+        + [pl.BlockSpec((half_rows,), lambda i: (0,))] * 3,
         compiler_params=pltpu.CompilerParams(vmem_limit_bytes=63 * 2**20),
         name="unpack",
-    )(weight_grads, memgrad, out, grad)
-    qkv, so, cq, ckv, co, fi, fo, mem, out, grad = results
+    )(weight_grads, memgrad, out, grad, gain_grads)
+    qkv, so, cq, ckv, co, fi, fo, mem, out, grad, gain_one, gain_two, gain_three = results
     return (
         out[None], grad[None], mem.reshape(1, own_rows, D),
-        gain_grads[0], qkv, so, gain_grads[1], cq, ckv, co, gain_grads[2], fi, fo.reshape(4 * half_rows, D),
+        gain_one, qkv, so, gain_two, cq, ckv, co, gain_three, fi, fo.reshape(4 * half_rows, D),
     )
 
 

time: 175 us -> 172 us (0.983)
  no operation moved by 1% of the time
where the time goes in v6:
time: 172 us
  Pallas kernels  170 us (99%)
    pallas_call x1, Pallas kernels, fused_body(): pl.pallas_call(partial(layer_kernel, ranks, columns), out_shape=(jax.Shap...  161 us
    pallas_call x1, Pallas kernels, unpack(): pl.pallas_call(unpack_kernel, grid=(steps,), out_shape=[jax.ShapeDtypeStr...  9.77 us

profile of v6, /device:TPU:3, one launch (start us, length us, event | category | flops | bytes accessed | tf_op | source)
XLA Modules:
  0.0 171.9 jit_solution(2112270166417007285)
XLA Ops:
  1.3 160.6 %layer.1 = (f32[32,768]{1,0:T(8,128)}, f32[32,768]{1,0:T(8,128)}, f32[418,768]{1,0:T(8,128)}, f32[8,384]{1,0:T(8,128)}, bf16[384,12288]{1,0:T(8,128)(2,1)}) custom-call(f32[32,768]{1,0:T(8,128)} %bitcast.8, f32[32,768]{1,0:T(8,128)} %bitcast.9, bf16[418,768]{1,0:T(8,128)(2,1)} %bitcast.7, s32[1,16]{1,0:T(1,128)} %res_ref.1, s32[1,1]{1,0:T(1,128)S(6)} %copy.28.pre_ref, ...), custom_call_target="tpu_custom_call" | custom-call | tf_op jit(solution)/shard_map/layer/pallas_call | solution.py:1430
  161.9 9.8 %unpack.1 = (f32[384,2304]{1,0:T(8,128)}, f32[384,768]{1,0:T(8,128)}, f32[384,768]{1,0:T(8,128)}, f32[384,1536]{1,0:T(8,128)}, f32[384,768]{1,0:T(8,128)}, /*ind...) custom-call(bf16[384,12288]{1,0:T(8,128)(2,1)} %get-tuple-element.31, ...), custom_call_target="tpu_custom_call" | custom-call | tf_op jit(solution)/shard_map/unpack/pallas_call | solution.py:1485

commit v7 on v6

--- a/solution.py
+++ b/solution.py
@@ -198,7 +198,7 @@
         block, part, cond = self.over[n]
         ref = view(*block, part)
         return pltpu.make_async_remote_copy(
-            src_ref=ref, dst_ref=ref, send_sem=self.send.at[self.at, 15 + n], recv_sem=self.recv.at[self.at, 10 + n],
+            src_ref=ref, dst_ref=ref, send_sem=self.send.at[self.at, 13 + n], recv_sem=self.recv.at[self.at, 10 + n],
             device_id=(self.z * (SIDE * CORES) + self.x * CORES + self.c, 1 - self.f), device_id_type=MESH,
         )
 
@@ -305,7 +305,7 @@
     wb, gb, rl, rr, lb, sb, xb, cb, nb, olr, ob, pb, gainb, memp, kvb, kvg, kp, kr, kc, ky, cp,
     kx, ks, hb, ab, ug, usend_b, urecv_b,
     cqb, qbuf, osend, ostat_send, obuf, ostat, dob, dstat_b, dobuf, dstat, dqsend, dqbuf, gmine, gpeer,
-    load_sem, wsend, wrecv, gsend, grecv, bsend, brecv, gain_sem, asend, arecv, fsend, frecv, ysend, yrecv, psend, precv, usend, urecv,
+    load_sem, wsend, wrecv, gsend, grecv, ssend, srecv, bsend, brecv, gain_sem, asend, arecv, fsend, frecv, ysend, yrecv, psend, precv, usend, urecv,
     ksend, krecv,
 ):
     me = lax.axis_index("dp")
@@ -498,10 +498,10 @@
             self.copy(plane, 0, (me, other)).wait_send()
             self.copy(plane_in, 1, mate).wait_send()
 
-    sems = (gsend, grecv)
+    sems, short_sems = (gsend, grecv), (ssend, srecv)
     ag_x = Gather(place, block_view(xb), block_bulk(xb), sems, 0)
     ag_c = Gather(place, block_view(cb), block_bulk(cb), sems, 1)
-    ag_n = ShortGather(place, token_view(nb), token_bulk(nb), sems, 2)
+    ag_n = ShortGather(place, token_view(nb), token_bulk(nb), short_sems, 0)
     tell_p = Tell(pb, 0)
     spread = [
         Spread(place, slab_view(first, width, other), slab_view(first, width, f), chunk_bulk(first, width), (wsend, wrecv), n)
@@ -882,7 +882,7 @@
         )
         down = down + mm(lhs, wb[:, LANE_FO + D * j : LANE_FO + D * (j + 1)])
     ob[0, my_slot] = (after_cross + down).astype(BF16)
-    ag_out = ShortGather(place, block_view(ob.at[0]), block_bulk(ob.at[0]), sems, 4)
+    ag_out = ShortGather(place, block_view(ob.at[0]), block_bulk(ob.at[0]), short_sems, 1)
     ag_out.step_one()
 
     at_holders(d_pairs)
@@ -981,7 +981,7 @@
         n1_grad = n1_grad + mm_nt(packed_grad[j], wb[:, D * j : D * (j + 1)])
     part, self_gain_grad = norm_back(n1_grad, hat_one, rs_one, gain[0])
     ob[1, my_slot] = (self_res + part).astype(BF16)
-    ag_grad = ShortGather(place, block_view(ob.at[1]), block_bulk(ob.at[1]), sems, 6)
+    ag_grad = ShortGather(place, block_view(ob.at[1]), block_bulk(ob.at[1]), short_sems, 2)
     gmine[0] = jnp.concatenate(
         [self_gain_grad, cross_gain_grad, ffn_gain_grad, jnp.zeros((5, D), F32)], axis=0
     )
@@ -1146,7 +1146,7 @@
             parts = [unit_rows(n) for n in range(2)]
             self.gathers = [
                 Gather(place, gb_view(unit_lane, rows), unit_bulk(rows), sems, at, has_block)
-                for at, rows in zip((3, 7), parts)
+                for at, rows in zip((2, 3), parts)
             ]
 
         def step(self, name):
@@ -1235,7 +1235,7 @@
         row = pl.multiple_of(xx * half_slabs + zz * slab, 16)
         return gb.at[pl.ds(row, slab), pl.ds(pl.multiple_of(OUT_CKV + cc * D, 128), D)]
 
-    ag_k = Gather(place, kv_view, lambda cc, xx: gb.at[pl.ds(pl.multiple_of(xx * half_slabs, 16), half_slabs), pl.ds(pl.multiple_of(OUT_CKV + cc * D, 128), D)], sems, 5)
+    ag_k = Gather(place, kv_view, lambda cc, xx: gb.at[pl.ds(pl.multiple_of(xx * half_slabs, 16), half_slabs), pl.ds(pl.multiple_of(OUT_CKV + cc * D, 128), D)], sems, 4)
     ag_k.step_one()
 
     def mg_step(i, carry):
@@ -1250,25 +1250,30 @@
         memgrad_ref[full * 128 : own_rows] = tail[0 : own_rows - full * 128]
 
 
-    ag_u.step("step_two")
-    ffn_rows(6, 8)
+    ag_u.gathers[0].step_two()
+    ffn_rows(6, 7)
+    ag_u.gathers[1].step_two()
+    ffn_rows(7, 8)
+    ag_u.gathers[0].step_three()
     gain_step(4)
-    ag_u.step("step_three")
     ag_k.step_two()
     ffn_in_sum(0)
     to_mate(LANE_FI + hidden[0], D)
+    ag_u.gathers[1].step_three()
     ag_grad.step_two()
-    ag_k.step_three()
-    ag_u.step("step_four")
     ffn_in_sum(1)
     to_mate(LANE_FI + hidden[1], D)
-    ag_k.step_four()
+    ag_u.gathers[0].step_four()
+    ag_k.step_three()
+    ffn_out_sum(0)
+    ag_u.gathers[1].step_four()
+    ffn_out_sum(1)
+    to_mate(LANE_FO + CORES * D * c, CORES * D)
     ag_grad.step_three()
     ag_out.step_six()
-    ffn_out_sum(0)
-    ffn_out_sum(1)
-    to_mate(LANE_FO + CORES * D * c, CORES * D)
-    ag_u.step("step_five")
+    ag_u.gathers[0].step_five()
+    ag_k.step_four()
+    ag_u.gathers[1].step_five()
     for n, (lane, width) in enumerate(
         [(LANE_FI + col * 4 * half_rows + D * (1 - c), D) for col in range(columns)] + [(LANE_FO + CORES * D * (1 - c), CORES * D)]
     ):
@@ -1407,10 +1412,12 @@
         pltpu.VMEM((5, 8, D), F32),
         pltpu.VMEM((5, 8, D), F32),
         dma((10,)),
-        dma((len(CHUNKS), 19)),
+        dma((len(CHUNKS), 17)),
         dma((len(CHUNKS), 14)),
-        dma((8, 17)),
-        dma((8, 10)),
+        dma((5, 17)),
+        dma((5, 10)),
+        dma((3, 9)),
+        dma((3, 10)),
         dma((1, ranks)),
         dma((1, ranks)),
         dma((2, 5)),

time: 172 us -> 170 us (0.988)
  Pallas kernels: 170 us -> 168 us
    pallas_call x1, Pallas kernels: 161 us -> 158 us  [fused_body(): pl.pallas_call(partial(layer_kernel, ranks, columns), out_shape=(jax.Shap...]
where the time goes in v7:
time: 170 us; the launch traced here: 169 us
  Pallas kernels  168 us (99%)
    pallas_call x1, Pallas kernels, fused_body(): pl.pallas_call(partial(layer_kernel, ranks, columns), out_shape=(jax.Shap...  158 us
    pallas_call x1, Pallas kernels, unpack(): pl.pallas_call(unpack_kernel, grid=(steps,), out_shape=[jax.ShapeDtypeStr...  9.77 us

profile of v7, /device:TPU:3, one launch (start us, length us, event | category | flops | bytes accessed | tf_op | source)
XLA Modules:
  0.0 169.4 jit_solution(3049507027618319094)
XLA Ops:
  1.3 158.2 %layer.1 = (f32[32,768]{1,0:T(8,128)}, f32[32,768]{1,0:T(8,128)}, f32[418,768]{1,0:T(8,128)}, f32[8,384]{1,0:T(8,128)}, bf16[384,12288]{1,0:T(8,128)(2,1)}) custom-call(f32[32,768]{1,0:T(8,128)} %bitcast.8, f32[32,768]{1,0:T(8,128)} %bitcast.9, bf16[418,768]{1,0:T(8,128)(2,1)} %bitcast.7, s32[1,16]{1,0:T(1,128)} %res_ref.1, s32[1,1]{1,0:T(1,128)S(6)} %copy.28.pre_ref, ...), custom_call_target="tpu_custom_call" | custom-call | tf_op jit(solution)/shard_map/layer/pallas_call | solution.py:1437
  159.5 9.8 %unpack.1 = (f32[384,2304]{1,0:T(8,128)}, f32[384,768]{1,0:T(8,128)}, f32[384,768]{1,0:T(8,128)}, f32[384,1536]{1,0:T(8,128)}, f32[384,768]{1,0:T(8,128)}, /*ind...) custom-call(bf16[384,12288]{1,0:T(8,128)(2,1)} %get-tuple-element.31, ...), custom_call_target="tpu_custom_call" | custom-call | tf_op jit(solution)/shard_map/unpack/pallas_call | solution.py:1492

commit v8 on v7

--- a/solution.py
+++ b/solution.py
@@ -883,7 +883,6 @@
         down = down + mm(lhs, wb[:, LANE_FO + D * j : LANE_FO + D * (j + 1)])
     ob[0, my_slot] = (after_cross + down).astype(BF16)
     ag_out = ShortGather(place, block_view(ob.at[0]), block_bulk(ob.at[0]), short_sems, 1)
-    ag_out.step_one()
 
     at_holders(d_pairs)
 
@@ -923,7 +922,7 @@
     kr_item.start()
 
     across_o.relay()
-    ag_out.step_two()
+    ag_out.step_one()
     at_owners(dq_pairs)
     push_left((5,), 3, cm)
     push_right(5, cross_low)
@@ -1009,7 +1008,7 @@
 
     gain_copy(0).start()
     ag_grad.step_one()
-    ag_out.step_three()
+    ag_out.step_two()
 
     ag_n.step_six()
     across_n.relay()
@@ -1067,7 +1066,7 @@
     has_unit = (seat >= 1) & (seat <= UNIT_CHIPS)
 
     def unit_lane(n, cc):
-        return PIECE * (n - 1) + UNIT_CHIPS * PIECE * cc
+        return PIECE * jnp.clip(n - 1, 0, UNIT_CHIPS - 1) + UNIT_CHIPS * PIECE * cc
 
     def unit_take(which, src, dst):
         def take(i, carry):
@@ -1261,6 +1260,7 @@
     to_mate(LANE_FI + hidden[0], D)
     ag_u.gathers[1].step_three()
     ag_grad.step_two()
+    ag_out.step_three()
     ffn_in_sum(1)
     to_mate(LANE_FI + hidden[1], D)
     ag_u.gathers[0].step_four()

time: 170 us -> 169 us (level)
  no operation moved by 1% of the time
where the time goes in v8:
time: 169 us
  Pallas kernels  168 us (99%)
    pallas_call x1, Pallas kernels, fused_body(): pl.pallas_call(partial(layer_kernel, ranks, columns), out_shape=(jax.Shap...  158 us
    pallas_call x1, Pallas kernels, unpack(): pl.pallas_call(unpack_kernel, grid=(steps,), out_shape=[jax.ShapeDtypeStr...  9.77 us

profile of v8, /device:TPU:3, one launch (start us, length us, event | category | flops | bytes accessed | tf_op | source)
XLA Modules:
  0.0 169.2 jit_solution(17398561940141843323)
XLA Ops:
  1.3 157.9 %layer.1 = (f32[32,768]{1,0:T(8,128)}, f32[32,768]{1,0:T(8,128)}, f32[418,768]{1,0:T(8,128)}, f32[8,384]{1,0:T(8,128)}, bf16[384,12288]{1,0:T(8,128)(2,1)}) custom-call(f32[32,768]{1,0:T(8,128)} %bitcast.8, f32[32,768]{1,0:T(8,128)} %bitcast.9, bf16[418,768]{1,0:T(8,128)(2,1)} %bitcast.7, s32[1,16]{1,0:T(1,128)} %res_ref.1, s32[1,1]{1,0:T(1,128)S(6)} %copy.28.pre_ref, ...), custom_call_target="tpu_custom_call" | custom-call | tf_op jit(solution)/shard_map/layer/pallas_call | solution.py:1437
  159.2 9.8 %unpack.1 = (f32[384,2304]{1,0:T(8,128)}, f32[384,768]{1,0:T(8,128)}, f32[384,768]{1,0:T(8,128)}, f32[384,1536]{1,0:T(8,128)}, f32[384,768]{1,0:T(8,128)}, /*ind...) custom-call(bf16[384,12288]{1,0:T(8,128)(2,1)} %get-tuple-element.31, ...), custom_call_target="tpu_custom_call" | custom-call | tf_op jit(solution)/shard_map/unpack/pallas_call | solution.py:1492

commit v9 on v8

--- a/solution.py
+++ b/solution.py
@@ -1144,7 +1144,7 @@
         def __init__(self):
             parts = [unit_rows(n) for n in range(2)]
             self.gathers = [
-                Gather(place, gb_view(unit_lane, rows), unit_bulk(rows), sems, at, has_block)
+                Gather(place, gb_view(unit_lane, rows), unit_bulk(rows), (wsend, grecv), at, has_block)
                 for at, rows in zip((2, 3), parts)
             ]
 
@@ -1195,6 +1195,8 @@
 
             k_items.append((t, j, here))
 
+    for item in spread:
+        item.finish()
     k_over_x(0)
     ffn_rows(0, 2)
     gain_step(1)
@@ -1234,7 +1236,7 @@
         row = pl.multiple_of(xx * half_slabs + zz * slab, 16)
         return gb.at[pl.ds(row, slab), pl.ds(pl.multiple_of(OUT_CKV + cc * D, 128), D)]
 
-    ag_k = Gather(place, kv_view, lambda cc, xx: gb.at[pl.ds(pl.multiple_of(xx * half_slabs, 16), half_slabs), pl.ds(pl.multiple_of(OUT_CKV + cc * D, 128), D)], sems, 4)
+    ag_k = Gather(place, kv_view, lambda cc, xx: gb.at[pl.ds(pl.multiple_of(xx * half_slabs, 16), half_slabs), pl.ds(pl.multiple_of(OUT_CKV + cc * D, 128), D)], (wsend, grecv), 4)
     ag_k.step_one()
 
     def mg_step(i, carry):
@@ -1347,7 +1349,7 @@
     tell_p.finish()
     for k in range(len(partners)):
         gain_copy(k).wait_send()
-    for item in [ag_x, *spread, ag_c, ag_n, *ag_u.gathers, ag_out, ag_grad, ag_k]:
+    for item in [ag_x, ag_c, ag_n, *ag_u.gathers, ag_out, ag_grad, ag_k]:
         item.finish()
     for item in outs:
         item.wait()
@@ -1414,7 +1416,7 @@
         dma((10,)),
         dma((len(CHUNKS), 17)),
         dma((len(CHUNKS), 14)),
-        dma((5, 17)),
+        dma((2, 17)),
         dma((5, 10)),
         dma((3, 9)),
         dma((3, 10)),

time: 169 us -> 169 us (level)
  no operation moved by 1% of the time
where the time goes in v9:
time: 169 us
  Pallas kernels  167 us (99%)
    pallas_call x1, Pallas kernels, fused_body(): pl.pallas_call(partial(layer_kernel, ranks, columns), out_shape=(jax.Shap...  157 us
    pallas_call x1, Pallas kernels, unpack(): pl.pallas_call(unpack_kernel, grid=(steps,), out_shape=[jax.ShapeDtypeStr...  9.77 us

profile of v9, /device:TPU:3, one launch (start us, length us, event | category | flops | bytes accessed | tf_op | source)
XLA Modules:
  0.0 168.7 jit_solution(10277299539731157230)
XLA Ops:
  1.3 157.5 %layer.1 = (f32[32,768]{1,0:T(8,128)}, f32[32,768]{1,0:T(8,128)}, f32[418,768]{1,0:T(8,128)}, f32[8,384]{1,0:T(8,128)}, bf16[384,12288]{1,0:T(8,128)(2,1)}) custom-call(f32[32,768]{1,0:T(8,128)} %bitcast.8, f32[32,768]{1,0:T(8,128)} %bitcast.9, bf16[418,768]{1,0:T(8,128)(2,1)} %bitcast.7, s32[1,16]{1,0:T(1,128)} %res_ref.1, s32[1,1]{1,0:T(1,128)S(6)} %copy.28.pre_ref, ...), custom_call_target="tpu_custom_call" | custom-call | tf_op jit(solution)/shard_map/layer/pallas_call | solution.py:1439
  158.8 9.8 %unpack.1 = (f32[384,2304]{1,0:T(8,128)}, f32[384,768]{1,0:T(8,128)}, f32[384,768]{1,0:T(8,128)}, f32[384,1536]{1,0:T(8,128)}, f32[384,768]{1,0:T(8,128)}, /*ind...) custom-call(bf16[384,12288]{1,0:T(8,128)(2,1)} %get-tuple-element.31, ...), custom_call_target="tpu_custom_call" | custom-call | tf_op jit(solution)/shard_map/unpack/pallas_call | solution.py:1494
